TPU v7x, 32 devices: a whole 2x2x4 slice. The times are simulated.
32 devices in a mesh: mesh: 16 (over z, y, x), obs: 2 (over core).
Axes of the slice: x: 2, y: 2, z: 4, core: 2. Of those that a mesh axis runs over, the one named last changes fastest.
Arguments:
- probes: bfloat16 [64, 128, 512], P(None, 'mesh', 'obs'), may hold values from -6 to 6
- velocity: float32 [128, 512], P('mesh', 'obs'), may hold values from 0.5 to 2
- viscosity: float32 [128, 512], P('mesh', 'obs'), may hold values from 0.1 to 3
- friction: float32 [128, 512], P('mesh', 'obs'), may hold values from 0.5 to 4
- obs_block: int32 [16, 128], P('mesh', 'obs'), may hold values from 0 to 31
- obs_weight: float32 [16, 128, 128], P('mesh', 'obs'), may hold values from -0.5 to 0.5
- obs_prec: float32 [16, 128], P('mesh', 'obs'), may hold values from 0.05 to 0.5
- rank: int32 [1], replicated, may hold values from 1 to 64
Outputs:
- basis: float32 [64, 128, 512], P(None, 'mesh', 'obs')
- factor: float32 [64, 64], replicated
All inputs are finite; a program needn't handle non-finite values.
Results may differ from a plain program's by a relative error of at most 0.0027.
Values may be sent and summed in bfloat16 or wider, within the bound.
No kernel may reach another device: no remote copies, remote signals or barrier semaphores. Data moves between devices by JAX's collectives and lax.ppermute only.
A program may use at most 64 MiB of HBM per device.

v0:
```python
import jax
import jax.numpy as jnp
from jax import lax
from jax.sharding import PartitionSpec as P

BLOCK = 128


PRIOR = 1.0


def extended(block, sides, width):
    for axis, dim in sides:
        count = lax.axis_size(axis)
        forward = [(i, i + 1) for i in range(count - 1)]
        backward = [(target, source) for source, target in forward]
        low = lax.ppermute(
            lax.slice_in_dim(block, block.shape[dim] - width, None, axis=dim), axis, forward
        )
        high = lax.ppermute(lax.slice_in_dim(block, 0, width, axis=dim), axis, backward)
        block = jnp.concatenate([low, block, high], axis=dim)
    return block


def apply_padded(padded, visc_pad, friction):
    height = padded.shape[1] - 2
    width = padded.shape[2] - 2
    centre = padded[:, 1:-1, 1:-1]
    visc_mid = visc_pad[1:-1, 1:-1]
    result = friction * centre
    for shift_row, shift_col in ((2, 1), (0, 1), (1, 2), (1, 0)):
        neighbor = padded[:, shift_row : shift_row + height, shift_col : shift_col + width]
        face_coef = 0.5 * (
            visc_mid + visc_pad[shift_row : shift_row + height, shift_col : shift_col + width]
        )
        result = result + face_coef * (centre - neighbor)
    return result


def per_device(probes, velocity, viscosity, friction, obs_block, obs_weight, obs_prec, rank):
    probe_count = probes.shape[0]
    rows_here, cols_here = velocity.shape
    obs_devices = lax.axis_size("obs")
    slab_columns = cols_here * obs_devices // BLOCK
    owned_blocks = cols_here // BLOCK
    cell_total = rows_here * cols_here * lax.axis_size("mesh") * obs_devices
    omega = probes.astype(jnp.float32)
    stacked = jnp.concatenate([velocity[None] * omega, viscosity[None]], axis=0)
    padded = extended(stacked, (("mesh", 1), ("obs", 2)), 1)
    visc_pad = padded[-1]
    tangent = apply_padded(padded[:-1], visc_pad, friction).astype(jnp.bfloat16)
    block_float, weights, precision = (
        lax.all_gather(obs_block.astype(jnp.float32), "obs", axis=1, tiled=True),
        lax.all_gather(obs_weight, "obs", axis=1, tiled=True),
        lax.all_gather(obs_prec, "obs", axis=1, tiled=True),
    )
    block_ids = block_float[0].astype(jnp.int32)
    weights = weights[0]
    precision = precision[0]
    row_ids = block_ids // slab_columns
    local_col = block_ids % slab_columns - lax.axis_index("obs") * owned_blocks
    inside = (local_col >= 0) & (local_col < owned_blocks)
    block_index = row_ids * owned_blocks + jnp.clip(local_col, 0, owned_blocks - 1)
    blocks = tangent.reshape(probe_count, rows_here * owned_blocks, BLOCK)
    picked = jnp.take(blocks, block_index, axis=1).astype(jnp.float32)
    misfit = jnp.where(inside, precision * jnp.sum(picked * weights, axis=-1), 0.0)
    contrib = jnp.where(inside[None, :, None], misfit[:, :, None] * weights[None], 0.0)
    source = (
        jnp.zeros((probe_count, rows_here * owned_blocks, BLOCK), jnp.float32)
        .at[:, block_index]
        .add(contrib)
    )
    source = source.reshape(probe_count, rows_here, cols_here)
    padded_source = extended(source, (("mesh", 1), ("obs", 2)), 1)
    gradient = velocity * apply_padded(padded_source, visc_pad, friction)
    sketch = (gradient + PRIOR * omega).reshape(probe_count, rows_here * cols_here)
    local_gram = (
        jnp.dot(
            sketch, sketch.T, precision=lax.Precision.HIGHEST, preferred_element_type=jnp.float32
        )
        / cell_total
    )
    factor = jnp.linalg.cholesky(lax.psum(local_gram, ("mesh", "obs")))
    solved = lax.linalg.triangular_solve(factor, sketch, left_side=True, lower=True)
    retained = (jnp.arange(probe_count, dtype=jnp.int32) < rank[0])[:, None]
    basis = jnp.where(retained, solved, 0.0).reshape(probe_count, rows_here, cols_here)
    return (basis, factor)


def solution(mesh):
    in_specs = (
        P(None, "mesh", "obs"),
        P("mesh", "obs"),
        P("mesh", "obs"),
        P("mesh", "obs"),
        P("mesh", "obs"),
        P("mesh", "obs", None),
        P("mesh", "obs"),
        P(),
    )
    out_specs = (P(None, "mesh", "obs"), P())
    return jax.shard_map(
        per_device, mesh=mesh, in_specs=in_specs, out_specs=out_specs, check_vma=False
    )
```

profile of v0, /device:TPU:0, one launch (start us, length us, event | category | flops | bytes accessed | tf_op | source)
XLA Modules:
  0.0 120.0 jit_solution(5822899715644588852)
XLA Ops:
  0.6 1.0 convert_multiply_fusion
  1.6 0.9 pad_maximum_fusion.23
  2.5 4.8 %collective-permute-start = (f32[65,1,256]{2,1,0:T(1,128)S(1)}, f32[65,1,256]{2,1,0:T(1,128)S(1)}, u32[]{:S(2)}, u32[]{:S(2)}) collective-permute-start(f32[65,1,256]{2,1,0:T(1,128)S(1)} %get-tuple-element.12), channel_id=1, source_target_pairs={{0,2},{2,4},{4,6},{6,8},{8,10},{10,12},{12,14},{14,16},{16,18},{18... | collective-permute-start | bytes 199688 | tf_op jit(solution)/shard_map/ppermute | solution.py:17
  7.3 1.3 %collective-permute-start.1 = (f32[65,1,256]{2,1,0:T(1,128)S(1)}, f32[65,1,256]{2,1,0:T(1,128)S(1)}, u32[]{:S(2)}, u32[]{:S(2)}) collective-permute-start(f32[65,1,256]{2,1,0:T(1,128)S(1)} %get-tuple-element.13), channel_id=1, source_target_pairs={{2,0},{4,2},{6,4},{8,6},{10,8},{12,10},{14,12},{16,14},{18,16},{20... | collective-permute-start | bytes 199688 | tf_op jit(solution)/shard_map/ppermute | solution.py:20
  8.6 1.2 %dynamic-slice = u32[1]{0:T(128)} dynamic-slice(u32[32]{0:T(128)} %constant.113, u32[]{:T(128)S(6)} %add.148), dynamic_slice_sizes={1} | dynamic-slice | bytes 12
  10.6 0.8 bitcast_dynamic-update-slice_fusion
  11.3 0.7 bitcast_dynamic-update-slice_fusion.1
  12.0 2.4 %all-reduce.2 = (f32[128]{0:T(128)S(1)}, f32[128]{0:T(128)S(1)}) all-reduce(f32[128]{0:T(128)S(1)} %bitcast_dynamic-update-slice_fusion.1, f32[128]{0:T(128)S(1)} %bitcast_dynamic-update-slice_fusion), channel_id=1, replica_groups=mesh['mesh'=16,'obs'=2] {'obs'}, use_global_device_ids=true, to_apply=%add | all-reduce | flops 256 | bytes 2048
  14.6 0.9 pad_maximum_fusion
  15.9 2.1 %collective-permute-start.2 = (f32[65,10,1]{0,2,1:T(1,128)S(1)}, f32[65,10,1]{0,2,1:T(1,128)S(1)}, u32[]{:S(2)}, u32[]{:S(2)}) collective-permute-start(f32[65,10,1]{0,2,1:T(1,128)S(1)} %copy.25), channel_id=1, source_target_pairs={{0,1},{2,3},{4,5},{6,7},{8,9},{10,11},{12,13},{14,15},{16,17},{18,... | collective-permute-start | bytes 7808 | tf_op jit(solution)/shard_map/ppermute | solution.py:17
  18.2 1.3 %collective-permute-start.3 = (f32[65,10,1]{0,2,1:T(1,128)S(1)}, f32[65,10,1]{0,2,1:T(1,128)S(1)}, u32[]{:S(2)}, u32[]{:S(2)}) collective-permute-start(f32[65,10,1]{0,2,1:T(1,128)S(1)} %copy.26), channel_id=1, source_target_pairs={{1,0},{3,2},{5,4},{7,6},{9,8},{11,10},{13,12},{15,14},{17,16},{19,... | collective-permute-start | bytes 7808 | tf_op jit(solution)/shard_map/ppermute | solution.py:20
  19.5 2.6 %all_gather.11 = f32[1,128,128]{2,1,0:T(8,128)S(1)} all-gather(f32[1,64,128]{2,1,0:T(8,128)S(1)} %copy-done.4), channel_id=1, replica_groups=mesh['mesh'=16,'obs'=2] {'obs'}, dimensions={1}, use_global_device_ids=true | all-gather | bytes 98304 | tf_op jit(solution)/shard_map/all_gather | solution.py:54
  23.0 1.0 fusion.17
  24.2 1.0 gather_fusion
  25.2 1.6 %multiply_reduce_fusion = f32[128,64]{1,0:T(8,128)S(1)} fusion(f32[128,128]{1,0:T(8,128)S(1)} %bitcast.53, bf16[128,64,128]{2,1,0:T(8,128)(2,1)S(1)} %gather_fusion, pred[128]{0:T(512)(128)(4,1)S(1)} %compare_and_fusion), kind=kLoop, calls=%fused_computation.2 | loop fusion | flops 4186112 | bytes 2195584 | tf_op jit(solution)/shard_map/reduce_sum | solution.py:66
  26.9 3.3 %select_bitcast_fusion = f32[128,64,128]{2,1,0:T(8,128)} fusion(f32[64,128]{0,1:T(8,128)S(1)} %select_bitcast_fusion.1, f32[128,128]{1,0:T(8,128)S(1)} %bitcast.54, pred[128]{0:T(512)(128)(4,1)S(1)} %get-tuple-element.6), kind=kLoop, calls=%fused_computation.3 | loop fusion | flops 2097152 | bytes 4292736 | tf_op jit(solution)/shard_map/jit(_where)/select_n | solution.py:67
  30.2 13.5 %scatter_fusion = f32[64,16,128]{2,0,1:T(8,128)S(1)} fusion(f32[64,16,128]{2,0,1:T(8,128)S(1)} %broadcast_in_dim.67, s32[128]{0:T(128)S(1)} %fusion.39, f32[128,64,128]{2,1,0:T(8,128)} %select_bitcast_fusion), kind=kCustom, calls=%fused_computation.1 | custom fusion | flops 1048576 | bytes 12583424 | tf_op jit(solution)/shard_map/scatter-add | solution.py:71
  44.3 1.3 %collective-permute-start.4 = (f32[64,1,256]{2,1,0:T(1,128)S(1)}, f32[64,1,256]{2,1,0:T(1,128)S(1)}, u32[]{:S(2)}, u32[]{:S(2)}) collective-permute-start(f32[64,1,256]{2,1,0:T(1,128)S(1)} %get-tuple-element.15), channel_id=1, source_target_pairs={{2,0},{4,2},{6,4},{8,6},{10,8},{12,10},{14,12},{16,14},{18,16},{20... | collective-permute-start | bytes 196616 | tf_op jit(solution)/shard_map/ppermute | solution.py:20
  45.6 5.2 %collective-permute-start.5 = (f32[64,1,256]{2,1,0:T(1,128)S(1)}, f32[64,1,256]{2,1,0:T(1,128)S(1)}, u32[]{:S(2)}, u32[]{:S(2)}) collective-permute-start(f32[64,1,256]{2,1,0:T(1,128)S(1)} %get-tuple-element.14), channel_id=1, source_target_pairs={{0,2},{2,4},{4,6},{6,8},{8,10},{10,12},{12,14},{14,16},{16,18},{18... | collective-permute-start | bytes 196616 | tf_op jit(solution)/shard_map/ppermute | solution.py:17
  51.5 2.5 %collective-permute-done.5 = f32[64,1,256]{2,1,0:T(1,128)S(1)} collective-permute-done((f32[64,1,256]{2,1,0:T(1,128)S(1)}, f32[64,1,256]{2,1,0:T(1,128)S(1)}, u32[]{:S(2)}, u32[]{:S(2)}) %collective-permute-start.5) | collective-permute-done | bytes 65568 | tf_op jit(solution)/shard_map/ppermute | solution.py:17
  54.4 1.3 %collective-permute-start.6 = (f32[64,10,1]{2,1,0:T(8,128)S(1)}, f32[64,10,1]{2,1,0:T(8,128)S(1)}, u32[]{:S(2)}, u32[]{:S(2)}) collective-permute-start(f32[64,10,1]{2,1,0:T(8,128)S(1)} %get-tuple-element.10), channel_id=1, source_target_pairs={{1,0},{3,2},{5,4},{7,6},{9,8},{11,10},{13,12},{15,14},{17,16},{19,... | collective-permute-start | bytes 7688 | tf_op jit(solution)/shard_map/ppermute | solution.py:20
  55.7 3.1 %collective-permute-start.7 = (f32[64,10,1]{2,1,0:T(8,128)S(1)}, f32[64,10,1]{2,1,0:T(8,128)S(1)}, u32[]{:S(2)}, u32[]{:S(2)}) collective-permute-start(f32[64,10,1]{2,1,0:T(8,128)S(1)} %get-tuple-element.11), channel_id=1, source_target_pairs={{0,1},{2,3},{4,5},{6,7},{8,9},{10,11},{12,13},{14,15},{16,17},{18,... | collective-permute-start | bytes 7688 | tf_op jit(solution)/shard_map/ppermute | solution.py:17
  58.8 1.5 %collective-permute-done.7 = f32[64,10,1]{2,1,0:T(8,128)S(1)} collective-permute-done((f32[64,10,1]{2,1,0:T(8,128)S(1)}, f32[64,10,1]{2,1,0:T(8,128)S(1)}, u32[]{:S(2)}, u32[]{:S(2)}) %collective-permute-start.7) | collective-permute-done | bytes 2592 | tf_op jit(solution)/shard_map/ppermute | solution.py:17
  60.3 0.8 convert_add_fusion
  61.1 0.7 fusion
  61.9 43.6 %psum.7 = f32[64,64]{0,1:T(8,128)S(1)} all-reduce(f32[64,64]{0,1:T(8,128)S(1)} %fusion), channel_id=1, replica_groups=mesh['mesh'=16,'obs'=2] {'mesh','obs'}, use_global_device_ids=true, to_apply=%region_2.3 | all-reduce | flops 4096 | bytes 32768 | tf_op jit(solution)/shard_map/psum | solution.py:83
  105.6 5.8 %cholesky.16 = f32[64,64]{1,0:T(8,128)S(1)} custom-call(f32[64,64]{1,0:T(8,128)S(1)} %fusion.29), custom_call_target="Cholesky" | custom-call | tf_op jit(solution)/shard_map/jit(cholesky)/cholesky | solution.py:83
  111.4 0.6 compare_reduce_fusion
  112.1 1.3 %select_bitcast_fusion.2 = (f32[1,64,64]{2,1,0:T(8,128)S(1)}, f32[64,64]{1,0:T(8,128)}) fusion(f32[64,64]{1,0:T(8,128)S(1)} %cholesky.16, pred[]{:T(512)} %compare_reduce_fusion), kind=kLoop, calls=%fused_computation.64 | loop fusion | flops 16384 | bytes 49153 | tf_op jit(solution)/shard_map/triangular_solve | solution.py:84
  113.3 4.9 %custom-call.6 = f32[1,64,64]{1,2,0:T(8,128)S(1)} custom-call(f32[1,64,64]{2,1,0:T(8,128)S(1)} %get-tuple-element.4), custom_call_target="InvertDiagBlocksLowerTriangular" | custom-call | tf_op jit(solution)/shard_map/triangular_solve | solution.py:84
  118.4 0.6 convolution_select_fusion
  119.1 1.0 copy.40
  (43 shorter events, 3.1 us)
Async XLA Ops:
  2.5 12.1 %collective-permute-start = (f32[65,1,256]{2,1,0:T(1,128)S(1)}, f32[65,1,256]{2,1,0:T(1,128)S(1)}, u32[]{:S(2)}, u32[]{:S(2)}) collective-permute-start(f32[65,1,256]{2,1,0:T(1,128)S(1)} %get-tuple-element.12), channel_id=1, source_target_pairs={{0,2},{2,4},{4,6},{6,8},{8,10},{10,12},{12,14},{14,16},{16,18},{18... | collective-permute-start | bytes 199688 | tf_op jit(solution)/shard_map/ppermute | solution.py:17
  7.3 7.3 %collective-permute-start.1 = (f32[65,1,256]{2,1,0:T(1,128)S(1)}, f32[65,1,256]{2,1,0:T(1,128)S(1)}, u32[]{:S(2)}, u32[]{:S(2)}) collective-permute-start(f32[65,1,256]{2,1,0:T(1,128)S(1)} %get-tuple-element.13), channel_id=1, source_target_pairs={{2,0},{4,2},{6,4},{8,6},{10,8},{12,10},{14,12},{16,14},{18,16},{20... | collective-permute-start | bytes 199688 | tf_op jit(solution)/shard_map/ppermute | solution.py:20
  14.6 4.9 %copy-start.4 = (f32[1,64,128]{2,1,0:T(8,128)S(1)}, f32[1,64,128]{2,1,0:T(8,128)}, u32[]{:S(2)}) copy-start(f32[1,64,128]{2,1,0:T(8,128)} %param.13) | copy-start | bytes 98308
  15.5 7.3 %copy-start.1 = (f32[8,256]{1,0:T(8,128)S(1)}, f32[8,256]{1,0:T(8,128)}, u32[]{:S(2)}) copy-start(f32[8,256]{1,0:T(8,128)} %param.10) | copy-start | bytes 24580
  15.7 7.3 %copy-start.3 = (f32[8,256]{1,0:T(8,128)S(1)}, f32[8,256]{1,0:T(8,128)}, u32[]{:S(2)}) copy-start(f32[8,256]{1,0:T(8,128)} %param.11) | copy-start | bytes 24580
  15.9 6.2 %collective-permute-start.2 = (f32[65,10,1]{0,2,1:T(1,128)S(1)}, f32[65,10,1]{0,2,1:T(1,128)S(1)}, u32[]{:S(2)}, u32[]{:S(2)}) collective-permute-start(f32[65,10,1]{0,2,1:T(1,128)S(1)} %copy.25), channel_id=1, source_target_pairs={{0,1},{2,3},{4,5},{6,7},{8,9},{10,11},{12,13},{14,15},{16,17},{18,... | collective-permute-start | bytes 7808 | tf_op jit(solution)/shard_map/ppermute | solution.py:17
  18.2 4.3 %collective-permute-start.3 = (f32[65,10,1]{0,2,1:T(1,128)S(1)}, f32[65,10,1]{0,2,1:T(1,128)S(1)}, u32[]{:S(2)}, u32[]{:S(2)}) collective-permute-start(f32[65,10,1]{0,2,1:T(1,128)S(1)} %copy.26), channel_id=1, source_target_pairs={{1,0},{3,2},{5,4},{7,6},{9,8},{11,10},{13,12},{15,14},{17,16},{19,... | collective-permute-start | bytes 7808 | tf_op jit(solution)/shard_map/ppermute | solution.py:20
  44.2 16.1 %copy-start = (bf16[64,8,256]{2,1,0:T(8,128)(2,1)S(1)}, bf16[64,8,256]{2,1,0:T(8,128)(2,1)}, u32[]{:S(2)}) copy-start(bf16[64,8,256]{2,1,0:T(8,128)(2,1)} %param.8) | copy-start | bytes 786436
  44.2 16.1 %copy-start.2 = (f32[8,256]{1,0:T(8,128)S(1)}, f32[8,256]{1,0:T(8,128)}, u32[]{:S(2)}) copy-start(f32[8,256]{1,0:T(8,128)} %param.9) | copy-start | bytes 24580
  44.3 7.1 %collective-permute-start.4 = (f32[64,1,256]{2,1,0:T(1,128)S(1)}, f32[64,1,256]{2,1,0:T(1,128)S(1)}, u32[]{:S(2)}, u32[]{:S(2)}) collective-permute-start(f32[64,1,256]{2,1,0:T(1,128)S(1)} %get-tuple-element.15), channel_id=1, source_target_pairs={{2,0},{4,2},{6,4},{8,6},{10,8},{12,10},{14,12},{16,14},{18,16},{20... | collective-permute-start | bytes 196616 | tf_op jit(solution)/shard_map/ppermute | solution.py:20
  45.6 8.4 %collective-permute-start.5 = (f32[64,1,256]{2,1,0:T(1,128)S(1)}, f32[64,1,256]{2,1,0:T(1,128)S(1)}, u32[]{:S(2)}, u32[]{:S(2)}) collective-permute-start(f32[64,1,256]{2,1,0:T(1,128)S(1)} %get-tuple-element.14), channel_id=1, source_target_pairs={{0,2},{2,4},{4,6},{6,8},{8,10},{10,12},{12,14},{14,16},{16,18},{18... | collective-permute-start | bytes 196616 | tf_op jit(solution)/shard_map/ppermute | solution.py:17
  54.4 4.4 %collective-permute-start.6 = (f32[64,10,1]{2,1,0:T(8,128)S(1)}, f32[64,10,1]{2,1,0:T(8,128)S(1)}, u32[]{:S(2)}, u32[]{:S(2)}) collective-permute-start(f32[64,10,1]{2,1,0:T(8,128)S(1)} %get-tuple-element.10), channel_id=1, source_target_pairs={{1,0},{3,2},{5,4},{7,6},{9,8},{11,10},{13,12},{15,14},{17,16},{19,... | collective-permute-start | bytes 7688 | tf_op jit(solution)/shard_map/ppermute | solution.py:20
  55.7 4.6 %collective-permute-start.7 = (f32[64,10,1]{2,1,0:T(8,128)S(1)}, f32[64,10,1]{2,1,0:T(8,128)S(1)}, u32[]{:S(2)}, u32[]{:S(2)}) collective-permute-start(f32[64,10,1]{2,1,0:T(8,128)S(1)} %get-tuple-element.11), channel_id=1, source_target_pairs={{0,1},{2,3},{4,5},{6,7},{8,9},{10,11},{12,13},{14,15},{16,17},{18,... | collective-permute-start | bytes 7688 | tf_op jit(solution)/shard_map/ppermute | solution.py:17
where the time goes:
time: 121 us; the launch traced here: 120 us
  blocking collectives  48.7 us (40%)
  other arithmetic  36.9 us (30%)
  starting transfers between devices  20.3 us (17%)
  local copies, waits for them, and re-layouts  6.42 us (5%)
  waiting for transfers between devices  4.02 us (3%)
  between operations  2.28 us (2%)
  matrix products  1.37 us (1%)
    psum x1, blocking collectives, per_device(): factor = jnp.linalg.cholesky(lax.psum(local_gram, ('mesh', 'obs')))  43.6 us
    ppermute x4, starting transfers between devices, extended(): lax.ppermute(lax.slice_in_dim(block, block.shape[dim] - width, None, axis...  15.2 us
    scatter-add x1, other arithmetic, per_device(): source = jnp.zeros((probe_count, rows_here * owned_blocks, BLOCK), jnp.fl...  13.5 us
    another operation x3, other arithmetic, per_device(): factor = jnp.linalg.cholesky(lax.psum(local_gram, ('mesh', 'obs')))  6.52 us
    another operation x2, other arithmetic, per_device(): lax.linalg.triangular_solve(factor, sketch, left_side=True, lower=True)  6.16 us
    ppermute x4, starting transfers between devices, extended(): lax.ppermute(lax.slice_in_dim(block, 0, width, axis=dim), axis, backward)  5.16 us
    ppermute x4, waiting for transfers between devices, extended(): lax.ppermute(lax.slice_in_dim(block, block.shape[dim] - width, None, axis...  3.99 us
    select_n x1, other arithmetic, per_device(): jnp.where(inside[None, :, None], misfit[:, :, None] * weights[None], 0.0)  3.26 us
  transfers between devices with their start and end apart: 8, of which 2 were waited for; matrix products, arithmetic and copies ran while one was open for 3% of the time, Pallas kernels for 0%

commit v1 on v0

v1 whole, which is shorter than its diff:
```python
import functools

import jax
import jax.numpy as jnp
from jax import lax
from jax.experimental import pallas as pl
from jax.experimental.pallas import tpu as pltpu
from jax.sharding import PartitionSpec as P

LANES = 128
RIGHT = 16
PAD = 8
F32 = jnp.float32
BF16 = jnp.bfloat16


def split(x):
    high = x.astype(BF16)
    return high, (x - high.astype(F32)).astype(BF16)


def lane_of(shape):
    return lax.broadcasted_iota(jnp.int32, shape, 1)


def row_of(shape):
    return lax.broadcasted_iota(jnp.int32, shape, 0)


def dot(a, b, rhs_dim=0):
    return lax.dot_general(
        a, b, (((1,), (rhs_dim,)), ((), ())), preferred_element_type=F32
    )


def call(body, outs, args, scratch=(), flops=0, name=None):
    outs = [jax.ShapeDtypeStruct(shape, kind) for shape, kind in outs]
    return pl.pallas_call(
        body,
        out_shape=outs,
        scratch_shapes=list(scratch),
        compiler_params=pltpu.CompilerParams(vmem_limit_bytes=8 * 2**20),
        cost_estimate=pl.CostEstimate(
            flops=flops, bytes_accessed=2**20, transcendentals=0
        ),
        name=name,
    )(*args)


def shifted(x, left_edge, right_edge):
    lane = lane_of(x.shape)
    width = x.shape[1]
    left = jnp.where(lane == 0, left_edge, pltpu.roll(x, 1, 1))
    right = jnp.where(lane == width - 1, right_edge, pltpu.roll(x, width - 1, 1))
    return left, right


def operate_row(centre, above, below, left, right, visc, friction):
    own, *others = visc
    faces = [0.5 * (own + other) for other in others]
    result = (friction + faces[0] + faces[1] + faces[2] + faces[3]) * centre
    for face, value in zip(faces, (above, below, left, right)):
        result = result - face * value
    return result


def tangent_row(count, centre, above, below, left_edge, right_edge, friction):
    left, right = shifted(centre, left_edge, right_edge)
    visc = [x[count : count + 1] for x in (centre, above, below, left, right)]
    values = [x[:count] for x in (centre, above, below, left, right)]
    return operate_row(*values, visc, friction).astype(BF16)


def edge_columns(rows):
    height, width = rows[0].shape
    lane = lane_of((height, LANES))
    out = jnp.zeros((height, LANES), F32)
    for at, x in enumerate(rows):
        out = jnp.where(lane == at, x[:, :1], out)
        out = jnp.where(lane == RIGHT + at, x[:, width - 1 :], out)
    return out


def edges_from(left_ref, right_ref, rows, at):
    here, last = lax.axis_index("obs"), lax.axis_size("obs") - 1
    left = left_ref[rows, RIGHT + at : RIGHT + at + 1]
    right = right_ref[rows, at : at + 1]
    return jnp.where(here > 0, left, 0.0), jnp.where(here < last, right, 0.0)


def sources(tangents, grid_rows, observed, slab_columns):
    count, width = tangents[0].shape
    owned = width // LANES
    first = lax.axis_index("obs") * owned
    blocks = jnp.concatenate(
        [t[:, c * LANES : (c + 1) * LANES] for t in tangents for c in range(owned)], axis=0
    )
    doubled = jnp.concatenate([blocks, blocks], axis=1)
    total = None
    for at in range(0, len(observed), 2):
        pair = observed[at : at + 2]
        if len(pair) == 1:
            pair = pair + [tuple(jnp.zeros_like(x) for x in pair[0])]
        high = jnp.concatenate([x[0] for x in pair], axis=0)
        low = jnp.concatenate([x[1] for x in pair], axis=0)
        share = pair[0][0].shape[0]
        lane = lane_of((1, LANES))
        ids = jnp.where(lane < share, pair[0][2], pltpu.roll(pair[1][2], share, 1))
        ids = ids.astype(jnp.int32)
        precision = jnp.where(lane < share, pair[0][3], pltpu.roll(pair[1][3], share, 1))
        misfit = dot(doubled, jnp.concatenate([high, low], axis=1), 1)
        kept = []
        for i, row in enumerate(grid_rows):
            for c in range(owned):
                k = i * owned + c
                scale = jnp.where(ids == row * slab_columns + first + c, precision, 0.0)
                kept.append(misfit[k * count : (k + 1) * count] * scale)
        misfit_high, misfit_low = split(jnp.concatenate(kept, axis=0))
        both = dot(
            jnp.concatenate([misfit_high, misfit_low], axis=1),
            jnp.concatenate(
                [
                    jnp.concatenate([high, low], axis=1),
                    jnp.concatenate([high, jnp.zeros_like(low)], axis=1),
                ],
                axis=0,
            ),
        )
        part = both[:, :LANES] + both[:, LANES:]
        total = part if total is None else total + part
    return [
        jnp.concatenate(
            [total[(i * owned + c) * count : (i * owned + c + 1) * count] for c in range(owned)],
            axis=1,
        )
        for i in range(len(tangents))
    ]


def own_share(weight_ref, ids_ref, precision_ref):
    share = weight_ref.shape[1]
    out = jnp.zeros((PAD, LANES), F32)
    row, lane = row_of(out.shape), lane_of(out.shape)

    def wide(x):
        return jnp.concatenate([x, jnp.zeros((1, LANES - share), F32)], axis=1)

    out = jnp.where(row == 0, wide(ids_ref[...].astype(F32)), out)
    return jnp.where(row == 1, wide(precision_ref[...]), out)


def read_share(ref, at, share):
    weight = ref[at : at + share, :]
    high, low = split(weight)
    return high, low, ref[at + share : at + share + 1, :], ref[at + share + 1 : at + share + 2, :]


def edges_kernel(probes, velocity, viscosity, friction, weight, ids, precision, omega, up, down, turned, small):
    count, rows, width = probes.shape
    share = weight.shape[1]
    for c in range(width // LANES):
        lanes = slice(c * LANES, (c + 1) * LANES)
        turned[c] = probes[:, :, lanes].astype(F32).reshape(count * rows, LANES)
        for r in range(rows):
            omega[r * count : (r + 1) * count, lanes] = turned[c, pl.ds(r, count, stride=rows), :]
    meta = own_share(weight, ids, precision)
    weight_high, weight_low = split(weight[0])
    for out, near, next_near in ((up, 0, 1), (down, rows - 1, rows - 2)):
        out[:count, :] = omega[near * count : (near + 1) * count, :].astype(BF16)
        out[count : 2 * count, :] = omega[next_near * count : (next_near + 1) * count, :].astype(BF16)
        out[2 * count : 2 * count + share, :] = jnp.concatenate([weight_high, weight_low], axis=1)
        small[...] = jnp.zeros_like(small)
        at = 0
        for ref, r in (
            (velocity, near),
            (velocity, next_near),
            (viscosity, near),
            (viscosity, next_near),
            (friction, near),
        ):
            value = ref[r : r + 1, :]
            high = value.astype(BF16).astype(F32)
            small[at : at + 1, :] = high
            small[at + 1 : at + 2, :] = value - high
            at += 2
        small[at : at + 1, :LANES] = meta[0:1]
        high = meta[1:2].astype(BF16).astype(F32)
        small[at + 1 : at + 2, :LANES] = high
        small[at + 2 : at + 3, :LANES] = meta[1:2] - high
        out[2 * count + share :, :] = small[...].astype(BF16)


def forced_kernel(omega, velocity, viscosity, weight, ids, precision, forced, sent):
    rows, width = velocity.shape
    count = omega.shape[0] // rows
    share = weight.shape[1]
    blocks = []
    first = row_of((PAD, width)) == 0
    for r in range(rows):
        block = jnp.concatenate(
            [
                velocity[r : r + 1, :] * omega[r * count : (r + 1) * count, :],
                jnp.where(first, viscosity[r : r + 1, :], 0.0),
            ],
            axis=0,
        )
        forced[r] = block
        blocks.append(block)
    sent[: count + PAD, :] = edge_columns(blocks)
    sent[count + PAD : count + PAD + share, :] = weight[0]
    sent[count + PAD + share :, :] = own_share(weight, ids, precision)


def shares_of(refs, at, share):
    return [read_share(ref, at, share) for ref in refs]


def inner_kernel(slab_columns, share, forced, friction, from_left, from_right, *rest):
    *observed, out = rest
    rows, height, width = forced.shape
    count = height - PAD
    tangents = []
    inner = range(1, rows - 1)
    for r in inner:
        edges = edges_from(from_left, from_right, slice(0, height), r)
        tangents.append(
            tangent_row(count, forced[r], forced[r - 1], forced[r + 1], *edges, friction[r : r + 1, :])
        )
    result = sources(tangents, inner, shares_of(observed, height, share), slab_columns)
    for i, x in enumerate(result):
        out[i * count : (i + 1) * count, :] = x


def received(ref, count, share):
    small = ref[2 * count + share :, :].astype(F32)
    parts = [small[i : i + 1] + small[i + 1 : i + 2] for i in range(0, 10, 2)]
    return parts, small[10:11, :LANES], small[11:12, :LANES] + small[12:13, :LANES]


def far_kernel(count, share, from_up, from_down, near, sent):
    blocks = []
    edge = lax.axis_index("mesh"), lax.axis_size("mesh") - 1
    width = from_up.shape[1]
    first = row_of((PAD, width)) == 0
    at = count + PAD
    for i, (ref, inside) in enumerate(((from_up, edge[0] > 0), (from_down, edge[0] < edge[1]))):
        (velocity, _, viscosity, _, _), ids, precision = received(ref, count, share)
        block = jnp.concatenate(
            [velocity * ref[:count, :].astype(F32), jnp.where(first, viscosity, 0.0)], axis=0
        )
        block = jnp.where(inside, block, 0.0)
        near[i] = block
        blocks.append(block)
        both = ref[2 * count : 2 * count + share, :].astype(F32)
        sent[at : at + share, :] = both[:, :LANES] + both[:, LANES:]
        row = row_of((PAD, LANES))
        sent[at + share : at + share + PAD, :] = jnp.where(
            row == 0, ids, jnp.where(row == 1, precision, 0.0)
        )
        at += share + PAD
    sent[: count + PAD, :] = edge_columns(blocks)


def outer_kernel(slab_columns, share, forced, near, friction, from_left, from_right, inner, *rest):
    *observed, out, sent = rest
    rows, height, width = forced.shape
    count = height - PAD
    tangents = []
    outer = (0, rows - 1)
    for r in outer:
        edges = edges_from(from_left, from_right, slice(0, height), r)
        above = near[0] if r == 0 else forced[r - 1]
        below = near[1] if r == rows - 1 else forced[r + 1]
        tangents.append(tangent_row(count, forced[r], above, below, *edges, friction[r : r + 1, :]))
    first, last = sources(tangents, outer, shares_of(observed, height, share), slab_columns)
    out[:count, :] = first
    out[count:, :] = last
    middle = [inner[i * count : (i + 1) * count, :] for i in range(rows - 2)]
    sent[...] = edge_columns([first, *middle, last])


def halo_kernel(slab_columns, share, forced, near, from_up, from_down, from_left, from_right, *rest):
    *observed, out = rest
    rows, height, width = forced.shape
    count = height - PAD
    here, last = lax.axis_index("mesh"), lax.axis_size("mesh") - 1
    for i, ref in enumerate((from_up, from_down)):
        (_, velocity, _, viscosity, friction), _, _ = received(ref, count, share)
        far = jnp.concatenate(
            [
                velocity * ref[count : 2 * count, :].astype(F32),
                jnp.broadcast_to(viscosity, (PAD, width)),
            ],
            axis=0,
        )
        own = forced[rows - 1 if i else 0]
        above, below = (own, far) if i else (far, own)
        edges = edges_from(from_left, from_right, slice(0, height), i)
        tangent = tangent_row(count, near[i], above, below, *edges, friction)
        at = height + i * (share + PAD)
        (source,) = sources(
            [tangent], (0 if i else rows - 1,), shares_of(observed, at, share), slab_columns
        )
        inside = here < last if i else here > 0
        out[i * count : (i + 1) * count, :] = jnp.where(inside, source, 0.0)


def packed(gram):
    half = gram.shape[0] // 2
    top, bottom = gram[:half], gram[half:]
    row, lane = row_of(top.shape), lane_of(top.shape) % (2 * half)
    mixed = jnp.where((lane >= half) & (row >= lane - half), pltpu.roll(top, half, 1), bottom)
    quarter = half // 2
    body = jnp.where(lane_of((quarter, LANES)) < 2 * half, mixed[:quarter], mixed[quarter:])
    diagonal = jnp.sum(jnp.where(row == lane - half, bottom, 0.0), axis=0, keepdims=True)
    return body, diagonal


def unpacked(body, diagonal):
    quarter = body.shape[0]
    half, size = 2 * quarter, 4 * quarter
    lane = lane_of(body.shape)
    turned = pltpu.roll(body, size, 1)
    mixed = jnp.concatenate(
        [jnp.where(lane < size, body, turned), jnp.where(lane < size, turned, body)], axis=0
    )
    row, lane = row_of(mixed.shape), lane_of(mixed.shape)
    top = pltpu.roll(mixed, LANES - half, 1)
    lower = jnp.concatenate(
        [
            jnp.where(row > lane, top, 0.0),
            jnp.where((lane < half) | ((lane < size) & (row < lane - half)), mixed, 0.0),
        ],
        axis=0,
    )
    spread = jnp.concatenate(
        [
            jnp.where(row == lane, top, 0.0),
            jnp.where(row == lane - half, diagonal, 0.0),
        ],
        axis=0,
    )
    square = jnp.concatenate([lower, jnp.zeros((LANES - size, LANES), F32)], axis=0)
    return lower + square.T[:size] + spread


def sketch_kernel(
    cells, forced, near, omega, velocity, friction, visc_left, visc_right,
    from_left, from_right, inner, outer, halo, sketch, gram, gram_diagonal,
):
    rows, height, width = forced.shape
    count = height - PAD
    values = [halo[:count, :], outer[:count, :]]
    values += [inner[i * count : (i + 1) * count, :] for i in range(rows - 2)]
    values += [outer[count:, :], halo[count:, :]]
    viscs = [near[0, count : count + 1, :]]
    viscs += [forced[r, count : count + 1, :] for r in range(rows)]
    viscs += [near[1, count : count + 1, :]]
    total = jnp.zeros((2 * count, 2 * count), F32)
    for r in range(rows):
        centre, visc = values[r + 1], viscs[r + 1]
        left, right = shifted(centre, *edges_from(from_left, from_right, slice(0, count), r))
        visc_side = shifted(
            visc, *edges_from(visc_left, visc_right, slice(count, count + 1), r)
        )
        gradient = velocity[r : r + 1, :] * operate_row(
            centre, values[r], values[r + 2], left, right,
            [visc, viscs[r], viscs[r + 2], *visc_side],
            friction[r : r + 1, :],
        )
        value = gradient + omega[r * count : (r + 1) * count, :]
        sketch[r * count : (r + 1) * count, :] = value
        parts = jnp.concatenate(split(value), axis=0)
        total = total + dot(parts, parts, 1)
    total = total + pltpu.roll(total, count, 1)
    total = (total[:count] + total[count:]) / cells
    body, diagonal = packed(total)
    gram[...] = body
    gram_diagonal[...] = jnp.broadcast_to(diagonal, gram_diagonal.shape)


def spread_kernel(body, other_body, diagonal, other_diagonal, out):
    total = body[...] + other_body[...]
    last = diagonal[0:1, :] + other_diagonal[0:1, :]
    for i in range(total.shape[0]):
        row = total[i : i + 1, :]
        for d in range(out.shape[0]):
            out[d, :, i * LANES : (i + 1) * LANES] = row
    for d in range(out.shape[0]):
        out[d, :, total.shape[0] * LANES :] = last


def factorize(matrix):
    size = matrix.shape[0]
    row = row_of((8, LANES))
    tiles = [matrix[8 * t : 8 * t + 8] for t in range(size // 8)]
    for j in range(size):
        t, s = divmod(j, 8)
        pivot_row = jnp.broadcast_to(tiles[t][s : s + 1], (8, LANES))
        pivot = jnp.broadcast_to(pivot_row[:, j : j + 1], (8, LANES))
        scaled = pivot_row / pivot
        for q in range(t, size // 8):
            column = jnp.broadcast_to(tiles[q][:, j : j + 1], (8, LANES))
            if q == t:
                column = jnp.where(row > s, column, 0.0)
            tiles[q] = tiles[q] - column * scaled
    out = []
    for t, tile in enumerate(tiles):
        diagonal = jnp.sum(
            jnp.where(lane_of((8, LANES)) == row + 8 * t, tile, 0.0), axis=1, keepdims=True
        )
        out.append(tile * lax.rsqrt(diagonal))
    return jnp.concatenate(out, axis=0)


def basis_kernel(rank, gathered, sketch, basis, factor, turned):
    count = factor.shape[0]
    parts = gathered.shape[2] // LANES - 1
    total = gathered[0]
    for d in range(1, gathered.shape[0]):
        total = total + gathered[d]
    row = row_of((parts, LANES))
    body = jnp.zeros((parts, LANES), F32)
    for i in range(parts):
        body = jnp.where(row == i, total[:, i * LANES : (i + 1) * LANES], body)
    matrix = unpacked(body, total[:, parts * LANES :])
    row, lane = row_of(matrix.shape), lane_of(matrix.shape)
    matrix = jnp.where(lane == row + count, 1.0, matrix)
    done = factorize(matrix)
    upper = jnp.where((lane < count) & (lane >= row), done, 0.0)
    square = jnp.concatenate([upper, jnp.zeros((LANES - count, LANES), F32)], axis=0)
    factor[...] = square.T[:count, :count]
    inverse = pltpu.roll(done, count, 1)
    inverse = jnp.where((lane <= row) & (row < rank[0]), inverse, 0.0)
    high = inverse.astype(BF16).astype(F32)
    high, low = (x + pltpu.roll(x, count, 1) for x in (high, inverse - high))
    left = jnp.concatenate([high, low], axis=1).astype(BF16)
    rows = sketch.shape[0] // count
    width = sketch.shape[1]
    for r in range(rows):
        parts = split(sketch[r * count : (r + 1) * count, :])
        value = dot(left, jnp.concatenate([*parts, *parts], axis=0))
        for c in range(width // LANES):
            turned[c, pl.ds(r, count, stride=rows), :] = value[:, c * LANES : (c + 1) * LANES]
    for c in range(width // LANES):
        basis[:, :, c * LANES : (c + 1) * LANES] = turned[c].reshape(count, rows, LANES)


def ring(x, axis, step):
    size = lax.axis_size(axis)
    return lax.ppermute(x, axis, [(i, (i + step) % size) for i in range(size)])


def both_sides(x):
    other = ring(x, "obs", 1)
    return other, (other if lax.axis_size("obs") == 2 else ring(x, "obs", -1))


def all_shares(x, sides):
    size = lax.axis_size("obs")
    if size == 2:
        return [x, sides[0]]
    gathered = lax.all_gather(x, "obs")
    return [gathered[i] for i in range(size)]


def per_device(probes, velocity, viscosity, friction, obs_block, obs_weight, obs_prec, rank):
    count, rows, width = probes.shape
    share = obs_weight.shape[1]
    mesh_size, obs_size = lax.axis_size("mesh"), lax.axis_size("obs")
    slab_columns = width * obs_size // LANES
    cells = rows * width * mesh_size * obs_size
    height = count + PAD

    payload = (2 * count + share + 16, width)
    omega, up, down = call(
        edges_kernel,
        [((rows * count, width), F32), (payload, BF16), (payload, BF16)],
        (probes, velocity, viscosity, friction, obs_weight, obs_block, obs_prec),
        [pltpu.VMEM((width // LANES, rows * count, LANES), F32), pltpu.VMEM((16, width), F32)],
        name="edges",
    )
    from_up, from_down = ring(down, "mesh", 1), ring(up, "mesh", -1)

    forced, sent = call(
        forced_kernel,
        [((rows, height, width), F32), ((height + share + PAD, LANES), F32)],
        (omega, velocity, viscosity, obs_weight, obs_block, obs_prec),
        name="forced",
    )
    sides = both_sides(sent)
    observed = all_shares(sent, sides)
    (inner,) = call(
        functools.partial(inner_kernel, slab_columns, share),
        [(((rows - 2) * count, width), F32)],
        (forced, friction, *sides, *observed),
        name="inner",
    )
    near, far_sent = call(
        functools.partial(far_kernel, count, share),
        [((2, height, width), F32), ((height + 2 * (share + PAD), LANES), F32)],
        (from_up, from_down),
        name="far",
    )
    far_sides = both_sides(far_sent)
    far_observed = all_shares(far_sent, far_sides)
    outer, source_sent = call(
        functools.partial(outer_kernel, slab_columns, share),
        [((2 * count, width), F32), ((count, LANES), F32)],
        (forced, near, friction, *sides, inner, *observed),
        name="outer",
    )
    source_sides = both_sides(source_sent)
    (halo,) = call(
        functools.partial(halo_kernel, slab_columns, share),
        [((2 * count, width), F32)],
        (forced, near, from_up, from_down, *far_sides, *far_observed),
        name="halo",
    )
    sketch, gram, gram_diagonal = call(
        functools.partial(sketch_kernel, cells),
        [((rows * count, width), F32), ((16, LANES), F32), ((8, LANES), F32)],
        (forced, near, omega, velocity, friction, *sides, *source_sides, inner, outer, halo),
        name="sketch",
    )
    gram = jnp.concatenate([gram, gram_diagonal], axis=0)
    if obs_size == 2:
        other = ring(gram, "obs", 1)
    else:
        other = lax.psum(gram, "obs") - gram
    (pieces,) = call(
        spread_kernel,
        [((mesh_size, 1, 17 * LANES), F32)],
        (gram[:16], other[:16], gram[16:], other[16:]),
        name="spread",
    )
    gathered = lax.all_to_all(pieces, "mesh", 0, 0, tiled=True)
    basis, factor = pl.pallas_call(
        basis_kernel,
        out_shape=[
            jax.ShapeDtypeStruct((count, rows, width), F32),
            jax.ShapeDtypeStruct((count, count), F32),
        ],
        in_specs=[
            pl.BlockSpec(memory_space=pltpu.SMEM),
            pl.BlockSpec(memory_space=pltpu.VMEM),
            pl.BlockSpec(memory_space=pltpu.VMEM),
        ],
        scratch_shapes=[pltpu.VMEM((width // LANES, rows * count, LANES), F32)],
        compiler_params=pltpu.CompilerParams(vmem_limit_bytes=8 * 2**20),
        name="basis",
    )(rank, gathered, sketch)
    return basis, factor


def solution(mesh):
    in_specs = (
        P(None, "mesh", "obs"),
        P("mesh", "obs"),
        P("mesh", "obs"),
        P("mesh", "obs"),
        P("mesh", "obs"),
        P("mesh", "obs", None),
        P("mesh", "obs"),
        P(),
    )
    out_specs = (P(None, "mesh", "obs"), P())
    return jax.shard_map(
        per_device, mesh=mesh, in_specs=in_specs, out_specs=out_specs, check_vma=False
    )
```

time: 121 us -> 48.9 us (0.40)
  blocking collectives: 48.7 us -> 0 us
  other arithmetic: 36.9 us -> 0.01 us
  Pallas kernels: 0 us -> 13.9 us
  waiting for transfers between devices: 4.02 us -> 13.1 us
  starting transfers between devices: 20.3 us -> 14.3 us
  matrix products: 1.37 us -> 0 us
    psum x1 -> x0, blocking collectives: 43.6 us -> none  [per_device(): factor = jnp.linalg.cholesky(lax.psum(local_gram, ('mesh', 'obs')))]
    pallas_call x0 -> x9, Pallas kernels: none -> 13.9 us  [the longest x1 9.9 us: per_device(): pl.pallas_call(basis_kernel, out_shape=[jax.ShapeDtypeStruct((count, rows...]
    scatter-add x1 -> x0, other arithmetic: 13.5 us -> none  [per_device(): source = jnp.zeros((probe_count, rows_here * owned_blocks, BLOCK), jnp.fl...]
    ppermute x8 -> x6, starting transfers between devices: 20.3 us -> 7.63 us  [ring(): return lax.ppermute(x, axis, [(i, (i + step) % size) for i in range(size)])]
    another operation x5 -> x0, other arithmetic: 12.7 us -> none  [the longest x3 6.52 us: per_device(): factor = jnp.linalg.cholesky(lax.psum(local_gram, ('mesh', 'obs')))]
    all_to_all x0 -> x1, waiting for transfers between devices: none -> 7.22 us  [per_device(): gathered = lax.all_to_all(pieces, 'mesh', 0, 0, tiled=True)]
    all_to_all x0 -> x1, starting transfers between devices: none -> 6.68 us  [per_device(): gathered = lax.all_to_all(pieces, 'mesh', 0, 0, tiled=True)]
    select_n x3 -> x0, other arithmetic: 3.38 us -> none  [the longest x1 3.26 us: per_device(): jnp.where(inside[None, :, None], misfit[:, :, None] * weights[None], 0.0)]
  transfers between devices with their start and end apart: 8 -> 7, of which waited for: 2 -> 5; matrix products, arithmetic and copies ran while one was open for 3% -> 0% of each run, Pallas kernels for 0% -> 4%
where the time goes in v1:
time: 48.9 us; the launch traced here: 48.4 us
  starting transfers between devices  14.3 us (29%)
  Pallas kernels  13.9 us (28%)
  waiting for transfers between devices  13.1 us (27%)
  local copies, waits for them, and re-layouts  5.68 us (12%)
  between operations  1.38 us (3%)
    pallas_call x1, Pallas kernels, per_device(): pl.pallas_call(basis_kernel, out_shape=[jax.ShapeDtypeStruct((count, rows...  9.9 us
    ppermute x6, starting transfers between devices, ring(): return lax.ppermute(x, axis, [(i, (i + step) % size) for i in range(size)])  7.63 us
    all_to_all x1, waiting for transfers between devices, per_device(): gathered = lax.all_to_all(pieces, 'mesh', 0, 0, tiled=True)  7.22 us
    all_to_all x1, starting transfers between devices, per_device(): gathered = lax.all_to_all(pieces, 'mesh', 0, 0, tiled=True)  6.68 us
    ppermute x6, waiting for transfers between devices, ring(): return lax.ppermute(x, axis, [(i, (i + step) % size) for i in range(size)])  5.87 us
    unnamed x26, local copies, waits for them, and re-layouts  5.68 us
    pallas_call x8, Pallas kernels, call(): pl.pallas_call(body, out_shape=outs, scratch_shapes=list(scratch), compil...  3.99 us
  transfers between devices with their start and end apart: 7, of which 5 were waited for; matrix products, arithmetic and copies ran while one was open for 0% of the time, Pallas kernels for 4%

profile of v1, /device:TPU:0, one launch (start us, length us, event | category | flops | bytes accessed | tf_op | source)
XLA Modules:
  0.0 48.4 jit_solution(1081771177461749591)
XLA Ops:
  0.6 0.9 %copy-done = bf16[64,8,256]{2,1,0:T(8,128)(2,1)S(1)} copy-done((bf16[64,8,256]{2,1,0:T(8,128)(2,1)S(1)}, bf16[64,8,256]{2,1,0:T(8,128)(2,1)}, u32[]{:S(2)}) %copy-start) | copy-done | bytes 262168
  1.6 0.7 %copy-done.1 = f32[8,256]{1,0:T(8,128)S(1)} copy-done((f32[8,256]{1,0:T(8,128)S(1)}, f32[8,256]{1,0:T(8,128)}, u32[]{:S(2)}) %copy-start.1) | copy-done | bytes 8216
  2.3 0.8 %copy-done.3 = f32[1,64,128]{2,1,0:T(8,128)S(1)} copy-done((f32[1,64,128]{2,1,0:T(8,128)S(1)}, f32[1,64,128]{2,1,0:T(8,128)}, u32[]{:S(2)}) %copy-start.3) | copy-done | bytes 32792
  3.0 0.7 %copy-done.5 = f32[8,256]{1,0:T(8,128)S(1)} copy-done((f32[8,256]{1,0:T(8,128)S(1)}, f32[8,256]{1,0:T(8,128)}, u32[]{:S(2)}) %copy-start.5) | copy-done | bytes 8216
  3.7 0.7 %copy-done.7 = f32[8,256]{1,0:T(8,128)S(1)} copy-done((f32[8,256]{1,0:T(8,128)S(1)}, f32[8,256]{1,0:T(8,128)}, u32[]{:S(2)}) %copy-start.7) | copy-done | bytes 8216
  4.4 0.7 %copy-done.9 = s32[1,64]{1,0:T(1,128)S(1)} copy-done((s32[1,64]{1,0:T(1,128)S(1)}, s32[1,64]{1,0:T(1,128)}, u32[]{:S(2)}) %copy-start.9) | copy-done | bytes 280
  5.1 0.7 %copy-done.11 = f32[1,64]{1,0:T(1,128)S(1)} copy-done((f32[1,64]{1,0:T(1,128)S(1)}, f32[1,64]{1,0:T(1,128)}, u32[]{:S(2)}) %copy-start.11) | copy-done | bytes 280
  5.7 0.2 edges.1
  5.9 3.0 %collective-permute-start = (bf16[208,256]{1,0:T(8,128)(2,1)S(1)}, bf16[208,256]{1,0:T(8,128)(2,1)S(1)}, u32[]{:S(2)}, u32[]{:S(2)}) collective-permute-start(bf16[208,256]{1,0:T(8,128)(2,1)S(1)} %get-tuple-element.16), channel_id=1, source_target_pairs={{0,2},{2,4},{4,6},{6,8},{8,10},{10,12},{12,14},{14,16},{16,18},{18... | collective-permute-start | bytes 319496 | tf_op jit(solution)/shard_map/ppermute | solution.py:451
  8.9 4.1 %collective-permute-start.1 = (bf16[208,256]{1,0:T(8,128)(2,1)S(1)}, bf16[208,256]{1,0:T(8,128)(2,1)S(1)}, u32[]{:S(2)}, u32[]{:S(2)}) collective-permute-start(bf16[208,256]{1,0:T(8,128)(2,1)S(1)} %get-tuple-element.17), channel_id=1, source_target_pairs={{0,30},{2,0},{4,2},{6,4},{8,6},{10,8},{12,10},{14,12},{16,14},{18,... | collective-permute-start | bytes 319496 | tf_op jit(solution)/shard_map/ppermute | solution.py:451
  13.0 3.0 %collective-permute-done.from_up = bf16[208,256]{1,0:T(8,128)(2,1)S(1)} collective-permute-done((bf16[208,256]{1,0:T(8,128)(2,1)S(1)}, bf16[208,256]{1,0:T(8,128)(2,1)S(1)}, u32[]{:S(2)}, u32[]{:S(2)}) %collective-permute-start) | collective-permute-done | bytes 106528 | tf_op jit(solution)/shard_map/ppermute | solution.py:451
  16.0 0.1 far.1
  16.1 0.1 collective-permute-start.4
  16.2 0.5 copy-done.6
  16.7 0.0 copy-done.8
  16.7 0.1 copy-done.10
  16.8 0.0 copy-done.12
  16.8 0.2 forced.1
  17.0 0.1 collective-permute-start.2
  17.1 1.3 %collective-permute-done.2.from_left.from_right.rest_1_.visc_left.visc_right = f32[144,128]{1,0:T(8,128)S(1)} collective-permute-done((f32[144,128]{1,0:T(8,128)S(1)}, f32[144,128]{1,0:T(8,128)S(1)}, u32[]{:S(2)}, u32[]{:S(2)}) %collective-permute-start.2) | collective-permute-done | bytes 73760 | tf_op jit(solution)/shard_map/ppermute | solution.py:451
  18.4 0.7 %inner.1 = f32[384,256]{1,0:T(8,128)S(1)} custom-call(f32[8,72,256]{2,1,0:T(8,128)S(1)} %get-tuple-element.15.forced, f32[8,256]{1,0:T(8,128)S(1)} %copy-done.2, f32[144,128]{1,0:T(8,128)S(1)} %collective-permute-done.2.from_left.from_right.rest_1_.visc_left.visc_right, ...), custom_call_target="tpu_custom_call" | custom-call | bytes 1048576 | tf_op jit(solution)/shard_map/inner/pallas_call | solution.py:38
  19.1 0.5 %outer.1 = (f32[128,256]{1,0:T(8,128)S(1)}, f32[64,128]{1,0:T(8,128)S(1)}) custom-call(f32[8,72,256]{2,1,0:T(8,128)S(1)} %get-tuple-element.15.forced, f32[2,72,256]{2,1,0:T(8,128)S(1)} %get-tuple-element.18.near, f32[8,256]{1,0:T(8,128)S(1)} %copy-done.2, f32[144,128]{1,0:T(8,128)S(1)} %collective-permute-done.2.from_left.from_right.rest_1_.visc_left.visc_right, ...), custom_call_target="tpu_custom_call" | custom-call | bytes 1048576 | tf_op jit(solution)/shard_map/outer/pallas_call | solution.py:38
  19.6 0.2 collective-permute-start.3
  19.9 0.4 halo.1
  20.3 0.6 %collective-permute-done.3.from_left.from_right = f32[64,128]{1,0:T(8,128)S(1)} collective-permute-done((f32[64,128]{1,0:T(8,128)S(1)}, f32[64,128]{1,0:T(8,128)S(1)}, u32[]{:S(2)}, u32[]{:S(2)}) %collective-permute-start.3) | collective-permute-done | bytes 32800 | tf_op jit(solution)/shard_map/ppermute | solution.py:451
  20.9 1.0 %sketch.1 = (f32[512,256]{1,0:T(8,128)S(1)}, f32[16,128]{1,0:T(8,128)S(1)}, f32[8,128]{1,0:T(8,128)S(1)}) custom-call(f32[8,72,256]{2,1,0:T(8,128)S(1)} %get-tuple-element.15.forced, f32[2,72,256]{2,1,0:T(8,128)S(1)} %get-tuple-element.18.near, f32[512,256]{1,0:T(8,128)S(1)} %get-tuple-element.14.omega, f32[8,256]{1,0:T(8,128)S(1)} %copy-done.6, ...), custom_call_target="tpu_custom_call" | custom-call | bytes 1048576 | tf_op jit(solution)/shard_map/sketch/pallas_call | solution.py:38
  21.9 0.2 collective-permute-start.5
  22.2 1.0 %collective-permute-done.5 = f32[24,128]{1,0:T(8,128)S(1)} collective-permute-done((f32[24,128]{1,0:T(8,128)S(1)}, f32[24,128]{1,0:T(8,128)S(1)}, u32[]{:S(2)}, u32[]{:S(2)}) %collective-permute-start.5) | collective-permute-done | bytes 12320 | tf_op jit(solution)/shard_map/ppermute | solution.py:451
  23.2 0.7 %spread.1 = f32[16,1,2176]{2,1,0:T(1,128)} custom-call(f32[16,128]{1,0:T(8,128)S(1)} %get-tuple-element.23.body, f32[16,128]{1,0:T(8,128)S(1)} %slice.8.other_body, f32[8,128]{1,0:T(8,128)S(1)} %get-tuple-element.24.diagonal, f32[8,128]{1,0:T(8,128)S(1)} %slice.9.other_diagonal), custom_call_target="tpu_custom_call" | custom-call | bytes 1048576 | tf_op jit(solution)/shard_map/spread/pallas_call | solution.py:38
  23.9 6.7 %all-to-all-start = ((f32[16,1,2176]{2,1,0:T(1,128)}), f32[16,1,2176]{2,1,0:T(1,128)S(1)}, u32[]{:S(2)}, u32[]{:S(2)}) async-start(f32[16,1,2176]{2,1,0:T(1,128)} %spread.1), calls=%async_computation | async-start | bytes 278528 | tf_op jit(solution)/shard_map/all_to_all | solution.py:537
  31.2 7.2 %all-to-all-done.gathered = f32[16,1,2176]{2,1,0:T(1,128)S(1)} async-done(((f32[16,1,2176]{2,1,0:T(1,128)}), f32[16,1,2176]{2,1,0:T(1,128)S(1)}, u32[]{:S(2)}, u32[]{:S(2)}) %all-to-all-start) | async-done | bytes 139296 | tf_op jit(solution)/shard_map/all_to_all | solution.py:537
  38.5 9.9 %basis.1 = (f32[64,8,256]{2,1,0:T(8,128)}, f32[64,64]{1,0:T(8,128)}) custom-call(s32[1]{0:T(128)S(6)} %copy.10.rank, f32[16,1,2176]{2,1,0:T(1,128)S(1)} %all-to-all-done.gathered, f32[512,256]{1,0:T(8,128)S(1)} %get-tuple-element.25.sketch), custom_call_target="tpu_custom_call" | custom-call | tf_op jit(solution)/shard_map/basis/pallas_call | solution.py:538
  (20 shorter events, 0.0 us)
Async XLA Ops:
  0.6 1.0 %copy-start = (bf16[64,8,256]{2,1,0:T(8,128)(2,1)S(1)}, bf16[64,8,256]{2,1,0:T(8,128)(2,1)}, u32[]{:S(2)}) copy-start(bf16[64,8,256]{2,1,0:T(8,128)(2,1)} %probes.1) | copy-start | bytes 786436
  1.6 0.7 %copy-start.1 = (f32[8,256]{1,0:T(8,128)S(1)}, f32[8,256]{1,0:T(8,128)}, u32[]{:S(2)}) copy-start(f32[8,256]{1,0:T(8,128)} %friction.7) | copy-start | bytes 24580
  2.3 0.8 %copy-start.3 = (f32[1,64,128]{2,1,0:T(8,128)S(1)}, f32[1,64,128]{2,1,0:T(8,128)}, u32[]{:S(2)}) copy-start(f32[1,64,128]{2,1,0:T(8,128)} %weight.3) | copy-start | bytes 98308
  3.0 0.7 %copy-start.5 = (f32[8,256]{1,0:T(8,128)S(1)}, f32[8,256]{1,0:T(8,128)}, u32[]{:S(2)}) copy-start(f32[8,256]{1,0:T(8,128)} %velocity.5) | copy-start | bytes 24580
  3.7 0.7 %copy-start.7 = (f32[8,256]{1,0:T(8,128)S(1)}, f32[8,256]{1,0:T(8,128)}, u32[]{:S(2)}) copy-start(f32[8,256]{1,0:T(8,128)} %viscosity.3) | copy-start | bytes 24580
  4.4 0.7 %copy-start.9 = (s32[1,64]{1,0:T(1,128)S(1)}, s32[1,64]{1,0:T(1,128)}, u32[]{:S(2)}) copy-start(s32[1,64]{1,0:T(1,128)} %ids.3) | copy-start | bytes 772
  5.1 0.7 %copy-start.11 = (f32[1,64]{1,0:T(1,128)S(1)}, f32[1,64]{1,0:T(1,128)}, u32[]{:S(2)}) copy-start(f32[1,64]{1,0:T(1,128)} %precision.3) | copy-start | bytes 772
  5.9 10.1 %collective-permute-start = (bf16[208,256]{1,0:T(8,128)(2,1)S(1)}, bf16[208,256]{1,0:T(8,128)(2,1)S(1)}, u32[]{:S(2)}, u32[]{:S(2)}) collective-permute-start(bf16[208,256]{1,0:T(8,128)(2,1)S(1)} %get-tuple-element.16), channel_id=1, source_target_pairs={{0,2},{2,4},{4,6},{6,8},{8,10},{10,12},{12,14},{14,16},{16,18},{18... | collective-permute-start | bytes 319496 | tf_op jit(solution)/shard_map/ppermute | solution.py:451
  8.9 7.3 %copy-start.4 = (f32[1,64,128]{2,1,0:T(8,128)S(1)}, f32[1,64,128]{2,1,0:T(8,128)}, u32[]{:S(2)}) copy-start(f32[1,64,128]{2,1,0:T(8,128)} %weight.3) | copy-start | bytes 98308
  8.9 7.1 %collective-permute-start.1 = (bf16[208,256]{1,0:T(8,128)(2,1)S(1)}, bf16[208,256]{1,0:T(8,128)(2,1)S(1)}, u32[]{:S(2)}, u32[]{:S(2)}) collective-permute-start(bf16[208,256]{1,0:T(8,128)(2,1)S(1)} %get-tuple-element.17), channel_id=1, source_target_pairs={{0,30},{2,0},{4,2},{6,4},{8,6},{10,8},{12,10},{14,12},{16,14},{18,... | collective-permute-start | bytes 319496 | tf_op jit(solution)/shard_map/ppermute | solution.py:451
  16.0 0.7 %copy-start.6 = (f32[8,256]{1,0:T(8,128)S(1)}, f32[8,256]{1,0:T(8,128)}, u32[]{:S(2)}) copy-start(f32[8,256]{1,0:T(8,128)} %velocity.5) | copy-start | bytes 24580
  16.0 0.7 %copy-start.8 = (f32[8,256]{1,0:T(8,128)S(1)}, f32[8,256]{1,0:T(8,128)}, u32[]{:S(2)}) copy-start(f32[8,256]{1,0:T(8,128)} %viscosity.3) | copy-start | bytes 24580
  16.1 0.7 %copy-start.10 = (s32[1,64]{1,0:T(1,128)S(1)}, s32[1,64]{1,0:T(1,128)}, u32[]{:S(2)}) copy-start(s32[1,64]{1,0:T(1,128)} %ids.3) | copy-start | bytes 772
  16.1 0.7 %copy-start.12 = (f32[1,64]{1,0:T(1,128)S(1)}, f32[1,64]{1,0:T(1,128)}, u32[]{:S(2)}) copy-start(f32[1,64]{1,0:T(1,128)} %precision.3) | copy-start | bytes 772
  16.1 3.7 %collective-permute-start.4 = (f32[216,128]{1,0:T(8,128)S(1)}, f32[216,128]{1,0:T(8,128)S(1)}, u32[]{:S(2)}, u32[]{:S(2)}) collective-permute-start(f32[216,128]{1,0:T(8,128)S(1)} %get-tuple-element.22.rest_0_), channel_id=1, source_target_pairs={{0,1},{1,0},{2,3},{3,2},{4,5},{5,4},{6,7},{7,6},{8,9},{9,8},{10,11... | collective-permute-start | bytes 331784 | tf_op jit(solution)/shard_map/ppermute | solution.py:451
  16.8 1.6 %copy-start.2 = (f32[8,256]{1,0:T(8,128)S(1)}, f32[8,256]{1,0:T(8,128)}, u32[]{:S(2)}) copy-start(f32[8,256]{1,0:T(8,128)} %friction.7) | copy-start | bytes 24580
  17.0 1.3 %collective-permute-start.2 = (f32[144,128]{1,0:T(8,128)S(1)}, f32[144,128]{1,0:T(8,128)S(1)}, u32[]{:S(2)}, u32[]{:S(2)}) collective-permute-start(f32[144,128]{1,0:T(8,128)S(1)} %get-tuple-element.19.rest_0_), channel_id=1, source_target_pairs={{0,1},{1,0},{2,3},{3,2},{4,5},{5,4},{6,7},{7,6},{8,9},{9,8},{10,11... | collective-permute-start | bytes 221192 | tf_op jit(solution)/shard_map/ppermute | solution.py:451
  19.6 1.3 %collective-permute-start.3 = (f32[64,128]{1,0:T(8,128)S(1)}, f32[64,128]{1,0:T(8,128)S(1)}, u32[]{:S(2)}, u32[]{:S(2)}) collective-permute-start(f32[64,128]{1,0:T(8,128)S(1)} %get-tuple-element.20), channel_id=1, source_target_pairs={{0,1},{1,0},{2,3},{3,2},{4,5},{5,4},{6,7},{7,6},{8,9},{9,8},{10,11... | collective-permute-start | bytes 98312 | tf_op jit(solution)/shard_map/ppermute | solution.py:451
  21.9 1.2 %collective-permute-start.5 = (f32[24,128]{1,0:T(8,128)S(1)}, f32[24,128]{1,0:T(8,128)S(1)}, u32[]{:S(2)}, u32[]{:S(2)}) collective-permute-start(f32[24,128]{1,0:T(8,128)S(1)} %pad_maximum_fusion), channel_id=1, source_target_pairs={{0,1},{1,0},{2,3},{3,2},{4,5},{5,4},{6,7},{7,6},{8,9},{9,8},{10,11... | collective-permute-start | bytes 36872 | tf_op jit(solution)/shard_map/ppermute | solution.py:451
  23.9 14.6 %all-to-all-start = ((f32[16,1,2176]{2,1,0:T(1,128)}), f32[16,1,2176]{2,1,0:T(1,128)S(1)}, u32[]{:S(2)}, u32[]{:S(2)}) async-start(f32[16,1,2176]{2,1,0:T(1,128)} %spread.1), calls=%async_computation | async-start | bytes 278528 | tf_op jit(solution)/shard_map/all_to_all | solution.py:537

commit v2 on v1

--- a/solution.py
+++ b/solution.py
@@ -33,11 +33,14 @@
     )
 
 
-def call(body, outs, args, scratch=(), flops=0, name=None):
+def call(body, outs, args, scratch=(), flops=0, space=pltpu.VMEM, name=None):
+    if space != pltpu.VMEM:
+        args = [pltpu.with_memory_space_constraint(x, space) for x in args]
     outs = [jax.ShapeDtypeStruct(shape, kind) for shape, kind in outs]
     return pl.pallas_call(
         body,
         out_shape=outs,
+        in_specs=[pl.BlockSpec(memory_space=space)] * len(args),
         scratch_shapes=list(scratch),
         compiler_params=pltpu.CompilerParams(vmem_limit_bytes=8 * 2**20),
         cost_estimate=pl.CostEstimate(
@@ -137,16 +140,14 @@
     ]
 
 
-def own_share(weight_ref, ids_ref, precision_ref):
-    share = weight_ref.shape[1]
+def share_rows(ids, precision):
     out = jnp.zeros((PAD, LANES), F32)
-    row, lane = row_of(out.shape), lane_of(out.shape)
+    row = row_of(out.shape)
 
     def wide(x):
-        return jnp.concatenate([x, jnp.zeros((1, LANES - share), F32)], axis=1)
-
-    out = jnp.where(row == 0, wide(ids_ref[...].astype(F32)), out)
-    return jnp.where(row == 1, wide(precision_ref[...]), out)
+        return jnp.concatenate([x, jnp.zeros((1, LANES - x.shape[1]), F32)], axis=1)
+
+    return jnp.where(row == 0, wide(ids), jnp.where(row == 1, wide(precision), out))
 
 
 def read_share(ref, at, share):
@@ -155,67 +156,81 @@
     return high, low, ref[at + share : at + share + 1, :], ref[at + share + 1 : at + share + 2, :]
 
 
-def edges_kernel(probes, velocity, viscosity, friction, weight, ids, precision, omega, up, down, turned, small):
+def edges_kernel(
+    probes, velocity, viscosity, friction, weight, ids, precision,
+    omega, up, down, grid, owned, staged, staged_ids, staged_precision, turned, small, sems,
+):
     count, rows, width = probes.shape
     share = weight.shape[1]
+    copies = [
+        pltpu.make_async_copy(source, target, sems.at[i])
+        for i, (source, target) in enumerate(
+            (
+                (probes, staged),
+                (velocity, grid.at[0]),
+                (viscosity, grid.at[1]),
+                (friction, grid.at[2]),
+                (weight.at[0], owned.at[:share]),
+                (ids, staged_ids),
+                (precision, staged_precision),
+            )
+        )
+    ]
+    for copy in copies:
+        copy.start()
+    for copy in copies:
+        copy.wait()
+    owned[share:, :] = share_rows(staged_ids[...].astype(F32), staged_precision[...])
     for c in range(width // LANES):
         lanes = slice(c * LANES, (c + 1) * LANES)
-        turned[c] = probes[:, :, lanes].astype(F32).reshape(count * rows, LANES)
+        turned[c] = staged[:, :, lanes].astype(F32).reshape(count * rows, LANES)
         for r in range(rows):
             omega[r * count : (r + 1) * count, lanes] = turned[c, pl.ds(r, count, stride=rows), :]
-    meta = own_share(weight, ids, precision)
-    weight_high, weight_low = split(weight[0])
+    weights = jnp.concatenate(split(owned[:share, :]), axis=1)
     for out, near, next_near in ((up, 0, 1), (down, rows - 1, rows - 2)):
         out[:count, :] = omega[near * count : (near + 1) * count, :].astype(BF16)
         out[count : 2 * count, :] = omega[next_near * count : (next_near + 1) * count, :].astype(BF16)
-        out[2 * count : 2 * count + share, :] = jnp.concatenate([weight_high, weight_low], axis=1)
+        out[2 * count : 2 * count + share, :] = weights
         small[...] = jnp.zeros_like(small)
         at = 0
-        for ref, r in (
-            (velocity, near),
-            (velocity, next_near),
-            (viscosity, near),
-            (viscosity, next_near),
-            (friction, near),
-        ):
-            value = ref[r : r + 1, :]
+        for field, r in ((0, near), (0, next_near), (1, near), (1, next_near), (2, near)):
+            value = grid[field, r : r + 1, :]
             high = value.astype(BF16).astype(F32)
             small[at : at + 1, :] = high
             small[at + 1 : at + 2, :] = value - high
             at += 2
-        small[at : at + 1, :LANES] = meta[0:1]
-        high = meta[1:2].astype(BF16).astype(F32)
+        small[at : at + 1, :LANES] = owned[share : share + 1, :]
+        value = owned[share + 1 : share + 2, :]
+        high = value.astype(BF16).astype(F32)
         small[at + 1 : at + 2, :LANES] = high
-        small[at + 2 : at + 3, :LANES] = meta[1:2] - high
+        small[at + 2 : at + 3, :LANES] = value - high
         out[2 * count + share :, :] = small[...].astype(BF16)
 
 
-def forced_kernel(omega, velocity, viscosity, weight, ids, precision, forced, sent):
-    rows, width = velocity.shape
+def forced_kernel(omega, grid, owned, forced, sent):
+    _, rows, width = grid.shape
     count = omega.shape[0] // rows
-    share = weight.shape[1]
     blocks = []
     first = row_of((PAD, width)) == 0
     for r in range(rows):
         block = jnp.concatenate(
             [
-                velocity[r : r + 1, :] * omega[r * count : (r + 1) * count, :],
-                jnp.where(first, viscosity[r : r + 1, :], 0.0),
+                grid[0, r : r + 1, :] * omega[r * count : (r + 1) * count, :],
+                jnp.where(first, grid[1, r : r + 1, :], 0.0),
             ],
             axis=0,
         )
         forced[r] = block
         blocks.append(block)
     sent[: count + PAD, :] = edge_columns(blocks)
-    sent[count + PAD : count + PAD + share, :] = weight[0]
-    sent[count + PAD + share :, :] = own_share(weight, ids, precision)
+    sent[count + PAD :, :] = owned[...]
 
 
 def shares_of(refs, at, share):
     return [read_share(ref, at, share) for ref in refs]
 
 
-def inner_kernel(slab_columns, share, forced, friction, from_left, from_right, *rest):
+def inner_kernel(slab_columns, share, forced, grid, from_left, from_right, *rest):
     *observed, out = rest
     rows, height, width = forced.shape
     count = height - PAD
@@ -224,7 +239,7 @@
     for r in inner:
         edges = edges_from(from_left, from_right, slice(0, height), r)
         tangents.append(
-            tangent_row(count, forced[r], forced[r - 1], forced[r + 1], *edges, friction[r : r + 1, :])
+            tangent_row(count, forced[r], forced[r - 1], forced[r + 1], *edges, grid[2, r : r + 1, :])
         )
     result = sources(tangents, inner, shares_of(observed, height, share), slab_columns)
     for i, x in enumerate(result):
@@ -237,7 +252,7 @@
     return parts, small[10:11, :LANES], small[11:12, :LANES] + small[12:13, :LANES]
 
 
-def far_kernel(count, share, from_up, from_down, near, sent):
+def far_kernel(count, share, from_up, from_down, inner, near, sent):
     blocks = []
     edge = lax.axis_index("mesh"), lax.axis_size("mesh") - 1
     width = from_up.shape[1]
@@ -261,7 +276,7 @@
     sent[: count + PAD, :] = edge_columns(blocks)
 
 
-def outer_kernel(slab_columns, share, forced, near, friction, from_left, from_right, inner, *rest):
+def outer_kernel(slab_columns, share, forced, near, grid, from_left, from_right, inner, *rest):
     *observed, out, sent = rest
     rows, height, width = forced.shape
     count = height - PAD
@@ -271,7 +286,7 @@
         edges = edges_from(from_left, from_right, slice(0, height), r)
         above = near[0] if r == 0 else forced[r - 1]
         below = near[1] if r == rows - 1 else forced[r + 1]
-        tangents.append(tangent_row(count, forced[r], above, below, *edges, friction[r : r + 1, :]))
+        tangents.append(tangent_row(count, forced[r], above, below, *edges, grid[2, r : r + 1, :]))
     first, last = sources(tangents, outer, shares_of(observed, height, share), slab_columns)
     out[:count, :] = first
     out[count:, :] = last
@@ -345,8 +360,8 @@
 
 
 def sketch_kernel(
-    cells, forced, near, omega, velocity, friction, visc_left, visc_right,
-    from_left, from_right, inner, outer, halo, sketch, gram, gram_diagonal,
+    cells, forced, near, omega, grid, visc_left, visc_right,
+    from_left, from_right, inner, outer, halo, sketch, gram,
 ):
     rows, height, width = forced.shape
     count = height - PAD
@@ -363,10 +378,10 @@
         visc_side = shifted(
             visc, *edges_from(visc_left, visc_right, slice(count, count + 1), r)
         )
-        gradient = velocity[r : r + 1, :] * operate_row(
+        gradient = grid[0, r : r + 1, :] * operate_row(
             centre, values[r], values[r + 2], left, right,
             [visc, viscs[r], viscs[r + 2], *visc_side],
-            friction[r : r + 1, :],
+            grid[2, r : r + 1, :],
         )
         value = gradient + omega[r * count : (r + 1) * count, :]
         sketch[r * count : (r + 1) * count, :] = value
@@ -375,55 +390,53 @@
     total = total + pltpu.roll(total, count, 1)
     total = (total[:count] + total[count:]) / cells
     body, diagonal = packed(total)
-    gram[...] = body
-    gram_diagonal[...] = jnp.broadcast_to(diagonal, gram_diagonal.shape)
-
-
-def spread_kernel(body, other_body, diagonal, other_diagonal, out):
-    total = body[...] + other_body[...]
-    last = diagonal[0:1, :] + other_diagonal[0:1, :]
-    for i in range(total.shape[0]):
-        row = total[i : i + 1, :]
-        for d in range(out.shape[0]):
-            out[d, :, i * LANES : (i + 1) * LANES] = row
-    for d in range(out.shape[0]):
-        out[d, :, total.shape[0] * LANES :] = last
+    for i in range(body.shape[0]):
+        gram[:, i * LANES : (i + 1) * LANES] = body[i : i + 1, :]
+    gram[:, body.shape[0] * LANES :] = diagonal
 
 
 def factorize(matrix):
     size = matrix.shape[0]
     row = row_of((8, LANES))
-    tiles = [matrix[8 * t : 8 * t + 8] for t in range(size // 8)]
-    for j in range(size):
-        t, s = divmod(j, 8)
-        pivot_row = jnp.broadcast_to(tiles[t][s : s + 1], (8, LANES))
-        pivot = jnp.broadcast_to(pivot_row[:, j : j + 1], (8, LANES))
-        scaled = pivot_row / pivot
-        for q in range(t, size // 8):
-            column = jnp.broadcast_to(tiles[q][:, j : j + 1], (8, LANES))
-            if q == t:
-                column = jnp.where(row > s, column, 0.0)
-            tiles[q] = tiles[q] - column * scaled
-    out = []
-    for t, tile in enumerate(tiles):
-        diagonal = jnp.sum(
-            jnp.where(lane_of((8, LANES)) == row + 8 * t, tile, 0.0), axis=1, keepdims=True
-        )
-        out.append(tile * lax.rsqrt(diagonal))
-    return jnp.concatenate(out, axis=0)
-
-
-def basis_kernel(rank, gathered, sketch, basis, factor, turned):
+    tiles = [matrix[t : t + 8] for t in range(0, size, 8)]
+    whole = functools.partial(jnp.broadcast_to, shape=(8, LANES))
+    for t in range(size // 8):
+        later = range(t + 1, size // 8)
+        columns = {
+            q: [whole(tiles[q][:, j : j + 1]) for j in range(8 * t, 8 * t + 8)]
+            for q in (t, *later)
+        }
+        square = [
+            [whole(columns[t][c][d : d + 1]) if d >= c else None for d in range(8)] for c in range(8)
+        ]
+        rows = [whole(tiles[t][c : c + 1]) for c in range(8)]
+        for c in range(8):
+            root = lax.rsqrt(square[c][c])
+            rows[c] = rows[c] * root
+            left = [square[c][d] * root if d > c else None for d in range(8)]
+            for d in range(c + 1, 8):
+                for e in range(d, 8):
+                    square[d][e] = square[d][e] - left[d] * left[e]
+                rows[d] = rows[d] - left[d] * rows[c]
+            for q in later:
+                columns[q][c] = columns[q][c] * root
+                for d in range(c + 1, 8):
+                    columns[q][d] = columns[q][d] - left[d] * columns[q][c]
+                tiles[q] = tiles[q] - columns[q][c] * rows[c]
+        tiles[t] = rows[0]
+        for c in range(1, 8):
+            tiles[t] = jnp.where(row == c, rows[c], tiles[t])
+    return jnp.concatenate(tiles, axis=0)
+
+
+def basis_kernel(rank, gram, sketch, basis, factor, turned):
     count = factor.shape[0]
-    parts = gathered.shape[2] // LANES - 1
-    total = gathered[0]
-    for d in range(1, gathered.shape[0]):
-        total = total + gathered[d]
+    parts = gram.shape[1] // LANES - 1
     row = row_of((parts, LANES))
     body = jnp.zeros((parts, LANES), F32)
     for i in range(parts):
-        body = jnp.where(row == i, total[:, i * LANES : (i + 1) * LANES], body)
-    matrix = unpacked(body, total[:, parts * LANES :])
+        body = jnp.where(row == i, gram[:, i * LANES : (i + 1) * LANES], body)
+    matrix = unpacked(body, gram[:, parts * LANES :])
     row, lane = row_of(matrix.shape), lane_of(matrix.shape)
     matrix = jnp.where(lane == row + count, 1.0, matrix)
     done = factorize(matrix)
@@ -473,11 +486,25 @@
     height = count + PAD
 
     payload = (2 * count + share + 16, width)
-    omega, up, down = call(
+    omega, up, down, grid, owned = call(
         edges_kernel,
-        [((rows * count, width), F32), (payload, BF16), (payload, BF16)],
+        [
+            ((rows * count, width), F32),
+            (payload, BF16),
+            (payload, BF16),
+            ((3, rows, width), F32),
+            ((share + PAD, LANES), F32),
+        ],
         (probes, velocity, viscosity, friction, obs_weight, obs_block, obs_prec),
-        [pltpu.VMEM((width // LANES, rows * count, LANES), F32), pltpu.VMEM((16, width), F32)],
+        [
+            pltpu.VMEM(probes.shape, probes.dtype),
+            pltpu.VMEM(obs_block.shape, obs_block.dtype),
+            pltpu.VMEM(obs_prec.shape, F32),
+            pltpu.VMEM((width // LANES, rows * count, LANES), F32),
+            pltpu.VMEM((16, width), F32),
+            pltpu.SemaphoreType.DMA((7,)),
+        ],
+        space=pltpu.HBM,
         name="edges",
     )
     from_up, from_down = ring(down, "mesh", 1), ring(up, "mesh", -1)
@@ -485,7 +512,7 @@
     forced, sent = call(
         forced_kernel,
         [((rows, height, width), F32), ((height + share + PAD, LANES), F32)],
-        (omega, velocity, viscosity, obs_weight, obs_block, obs_prec),
+        (omega, grid, owned),
         name="forced",
     )
     sides = both_sides(sent)
@@ -493,13 +520,13 @@
     (inner,) = call(
         functools.partial(inner_kernel, slab_columns, share),
         [(((rows - 2) * count, width), F32)],
-        (forced, friction, *sides, *observed),
+        (forced, grid, *sides, *observed),
         name="inner",
     )
     near, far_sent = call(
         functools.partial(far_kernel, count, share),
         [((2, height, width), F32), ((height + 2 * (share + PAD), LANES), F32)],
-        (from_up, from_down),
+        (from_up, from_down, inner),
         name="far",
     )
     far_sides = both_sides(far_sent)
@@ -507,7 +534,7 @@
     outer, source_sent = call(
         functools.partial(outer_kernel, slab_columns, share),
         [((2 * count, width), F32), ((count, LANES), F32)],
-        (forced, near, friction, *sides, inner, *observed),
+        (forced, near, grid, *sides, inner, *observed),
         name="outer",
     )
     source_sides = both_sides(source_sent)
@@ -517,24 +544,15 @@
         (forced, near, from_up, from_down, *far_sides, *far_observed),
         name="halo",
     )
-    sketch, gram, gram_diagonal = call(
+    sketch, gram = call(
         functools.partial(sketch_kernel, cells),
-        [((rows * count, width), F32), ((16, LANES), F32), ((8, LANES), F32)],
-        (forced, near, omega, velocity, friction, *sides, *source_sides, inner, outer, halo),
+        [((rows * count, width), F32), ((1, 17 * LANES), F32)],
+        (forced, near, omega, grid, *sides, *source_sides, inner, outer, halo),
         name="sketch",
     )
-    gram = jnp.concatenate([gram, gram_diagonal], axis=0)
-    if obs_size == 2:
-        other = ring(gram, "obs", 1)
-    else:
-        other = lax.psum(gram, "obs") - gram
-    (pieces,) = call(
-        spread_kernel,
-        [((mesh_size, 1, 17 * LANES), F32)],
-        (gram[:16], other[:16], gram[16:], other[16:]),
-        name="spread",
-    )
-    gathered = lax.all_to_all(pieces, "mesh", 0, 0, tiled=True)
+    gram = gram + ring(gram, "obs", 1) if obs_size == 2 else lax.psum(gram, "obs")
+    pieces = jnp.broadcast_to(gram, (mesh_size, *gram.shape))
+    gram = jnp.sum(lax.all_to_all(pieces, "mesh", 0, 0, tiled=True), axis=0)
     basis, factor = pl.pallas_call(
         basis_kernel,
         out_shape=[
@@ -549,7 +567,7 @@
         scratch_shapes=[pltpu.VMEM((width // LANES, rows * count, LANES), F32)],
         compiler_params=pltpu.CompilerParams(vmem_limit_bytes=8 * 2**20),
         name="basis",
-    )(rank, gathered, sketch)
+    )(rank, gram, sketch)
     return basis, factor
 
 

time: 48.9 us -> 35.4 us (0.72)
  Pallas kernels: 13.9 us -> 7.55 us
  local copies, waits for them, and re-layouts: 5.68 us -> 0.74 us
  waiting for transfers between devices: 13.1 us -> 10.6 us
  starting transfers between devices: 14.3 us -> 14.8 us
    pallas_call x1, Pallas kernels: 9.9 us -> 3.27 us  [per_device(): pl.pallas_call(basis_kernel, out_shape=[jax.ShapeDtypeStruct((count, rows...]
    unnamed x26 -> x0, local copies, waits for them, and re-layouts: 5.68 us -> none
    ppermute x6, waiting for transfers between devices: 5.87 us -> 3.17 us  [ring(): return lax.ppermute(x, axis, [(i, (i + step) % size) for i in range(size)])]
    broadcast_in_dim x0 -> x1, local copies, waits for them, and re-layouts: none -> 0.73 us  [per_device(): pieces = jnp.broadcast_to(gram, (mesh_size, *gram.shape))]
    ppermute x6, starting transfers between devices: 7.63 us -> 8.17 us  [ring(): return lax.ppermute(x, axis, [(i, (i + step) % size) for i in range(size)])]
    pallas_call x8 -> x7, Pallas kernels: 3.99 us -> 4.28 us  [call(): pl.pallas_call(body, out_shape=outs, in_specs=[pl.BlockSpec(memory_space=...]
  transfers between devices with their start and end apart: 7 -> 7, of which waited for: 5 -> 6; matrix products, arithmetic and copies ran while one was open for 0% -> 0% of each run, Pallas kernels for 4% -> 6%
where the time goes in v2:
time: 35.4 us; the launch traced here: 35.2 us
  starting transfers between devices  14.8 us (42%)
  waiting for transfers between devices  10.6 us (30%)
  Pallas kernels  7.55 us (21%)
  between operations  1.37 us (4%)
  local copies, waits for them, and re-layouts  0.74 us (2%)
    ppermute x6, starting transfers between devices, ring(): return lax.ppermute(x, axis, [(i, (i + step) % size) for i in range(size)])  8.17 us
    all_to_all x1, waiting for transfers between devices, per_device(): gram = jnp.sum(lax.all_to_all(pieces, 'mesh', 0, 0, tiled=True), axis=0)  7.39 us
    all_to_all x1, starting transfers between devices, per_device(): gram = jnp.sum(lax.all_to_all(pieces, 'mesh', 0, 0, tiled=True), axis=0)  6.67 us
    pallas_call x7, Pallas kernels, call(): pl.pallas_call(body, out_shape=outs, in_specs=[pl.BlockSpec(memory_space=...  4.28 us
    pallas_call x1, Pallas kernels, per_device(): pl.pallas_call(basis_kernel, out_shape=[jax.ShapeDtypeStruct((count, rows...  3.27 us
    ppermute x6, waiting for transfers between devices, ring(): return lax.ppermute(x, axis, [(i, (i + step) % size) for i in range(size)])  3.17 us
    broadcast_in_dim x1, local copies, waits for them, and re-layouts, per_device(): pieces = jnp.broadcast_to(gram, (mesh_size, *gram.shape))  0.73 us
  transfers between devices with their start and end apart: 7, of which 6 were waited for; matrix products, arithmetic and copies ran while one was open for 0% of the time, Pallas kernels for 6%

profile of v2, /device:TPU:0, one launch (start us, length us, event | category | flops | bytes accessed | tf_op | source)
XLA Modules:
  0.0 35.2 jit_solution(221858654063933910)
XLA Ops:
  0.6 1.2 %edges.1 = (f32[512,256]{1,0:T(8,128)S(1)}, bf16[208,256]{1,0:T(8,128)(2,1)S(1)}, bf16[208,256]{1,0:T(8,128)(2,1)S(1)}, f32[3,8,256]{2,1,0:T(8,128)S(1)}, f32[72,128]{1,0:T(8,128)S(1)}) custom-call(bf16[64,8,256]{2,1,0:T(8,128)(2,1)} %probes.1, f32[8,256]{1,0:T(8,128)} %velocity.1, f32[8,256]{1,0:T(8,128)} %viscosity.1, f32[8,256]{1,0:T(8,128)} %friction.1, ...), custom_call_target="tpu_custom_call" | custom-call | bytes 1048576 | tf_op jit(solution)/shard_map/edges/pallas_call | solution.py:40
  1.8 3.0 %collective-permute-start = (bf16[208,256]{1,0:T(8,128)(2,1)S(1)}, bf16[208,256]{1,0:T(8,128)(2,1)S(1)}, u32[]{:S(2)}, u32[]{:S(2)}) collective-permute-start(bf16[208,256]{1,0:T(8,128)(2,1)S(1)} %get-tuple-element.19), channel_id=1, source_target_pairs={{0,2},{2,4},{4,6},{6,8},{8,10},{10,12},{12,14},{14,16},{16,18},{18... | collective-permute-start | bytes 319496 | tf_op jit(solution)/shard_map/ppermute | solution.py:464
  4.8 4.1 %collective-permute-start.1 = (bf16[208,256]{1,0:T(8,128)(2,1)S(1)}, bf16[208,256]{1,0:T(8,128)(2,1)S(1)}, u32[]{:S(2)}, u32[]{:S(2)}) collective-permute-start(bf16[208,256]{1,0:T(8,128)(2,1)S(1)} %get-tuple-element.20), channel_id=1, source_target_pairs={{0,30},{2,0},{4,2},{6,4},{8,6},{10,8},{12,10},{14,12},{16,14},{18,... | collective-permute-start | bytes 319496 | tf_op jit(solution)/shard_map/ppermute | solution.py:464
  8.9 0.2 forced.1
  9.1 0.1 collective-permute-start.2
  9.2 1.3 %collective-permute-done.2.from_left.from_right.rest_1_.visc_left.visc_right = f32[144,128]{1,0:T(8,128)S(1)} collective-permute-done((f32[144,128]{1,0:T(8,128)S(1)}, f32[144,128]{1,0:T(8,128)S(1)}, u32[]{:S(2)}, u32[]{:S(2)}) %collective-permute-start.2) | collective-permute-done | bytes 73760 | tf_op jit(solution)/shard_map/ppermute | solution.py:464
  10.5 0.7 %inner.1 = f32[384,256]{1,0:T(8,128)S(1)} custom-call(f32[8,72,256]{2,1,0:T(8,128)S(1)} %get-tuple-element.18.forced, f32[3,8,256]{2,1,0:T(8,128)S(1)} %get-tuple-element.16.grid, f32[144,128]{1,0:T(8,128)S(1)} %collective-permute-done.2.from_left.from_right.rest_1_.visc_left.visc_right, ...), custom_call_target="tpu_custom_call" | custom-call | bytes 1048576 | tf_op jit(solution)/shard_map/inner/pallas_call | solution.py:40
  11.2 0.7 %collective-permute-done.from_up = bf16[208,256]{1,0:T(8,128)(2,1)S(1)} collective-permute-done((bf16[208,256]{1,0:T(8,128)(2,1)S(1)}, bf16[208,256]{1,0:T(8,128)(2,1)S(1)}, u32[]{:S(2)}, u32[]{:S(2)}) %collective-permute-start) | collective-permute-done | bytes 106528 | tf_op jit(solution)/shard_map/ppermute | solution.py:464
  11.9 0.0 collective-permute-done.1.from_down
  11.9 0.1 far.1
  12.0 0.1 collective-permute-start.4
  12.1 0.5 %outer.1 = (f32[128,256]{1,0:T(8,128)S(1)}, f32[64,128]{1,0:T(8,128)S(1)}) custom-call(f32[8,72,256]{2,1,0:T(8,128)S(1)} %get-tuple-element.18.forced, f32[2,72,256]{2,1,0:T(8,128)S(1)} %get-tuple-element.22.near, f32[3,8,256]{2,1,0:T(8,128)S(1)} %get-tuple-element.16.grid, ...), custom_call_target="tpu_custom_call" | custom-call | bytes 1048576 | tf_op jit(solution)/shard_map/outer/pallas_call | solution.py:40
  12.6 0.6 %collective-permute-start.3 = (f32[64,128]{1,0:T(8,128)S(1)}, f32[64,128]{1,0:T(8,128)S(1)}, u32[]{:S(2)}, u32[]{:S(2)}) collective-permute-start(f32[64,128]{1,0:T(8,128)S(1)} %get-tuple-element.23), channel_id=1, source_target_pairs={{0,1},{1,0},{2,3},{3,2},{4,5},{5,4},{6,7},{7,6},{8,9},{9,8},{10,11... | collective-permute-start | bytes 98312 | tf_op jit(solution)/shard_map/ppermute | solution.py:464
  13.2 0.2 collective-permute-done.4.from_left.from_right.rest_1_
  13.4 0.4 %halo.1 = f32[128,256]{1,0:T(8,128)S(1)} custom-call(f32[8,72,256]{2,1,0:T(8,128)S(1)} %get-tuple-element.18.forced, f32[2,72,256]{2,1,0:T(8,128)S(1)} %get-tuple-element.22.near, bf16[208,256]{1,0:T(8,128)(2,1)S(1)} %collective-permute-done.from_up, bf16[208,256]{1,0:T(8,128)(2,1)S(1)} %collective-permute-done.1.from_down, ...), custom_call_target="tpu_custom_call" | custom-call | bytes 1048576 | tf_op jit(solution)/shard_map/halo/pallas_call | solution.py:40
  13.9 0.2 collective-permute-done.3.from_left.from_right
  14.0 1.0 %sketch.1 = (f32[512,256]{1,0:T(8,128)S(1)}, f32[1,2176]{1,0:T(1,128)S(1)}) custom-call(f32[8,72,256]{2,1,0:T(8,128)S(1)} %get-tuple-element.18.forced, f32[2,72,256]{2,1,0:T(8,128)S(1)} %get-tuple-element.22.near, f32[512,256]{1,0:T(8,128)S(1)} %get-tuple-element.15.omega, f32[3,8,256]{2,1,0:T(8,128)S(1)} %get-tuple-element.16.grid, ...), custom_call_target="tpu_custom_call" | custom-call | bytes 1048576 | tf_op jit(solution)/shard_map/sketch/pallas_call | solution.py:40
  15.1 0.4 %collective-permute-start.5 = (f32[1,2176]{1,0:T(1,128)S(1)}, f32[1,2176]{1,0:T(1,128)S(1)}, u32[]{:S(2)}, u32[]{:S(2)}) collective-permute-start(f32[1,2176]{1,0:T(1,128)S(1)} %get-tuple-element.26), channel_id=1, source_target_pairs={{0,1},{1,0},{2,3},{3,2},{4,5},{5,4},{6,7},{7,6},{8,9},{9,8},{10,11... | collective-permute-start | bytes 26120 | tf_op jit(solution)/shard_map/ppermute | solution.py:464
  15.5 0.8 %collective-permute-done.5 = f32[1,2176]{1,0:T(1,128)S(1)} collective-permute-done((f32[1,2176]{1,0:T(1,128)S(1)}, f32[1,2176]{1,0:T(1,128)S(1)}, u32[]{:S(2)}, u32[]{:S(2)}) %collective-permute-start.5) | collective-permute-done | bytes 8736 | tf_op jit(solution)/shard_map/ppermute | solution.py:464
  16.3 0.7 %broadcast_in_dim.3 = f32[16,1,2176]{2,1,0:T(1,128)} broadcast(f32[2176]{0:T(1024)S(1)} %add_reduce_fusion), dimensions={2} | broadcast | bytes 147968 | tf_op jit(solution)/shard_map/broadcast_in_dim | solution.py:554
  17.1 6.7 %all-to-all-start = ((f32[16,1,2176]{2,1,0:T(1,128)}), f32[16,1,2176]{2,1,0:T(1,128)S(1)}, u32[]{:S(2)}, u32[]{:S(2)}) async-start(f32[16,1,2176]{2,1,0:T(1,128)} %broadcast_in_dim.3), calls=%async_computation | async-start | bytes 278528 | tf_op jit(solution)/shard_map/all_to_all | solution.py:555
  24.4 7.4 %all-to-all-done = f32[16,1,2176]{2,1,0:T(1,128)S(1)} async-done(((f32[16,1,2176]{2,1,0:T(1,128)}), f32[16,1,2176]{2,1,0:T(1,128)S(1)}, u32[]{:S(2)}, u32[]{:S(2)}) %all-to-all-start) | async-done | bytes 139296 | tf_op jit(solution)/shard_map/all_to_all | solution.py:555
  31.8 0.1 reduce_sum.11
  31.9 3.3 %basis.1 = (f32[64,8,256]{2,1,0:T(8,128)}, f32[64,64]{1,0:T(8,128)}) custom-call(s32[1]{0:T(128)S(6)} %copy.12.rank, f32[1,2176]{1,0:T(1,128)S(1)} %reduce_sum.12.gram, f32[512,256]{1,0:T(8,128)S(1)} %get-tuple-element.27.sketch), custom_call_target="tpu_custom_call" | custom-call | tf_op jit(solution)/shard_map/basis/pallas_call | solution.py:556
  (2 shorter events, 0.0 us)
Async XLA Ops:
  1.8 10.1 %collective-permute-start = (bf16[208,256]{1,0:T(8,128)(2,1)S(1)}, bf16[208,256]{1,0:T(8,128)(2,1)S(1)}, u32[]{:S(2)}, u32[]{:S(2)}) collective-permute-start(bf16[208,256]{1,0:T(8,128)(2,1)S(1)} %get-tuple-element.19), channel_id=1, source_target_pairs={{0,2},{2,4},{4,6},{6,8},{8,10},{10,12},{12,14},{14,16},{16,18},{18... | collective-permute-start | bytes 319496 | tf_op jit(solution)/shard_map/ppermute | solution.py:464
  4.8 7.1 %collective-permute-start.1 = (bf16[208,256]{1,0:T(8,128)(2,1)S(1)}, bf16[208,256]{1,0:T(8,128)(2,1)S(1)}, u32[]{:S(2)}, u32[]{:S(2)}) collective-permute-start(bf16[208,256]{1,0:T(8,128)(2,1)S(1)} %get-tuple-element.20), channel_id=1, source_target_pairs={{0,30},{2,0},{4,2},{6,4},{8,6},{10,8},{12,10},{14,12},{16,14},{18,... | collective-permute-start | bytes 319496 | tf_op jit(solution)/shard_map/ppermute | solution.py:464
  9.1 1.3 %collective-permute-start.2 = (f32[144,128]{1,0:T(8,128)S(1)}, f32[144,128]{1,0:T(8,128)S(1)}, u32[]{:S(2)}, u32[]{:S(2)}) collective-permute-start(f32[144,128]{1,0:T(8,128)S(1)} %get-tuple-element.21.rest_0_), channel_id=1, source_target_pairs={{0,1},{1,0},{2,3},{3,2},{4,5},{5,4},{6,7},{7,6},{8,9},{9,8},{10,11... | collective-permute-start | bytes 221192 | tf_op jit(solution)/shard_map/ppermute | solution.py:464
  12.0 1.4 %collective-permute-start.4 = (f32[216,128]{1,0:T(8,128)S(1)}, f32[216,128]{1,0:T(8,128)S(1)}, u32[]{:S(2)}, u32[]{:S(2)}) collective-permute-start(f32[216,128]{1,0:T(8,128)S(1)} %get-tuple-element.25.rest_0_), channel_id=1, source_target_pairs={{0,1},{1,0},{2,3},{3,2},{4,5},{5,4},{6,7},{7,6},{8,9},{9,8},{10,11... | collective-permute-start | bytes 331784 | tf_op jit(solution)/shard_map/ppermute | solution.py:464
  12.6 1.4 %collective-permute-start.3 = (f32[64,128]{1,0:T(8,128)S(1)}, f32[64,128]{1,0:T(8,128)S(1)}, u32[]{:S(2)}, u32[]{:S(2)}) collective-permute-start(f32[64,128]{1,0:T(8,128)S(1)} %get-tuple-element.23), channel_id=1, source_target_pairs={{0,1},{1,0},{2,3},{3,2},{4,5},{5,4},{6,7},{7,6},{8,9},{9,8},{10,11... | collective-permute-start | bytes 98312 | tf_op jit(solution)/shard_map/ppermute | solution.py:464
  15.1 1.2 %collective-permute-start.5 = (f32[1,2176]{1,0:T(1,128)S(1)}, f32[1,2176]{1,0:T(1,128)S(1)}, u32[]{:S(2)}, u32[]{:S(2)}) collective-permute-start(f32[1,2176]{1,0:T(1,128)S(1)} %get-tuple-element.26), channel_id=1, source_target_pairs={{0,1},{1,0},{2,3},{3,2},{4,5},{5,4},{6,7},{7,6},{8,9},{9,8},{10,11... | collective-permute-start | bytes 26120 | tf_op jit(solution)/shard_map/ppermute | solution.py:464
  17.1 14.7 %all-to-all-start = ((f32[16,1,2176]{2,1,0:T(1,128)}), f32[16,1,2176]{2,1,0:T(1,128)S(1)}, u32[]{:S(2)}, u32[]{:S(2)}) async-start(f32[16,1,2176]{2,1,0:T(1,128)} %broadcast_in_dim.3), calls=%async_computation | async-start | bytes 278528 | tf_op jit(solution)/shard_map/all_to_all | solution.py:555

commit v3 on v2

--- a/solution.py
+++ b/solution.py
@@ -158,7 +158,7 @@
 
 def edges_kernel(
     probes, velocity, viscosity, friction, weight, ids, precision,
-    omega, up, down, grid, owned, staged, staged_ids, staged_precision, turned, small, sems,
+    omega, first, second, grid, owned, staged, staged_ids, staged_precision, turned, small, sems,
 ):
     count, rows, width = probes.shape
     share = weight.shape[1]
@@ -186,15 +186,21 @@
         turned[c] = staged[:, :, lanes].astype(F32).reshape(count * rows, LANES)
         for r in range(rows):
             omega[r * count : (r + 1) * count, lanes] = turned[c, pl.ds(r, count, stride=rows), :]
-    weights = jnp.concatenate(split(owned[:share, :]), axis=1)
-    for out, near, next_near in ((up, 0, 1), (down, rows - 1, rows - 2)):
-        out[:count, :] = omega[near * count : (near + 1) * count, :].astype(BF16)
-        out[count : 2 * count, :] = omega[next_near * count : (next_near + 1) * count, :].astype(BF16)
-        out[2 * count : 2 * count + share, :] = weights
+    half = share // 2
+    weights = owned[:share, :].astype(BF16)
+    weights = jnp.concatenate([weights[:half], weights[half:]], axis=1)
+    even = lax.axis_index("mesh") % 2 == 0
+    for out, below in ((first, even), (second, jnp.logical_not(even))):
+        near = jnp.where(below, rows - 1, 0)
+        beyond = jnp.where(below, rows - 2, 1)
+        for i, r in enumerate((near, beyond)):
+            at = pl.multiple_of(r * count, count)
+            out[i * count : (i + 1) * count, :] = omega[pl.ds(at, count), :].astype(BF16)
+        out[2 * count : 2 * count + half, :] = weights
         small[...] = jnp.zeros_like(small)
         at = 0
-        for field, r in ((0, near), (0, next_near), (1, near), (1, next_near), (2, near)):
-            value = grid[field, r : r + 1, :]
+        for field, r in ((0, near), (0, beyond), (1, near), (1, beyond), (2, near)):
+            value = grid[field, pl.ds(r, 1), :]
             high = value.astype(BF16).astype(F32)
             small[at : at + 1, :] = high
             small[at + 1 : at + 2, :] = value - high
@@ -204,7 +210,7 @@
         high = value.astype(BF16).astype(F32)
         small[at + 1 : at + 2, :LANES] = high
         small[at + 2 : at + 3, :LANES] = value - high
-        out[2 * count + share :, :] = small[...].astype(BF16)
+        out[2 * count + half :, :] = small[...].astype(BF16)
 
 
 def forced_kernel(omega, grid, owned, forced, sent):
@@ -246,28 +252,35 @@
         out[i * count : (i + 1) * count, :] = x
 
 
-def received(ref, count, share):
-    small = ref[2 * count + share :, :].astype(F32)
+def arrival(first, second, below):
+    even = lax.axis_index("mesh") % 2 == 0
+    return jnp.where(even if below else jnp.logical_not(even), first[...], second[...])
+
+
+def received(x, count, share):
+    small = x[2 * count + share // 2 :].astype(F32)
     parts = [small[i : i + 1] + small[i + 1 : i + 2] for i in range(0, 10, 2)]
     return parts, small[10:11, :LANES], small[11:12, :LANES] + small[12:13, :LANES]
 
 
-def far_kernel(count, share, from_up, from_down, inner, near, sent):
+def far_kernel(count, share, first, second, inner, near, sent):
     blocks = []
-    edge = lax.axis_index("mesh"), lax.axis_size("mesh") - 1
-    width = from_up.shape[1]
-    first = row_of((PAD, width)) == 0
+    here, last = lax.axis_index("mesh"), lax.axis_size("mesh") - 1
+    width = first.shape[1]
+    top = row_of((PAD, width)) == 0
     at = count + PAD
-    for i, (ref, inside) in enumerate(((from_up, edge[0] > 0), (from_down, edge[0] < edge[1]))):
-        (velocity, _, viscosity, _, _), ids, precision = received(ref, count, share)
+    for i, inside in enumerate((here > 0, here < last)):
+        x = arrival(first, second, i == 1)
+        (velocity, _, viscosity, _, _), ids, precision = received(x, count, share)
         block = jnp.concatenate(
-            [velocity * ref[:count, :].astype(F32), jnp.where(first, viscosity, 0.0)], axis=0
+            [velocity * x[:count].astype(F32), jnp.where(top, viscosity, 0.0)], axis=0
         )
         block = jnp.where(inside, block, 0.0)
         near[i] = block
         blocks.append(block)
-        both = ref[2 * count : 2 * count + share, :].astype(F32)
-        sent[at : at + share, :] = both[:, :LANES] + both[:, LANES:]
+        weight = x[2 * count : 2 * count + share // 2].astype(F32)
+        sent[at : at + share // 2, :] = weight[:, :LANES]
+        sent[at + share // 2 : at + share, :] = weight[:, LANES:]
         row = row_of((PAD, LANES))
         sent[at + share : at + share + PAD, :] = jnp.where(
             row == 0, ids, jnp.where(row == 1, precision, 0.0)
@@ -294,16 +307,17 @@
     sent[...] = edge_columns([first, *middle, last])
 
 
-def halo_kernel(slab_columns, share, forced, near, from_up, from_down, from_left, from_right, *rest):
+def halo_kernel(slab_columns, share, forced, near, first, second, from_left, from_right, *rest):
     *observed, out = rest
     rows, height, width = forced.shape
     count = height - PAD
     here, last = lax.axis_index("mesh"), lax.axis_size("mesh") - 1
-    for i, ref in enumerate((from_up, from_down)):
-        (_, velocity, _, viscosity, friction), _, _ = received(ref, count, share)
+    for i in range(2):
+        x = arrival(first, second, i == 1)
+        (_, velocity, _, viscosity, friction), _, _ = received(x, count, share)
         far = jnp.concatenate(
             [
-                velocity * ref[count : 2 * count, :].astype(F32),
+                velocity * x[count : 2 * count].astype(F32),
                 jnp.broadcast_to(viscosity, (PAD, width)),
             ],
             axis=0,
@@ -464,6 +478,43 @@
     return lax.ppermute(x, axis, [(i, (i + step) % size) for i in range(size)])
 
 
+def exchanged(x, odd):
+    rows, columns = lax.axis_size("mesh"), lax.axis_size("obs")
+    pairs = []
+    for i in range(rows):
+        partner = i + 1 if i % 2 == odd else i - 1
+        for c in range(columns):
+            target = partner * columns + c if 0 <= partner < rows else i * columns + (c ^ 1)
+            pairs.append((i * columns + c, target))
+    return lax.ppermute(x, ("mesh", "obs"), pairs)
+
+
+def summed(x):
+    rows, columns = lax.axis_size("mesh"), lax.axis_size("obs")
+    x = x + ring(x, "obs", 1) if columns == 2 else lax.psum(x, "obs")
+    step = 1
+    while step < rows:
+        offsets = (step, 2 * step, 3 * step) if step == 1 else (step, 3 * step, 2 * step)
+        if rows % (4 * step):
+            offsets = (step,)
+        pieces = [
+            lax.ppermute(
+                x,
+                ("mesh", "obs"),
+                [
+                    (i * columns + c, (i ^ offset) * columns + (c ^ 1))
+                    for i in range(rows)
+                    for c in range(columns)
+                ],
+            )
+            for offset in offsets
+        ]
+        for piece in pieces:
+            x = x + piece
+        step = step * (len(offsets) + 1)
+    return x
+
+
 def both_sides(x):
     other = ring(x, "obs", 1)
     return other, (other if lax.axis_size("obs") == 2 else ring(x, "obs", -1))
@@ -485,8 +536,8 @@
     cells = rows * width * mesh_size * obs_size
     height = count + PAD
 
-    payload = (2 * count + share + 16, width)
-    omega, up, down, grid, owned = call(
+    payload = (2 * count + share // 2 + 16, width)
+    omega, first, second, grid, owned = call(
         edges_kernel,
         [
             ((rows * count, width), F32),
@@ -507,7 +558,7 @@
         space=pltpu.HBM,
         name="edges",
     )
-    from_up, from_down = ring(down, "mesh", 1), ring(up, "mesh", -1)
+    arrived = exchanged(first, 0), exchanged(second, 1)
 
     forced, sent = call(
         forced_kernel,
@@ -526,7 +577,7 @@
     near, far_sent = call(
         functools.partial(far_kernel, count, share),
         [((2, height, width), F32), ((height + 2 * (share + PAD), LANES), F32)],
-        (from_up, from_down, inner),
+        (*arrived, inner),
         name="far",
     )
     far_sides = both_sides(far_sent)
@@ -541,7 +592,7 @@
     (halo,) = call(
         functools.partial(halo_kernel, slab_columns, share),
         [((2 * count, width), F32)],
-        (forced, near, from_up, from_down, *far_sides, *far_observed),
+        (forced, near, *arrived, *far_sides, *far_observed),
         name="halo",
     )
     sketch, gram = call(
@@ -550,9 +601,7 @@
         (forced, near, omega, grid, *sides, *source_sides, inner, outer, halo),
         name="sketch",
     )
-    gram = gram + ring(gram, "obs", 1) if obs_size == 2 else lax.psum(gram, "obs")
-    pieces = jnp.broadcast_to(gram, (mesh_size, *gram.shape))
-    gram = jnp.sum(lax.all_to_all(pieces, "mesh", 0, 0, tiled=True), axis=0)
+    gram = summed(gram)
     basis, factor = pl.pallas_call(
         basis_kernel,
         out_shape=[

time: 35.4 us -> 31.4 us (0.89)
  waiting for transfers between devices: 10.6 us -> 7.77 us
  local copies, waits for them, and re-layouts: 0.74 us -> 0 us
    ppermute x0 -> x8, starting transfers between devices: none -> 13 us  [the longest x6 9.99 us: summed(): lax.ppermute(x, ('mesh', 'obs'), [(i * columns + c, (i ^ offset) * column...]
    all_to_all x1 -> x0, waiting for transfers between devices: 7.39 us -> none  [per_device(): gram = jnp.sum(lax.all_to_all(pieces, 'mesh', 0, 0, tiled=True), axis=0)]
    all_to_all x1 -> x0, starting transfers between devices: 6.67 us -> none  [per_device(): gram = jnp.sum(lax.all_to_all(pieces, 'mesh', 0, 0, tiled=True), axis=0)]
    ppermute x6 -> x4, starting transfers between devices: 8.17 us -> 1.54 us  [ring(): return lax.ppermute(x, axis, [(i, (i + step) % size) for i in range(size)])]
    ppermute x0 -> x8, waiting for transfers between devices: none -> 5.46 us  [the longest x6 5.33 us: summed(): lax.ppermute(x, ('mesh', 'obs'), [(i * columns + c, (i ^ offset) * column...]
    ppermute x6 -> x4, waiting for transfers between devices: 3.17 us -> 2.31 us  [ring(): return lax.ppermute(x, axis, [(i, (i + step) % size) for i in range(size)])]
    broadcast_in_dim x1 -> x0, local copies, waits for them, and re-layouts: 0.73 us -> none  [per_device(): pieces = jnp.broadcast_to(gram, (mesh_size, *gram.shape))]
  transfers between devices with their start and end apart: 7 -> 12, of which waited for: 6 -> 10; matrix products, arithmetic and copies ran while one was open for 0% -> 0% of each run, Pallas kernels for 6% -> 6%
where the time goes in v3:
time: 31.4 us; the launch traced here: 31.3 us
  starting transfers between devices  14.5 us (46%)
  waiting for transfers between devices  7.77 us (25%)
  Pallas kernels  7.56 us (24%)
  between operations  1.35 us (4%)
    ppermute x6, starting transfers between devices, summed(): lax.ppermute(x, ('mesh', 'obs'), [(i * columns + c, (i ^ offset) * column...  9.99 us
    ppermute x6, waiting for transfers between devices, summed(): lax.ppermute(x, ('mesh', 'obs'), [(i * columns + c, (i ^ offset) * column...  5.33 us
    pallas_call x7, Pallas kernels, call(): pl.pallas_call(body, out_shape=outs, in_specs=[pl.BlockSpec(memory_space=...  4.28 us
    pallas_call x1, Pallas kernels, per_device(): pl.pallas_call(basis_kernel, out_shape=[jax.ShapeDtypeStruct((count, rows...  3.27 us
    ppermute x2, starting transfers between devices, exchanged(): return lax.ppermute(x, ('mesh', 'obs'), pairs)  3.01 us
    ppermute x4, waiting for transfers between devices, ring(): return lax.ppermute(x, axis, [(i, (i + step) % size) for i in range(size)])  2.31 us
    ppermute x4, starting transfers between devices, ring(): return lax.ppermute(x, axis, [(i, (i + step) % size) for i in range(size)])  1.54 us
  transfers between devices with their start and end apart: 12, of which 10 were waited for; matrix products, arithmetic and copies ran while one was open for 0% of the time, Pallas kernels for 6%

profile of v3, /device:TPU:0, one launch (start us, length us, event | category | flops | bytes accessed | tf_op | source)
XLA Modules:
  0.0 31.3 jit_solution(9115311671702267899)
XLA Ops:
  0.6 1.2 %edges.1 = (f32[512,256]{1,0:T(8,128)S(1)}, bf16[176,256]{1,0:T(8,128)(2,1)S(1)}, bf16[176,256]{1,0:T(8,128)(2,1)S(1)}, f32[3,8,256]{2,1,0:T(8,128)S(1)}, f32[72,128]{1,0:T(8,128)S(1)}) custom-call(bf16[64,8,256]{2,1,0:T(8,128)(2,1)} %probes.1, f32[8,256]{1,0:T(8,128)} %velocity.1, f32[8,256]{1,0:T(8,128)} %viscosity.1, f32[8,256]{1,0:T(8,128)} %friction.1, ...), custom_call_target="tpu_custom_call" | custom-call | bytes 1048576 | tf_op jit(solution)/shard_map/edges/pallas_call | solution.py:40
  1.8 3.0 %collective-permute-start = (bf16[176,256]{1,0:T(8,128)(2,1)S(1)}, bf16[176,256]{1,0:T(8,128)(2,1)S(1)}, u32[]{:S(2)}, u32[]{:S(2)}) collective-permute-start(bf16[176,256]{1,0:T(8,128)(2,1)S(1)} %get-tuple-element.19), channel_id=1, source_target_pairs={{0,2},{1,3},{2,0},{3,1},{4,6},{5,7},{6,4},{7,5},{8,10},{9,11},{10,... | collective-permute-start | bytes 270344 | tf_op jit(solution)/shard_map/ppermute | solution.py:489
  4.8 0.0 collective-permute-start.1
  4.8 0.2 forced.1
  5.1 0.6 %collective-permute-start.2 = (f32[144,128]{1,0:T(8,128)S(1)}, f32[144,128]{1,0:T(8,128)S(1)}, u32[]{:S(2)}, u32[]{:S(2)}) collective-permute-start(f32[144,128]{1,0:T(8,128)S(1)} %get-tuple-element.21.rest_0_), channel_id=1, source_target_pairs={{0,1},{1,0},{2,3},{3,2},{4,5},{5,4},{6,7},{7,6},{8,9},{9,8},{10,11... | collective-permute-start | bytes 221192 | tf_op jit(solution)/shard_map/ppermute | solution.py:478
  5.7 0.9 %collective-permute-done.2.from_left.from_right.rest_1_.visc_left.visc_right = f32[144,128]{1,0:T(8,128)S(1)} collective-permute-done((f32[144,128]{1,0:T(8,128)S(1)}, f32[144,128]{1,0:T(8,128)S(1)}, u32[]{:S(2)}, u32[]{:S(2)}) %collective-permute-start.2) | collective-permute-done | bytes 73760 | tf_op jit(solution)/shard_map/ppermute | solution.py:478
  6.6 0.7 %inner.1 = f32[384,256]{1,0:T(8,128)S(1)} custom-call(f32[8,72,256]{2,1,0:T(8,128)S(1)} %get-tuple-element.18.forced, f32[3,8,256]{2,1,0:T(8,128)S(1)} %get-tuple-element.16.grid, f32[144,128]{1,0:T(8,128)S(1)} %collective-permute-done.2.from_left.from_right.rest_1_.visc_left.visc_right, ...), custom_call_target="tpu_custom_call" | custom-call | bytes 1048576 | tf_op jit(solution)/shard_map/inner/pallas_call | solution.py:40
  7.3 0.1 collective-permute-done.first
  7.5 0.0 collective-permute-done.1.second
  7.5 0.1 far.1
  7.6 0.3 %collective-permute-start.4 = (f32[216,128]{1,0:T(8,128)S(1)}, f32[216,128]{1,0:T(8,128)S(1)}, u32[]{:S(2)}, u32[]{:S(2)}) collective-permute-start(f32[216,128]{1,0:T(8,128)S(1)} %get-tuple-element.25.rest_0_), channel_id=1, source_target_pairs={{0,1},{1,0},{2,3},{3,2},{4,5},{5,4},{6,7},{7,6},{8,9},{9,8},{10,11... | collective-permute-start | bytes 331784 | tf_op jit(solution)/shard_map/ppermute | solution.py:478
  7.9 0.5 %outer.1 = (f32[128,256]{1,0:T(8,128)S(1)}, f32[64,128]{1,0:T(8,128)S(1)}) custom-call(f32[8,72,256]{2,1,0:T(8,128)S(1)} %get-tuple-element.18.forced, f32[2,72,256]{2,1,0:T(8,128)S(1)} %get-tuple-element.22.near, f32[3,8,256]{2,1,0:T(8,128)S(1)} %get-tuple-element.16.grid, ...), custom_call_target="tpu_custom_call" | custom-call | bytes 1048576 | tf_op jit(solution)/shard_map/outer/pallas_call | solution.py:40
  8.4 0.3 %collective-permute-start.3 = (f32[64,128]{1,0:T(8,128)S(1)}, f32[64,128]{1,0:T(8,128)S(1)}, u32[]{:S(2)}, u32[]{:S(2)}) collective-permute-start(f32[64,128]{1,0:T(8,128)S(1)} %get-tuple-element.23), channel_id=1, source_target_pairs={{0,1},{1,0},{2,3},{3,2},{4,5},{5,4},{6,7},{7,6},{8,9},{9,8},{10,11... | collective-permute-start | bytes 98312 | tf_op jit(solution)/shard_map/ppermute | solution.py:478
  8.7 0.2 collective-permute-done.4.from_left.from_right.rest_1_
  9.0 0.4 %halo.1 = f32[128,256]{1,0:T(8,128)S(1)} custom-call(f32[8,72,256]{2,1,0:T(8,128)S(1)} %get-tuple-element.18.forced, f32[2,72,256]{2,1,0:T(8,128)S(1)} %get-tuple-element.22.near, bf16[176,256]{1,0:T(8,128)(2,1)S(1)} %collective-permute-done.first, bf16[176,256]{1,0:T(8,128)(2,1)S(1)} %collective-permute-done.1.second, ...), custom_call_target="tpu_custom_call" | custom-call | bytes 1048576 | tf_op jit(solution)/shard_map/halo/pallas_call | solution.py:40
  9.4 0.3 collective-permute-done.3.from_left.from_right
  9.7 1.0 %sketch.1 = (f32[512,256]{1,0:T(8,128)S(1)}, f32[1,2176]{1,0:T(1,128)S(1)}) custom-call(f32[8,72,256]{2,1,0:T(8,128)S(1)} %get-tuple-element.18.forced, f32[2,72,256]{2,1,0:T(8,128)S(1)} %get-tuple-element.22.near, f32[512,256]{1,0:T(8,128)S(1)} %get-tuple-element.15.omega, f32[3,8,256]{2,1,0:T(8,128)S(1)} %get-tuple-element.16.grid, ...), custom_call_target="tpu_custom_call" | custom-call | bytes 1048576 | tf_op jit(solution)/shard_map/sketch/pallas_call | solution.py:40
  10.7 0.3 %collective-permute-start.5 = (f32[1,2176]{1,0:T(1,128)S(1)}, f32[1,2176]{1,0:T(1,128)S(1)}, u32[]{:S(2)}, u32[]{:S(2)}) collective-permute-start(f32[1,2176]{1,0:T(1,128)S(1)} %get-tuple-element.26), channel_id=1, source_target_pairs={{0,1},{1,0},{2,3},{3,2},{4,5},{5,4},{6,7},{7,6},{8,9},{9,8},{10,11... | collective-permute-start | bytes 26120 | tf_op jit(solution)/shard_map/ppermute | solution.py:478
  11.1 0.9 %collective-permute-done.5 = f32[1,2176]{1,0:T(1,128)S(1)} collective-permute-done((f32[1,2176]{1,0:T(1,128)S(1)}, f32[1,2176]{1,0:T(1,128)S(1)}, u32[]{:S(2)}, u32[]{:S(2)}) %collective-permute-start.5) | collective-permute-done | bytes 8736 | tf_op jit(solution)/shard_map/ppermute | solution.py:478
  12.0 4.6 %collective-permute-start.6 = (f32[1,2176]{1,0:T(1,128)S(1)}, f32[1,2176]{1,0:T(1,128)S(1)}, u32[]{:S(2)}, u32[]{:S(2)}) collective-permute-start(f32[1,2176]{1,0:T(1,128)S(1)} %add.21), channel_id=1, source_target_pairs={{0,3},{1,2},{2,1},{3,0},{4,7},{5,6},{6,5},{7,4},{8,11},{9,10},{10,... | collective-permute-start | bytes 26120 | tf_op jit(solution)/shard_map/ppermute | solution.py:501
  16.5 0.9 %collective-permute-start.7 = (f32[1,2176]{1,0:T(1,128)S(1)}, f32[1,2176]{1,0:T(1,128)S(1)}, u32[]{:S(2)}, u32[]{:S(2)}) collective-permute-start(f32[1,2176]{1,0:T(1,128)S(1)} %add.21), channel_id=1, source_target_pairs={{0,5},{1,4},{2,7},{3,6},{4,1},{5,0},{6,3},{7,2},{8,13},{9,12},{10,... | collective-permute-start | bytes 26120 | tf_op jit(solution)/shard_map/ppermute | solution.py:501
  17.4 0.4 %collective-permute-start.8 = (f32[1,2176]{1,0:T(1,128)S(1)}, f32[1,2176]{1,0:T(1,128)S(1)}, u32[]{:S(2)}, u32[]{:S(2)}) collective-permute-start(f32[1,2176]{1,0:T(1,128)S(1)} %add.21), channel_id=1, source_target_pairs={{0,7},{1,6},{2,5},{3,4},{4,3},{5,2},{6,1},{7,0},{8,15},{9,14},{10,... | collective-permute-start | bytes 26120 | tf_op jit(solution)/shard_map/ppermute | solution.py:501
  17.8 0.1 collective-permute-done.6
  17.9 1.7 %collective-permute-done.7 = f32[1,2176]{1,0:T(1,128)S(1)} collective-permute-done((f32[1,2176]{1,0:T(1,128)S(1)}, f32[1,2176]{1,0:T(1,128)S(1)}, u32[]{:S(2)}, u32[]{:S(2)}) %collective-permute-start.7) | collective-permute-done | bytes 8736 | tf_op jit(solution)/shard_map/ppermute | solution.py:501
  19.6 1.8 %collective-permute-done.8 = f32[1,2176]{1,0:T(1,128)S(1)} collective-permute-done((f32[1,2176]{1,0:T(1,128)S(1)}, f32[1,2176]{1,0:T(1,128)S(1)}, u32[]{:S(2)}, u32[]{:S(2)}) %collective-permute-start.8) | collective-permute-done | bytes 8736 | tf_op jit(solution)/shard_map/ppermute | solution.py:501
  21.4 2.5 %collective-permute-start.10 = (f32[1,2176]{1,0:T(1,128)S(1)}, f32[1,2176]{1,0:T(1,128)S(1)}, u32[]{:S(2)}, u32[]{:S(2)}) collective-permute-start(f32[1,2176]{1,0:T(1,128)S(1)} %add_add_fusion.1), channel_id=1, source_target_pairs={{0,25},{1,24},{2,27},{3,26},{4,29},{5,28},{6,31},{7,30},{8,17},{9,... | collective-permute-start | bytes 26120 | tf_op jit(solution)/shard_map/ppermute | solution.py:501
  24.0 0.3 collective-permute-start.11
  24.3 1.3 %collective-permute-start.9 = (f32[1,2176]{1,0:T(1,128)S(1)}, f32[1,2176]{1,0:T(1,128)S(1)}, u32[]{:S(2)}, u32[]{:S(2)}) collective-permute-start(f32[1,2176]{1,0:T(1,128)S(1)} %add_add_fusion.1), channel_id=1, source_target_pairs={{0,9},{1,8},{2,11},{3,10},{4,13},{5,12},{6,15},{7,14},{8,1},{9,0},... | collective-permute-start | bytes 26120 | tf_op jit(solution)/shard_map/ppermute | solution.py:501
  26.2 0.2 collective-permute-done.10
  26.4 1.6 %collective-permute-done.11 = f32[1,2176]{1,0:T(1,128)S(1)} collective-permute-done((f32[1,2176]{1,0:T(1,128)S(1)}, f32[1,2176]{1,0:T(1,128)S(1)}, u32[]{:S(2)}, u32[]{:S(2)}) %collective-permute-start.11) | collective-permute-done | bytes 8736 | tf_op jit(solution)/shard_map/ppermute | solution.py:501
  28.0 0.0 collective-permute-done.9
  28.0 3.3 %basis.1 = (f32[64,8,256]{2,1,0:T(8,128)}, f32[64,64]{1,0:T(8,128)}) custom-call(s32[1]{0:T(128)S(6)} %copy.10.rank, f32[1,2176]{1,0:T(1,128)S(1)} %add_add_fusion.gram, f32[512,256]{1,0:T(8,128)S(1)} %get-tuple-element.27.sketch), custom_call_target="tpu_custom_call" | custom-call | tf_op jit(solution)/shard_map/basis/pallas_call | solution.py:605
  (3 shorter events, 0.0 us)
Async XLA Ops:
  1.8 5.6 %collective-permute-start = (bf16[176,256]{1,0:T(8,128)(2,1)S(1)}, bf16[176,256]{1,0:T(8,128)(2,1)S(1)}, u32[]{:S(2)}, u32[]{:S(2)}) collective-permute-start(bf16[176,256]{1,0:T(8,128)(2,1)S(1)} %get-tuple-element.19), channel_id=1, source_target_pairs={{0,2},{1,3},{2,0},{3,1},{4,6},{5,7},{6,4},{7,5},{8,10},{9,11},{10,... | collective-permute-start | bytes 270344 | tf_op jit(solution)/shard_map/ppermute | solution.py:489
  4.8 2.6 %collective-permute-start.1 = (bf16[176,256]{1,0:T(8,128)(2,1)S(1)}, bf16[176,256]{1,0:T(8,128)(2,1)S(1)}, u32[]{:S(2)}, u32[]{:S(2)}) collective-permute-start(bf16[176,256]{1,0:T(8,128)(2,1)S(1)} %get-tuple-element.20), channel_id=1, source_target_pairs={{0,1},{1,0},{2,4},{3,5},{4,2},{5,3},{6,8},{7,9},{8,6},{9,7},{10,12... | collective-permute-start | bytes 270344 | tf_op jit(solution)/shard_map/ppermute | solution.py:489
  5.1 1.5 %collective-permute-start.2 = (f32[144,128]{1,0:T(8,128)S(1)}, f32[144,128]{1,0:T(8,128)S(1)}, u32[]{:S(2)}, u32[]{:S(2)}) collective-permute-start(f32[144,128]{1,0:T(8,128)S(1)} %get-tuple-element.21.rest_0_), channel_id=1, source_target_pairs={{0,1},{1,0},{2,3},{3,2},{4,5},{5,4},{6,7},{7,6},{8,9},{9,8},{10,11... | collective-permute-start | bytes 221192 | tf_op jit(solution)/shard_map/ppermute | solution.py:478
  7.6 1.4 %collective-permute-start.4 = (f32[216,128]{1,0:T(8,128)S(1)}, f32[216,128]{1,0:T(8,128)S(1)}, u32[]{:S(2)}, u32[]{:S(2)}) collective-permute-start(f32[216,128]{1,0:T(8,128)S(1)} %get-tuple-element.25.rest_0_), channel_id=1, source_target_pairs={{0,1},{1,0},{2,3},{3,2},{4,5},{5,4},{6,7},{7,6},{8,9},{9,8},{10,11... | collective-permute-start | bytes 331784 | tf_op jit(solution)/shard_map/ppermute | solution.py:478
  8.4 1.3 %collective-permute-start.3 = (f32[64,128]{1,0:T(8,128)S(1)}, f32[64,128]{1,0:T(8,128)S(1)}, u32[]{:S(2)}, u32[]{:S(2)}) collective-permute-start(f32[64,128]{1,0:T(8,128)S(1)} %get-tuple-element.23), channel_id=1, source_target_pairs={{0,1},{1,0},{2,3},{3,2},{4,5},{5,4},{6,7},{7,6},{8,9},{9,8},{10,11... | collective-permute-start | bytes 98312 | tf_op jit(solution)/shard_map/ppermute | solution.py:478
  10.7 1.2 %collective-permute-start.5 = (f32[1,2176]{1,0:T(1,128)S(1)}, f32[1,2176]{1,0:T(1,128)S(1)}, u32[]{:S(2)}, u32[]{:S(2)}) collective-permute-start(f32[1,2176]{1,0:T(1,128)S(1)} %get-tuple-element.26), channel_id=1, source_target_pairs={{0,1},{1,0},{2,3},{3,2},{4,5},{5,4},{6,7},{7,6},{8,9},{9,8},{10,11... | collective-permute-start | bytes 26120 | tf_op jit(solution)/shard_map/ppermute | solution.py:478
  12.0 5.9 %collective-permute-start.6 = (f32[1,2176]{1,0:T(1,128)S(1)}, f32[1,2176]{1,0:T(1,128)S(1)}, u32[]{:S(2)}, u32[]{:S(2)}) collective-permute-start(f32[1,2176]{1,0:T(1,128)S(1)} %add.21), channel_id=1, source_target_pairs={{0,3},{1,2},{2,1},{3,0},{4,7},{5,6},{6,5},{7,4},{8,11},{9,10},{10,... | collective-permute-start | bytes 26120 | tf_op jit(solution)/shard_map/ppermute | solution.py:501
  16.5 3.1 %collective-permute-start.7 = (f32[1,2176]{1,0:T(1,128)S(1)}, f32[1,2176]{1,0:T(1,128)S(1)}, u32[]{:S(2)}, u32[]{:S(2)}) collective-permute-start(f32[1,2176]{1,0:T(1,128)S(1)} %add.21), channel_id=1, source_target_pairs={{0,5},{1,4},{2,7},{3,6},{4,1},{5,0},{6,3},{7,2},{8,13},{9,12},{10,... | collective-permute-start | bytes 26120 | tf_op jit(solution)/shard_map/ppermute | solution.py:501
  17.4 4.0 %collective-permute-start.8 = (f32[1,2176]{1,0:T(1,128)S(1)}, f32[1,2176]{1,0:T(1,128)S(1)}, u32[]{:S(2)}, u32[]{:S(2)}) collective-permute-start(f32[1,2176]{1,0:T(1,128)S(1)} %add.21), channel_id=1, source_target_pairs={{0,7},{1,6},{2,5},{3,4},{4,3},{5,2},{6,1},{7,0},{8,15},{9,14},{10,... | collective-permute-start | bytes 26120 | tf_op jit(solution)/shard_map/ppermute | solution.py:501
  21.4 4.9 %collective-permute-start.10 = (f32[1,2176]{1,0:T(1,128)S(1)}, f32[1,2176]{1,0:T(1,128)S(1)}, u32[]{:S(2)}, u32[]{:S(2)}) collective-permute-start(f32[1,2176]{1,0:T(1,128)S(1)} %add_add_fusion.1), channel_id=1, source_target_pairs={{0,25},{1,24},{2,27},{3,26},{4,29},{5,28},{6,31},{7,30},{8,17},{9,... | collective-permute-start | bytes 26120 | tf_op jit(solution)/shard_map/ppermute | solution.py:501
  24.0 4.0 %collective-permute-start.11 = (f32[1,2176]{1,0:T(1,128)S(1)}, f32[1,2176]{1,0:T(1,128)S(1)}, u32[]{:S(2)}, u32[]{:S(2)}) collective-permute-start(f32[1,2176]{1,0:T(1,128)S(1)} %add_add_fusion.1), channel_id=1, source_target_pairs={{0,17},{1,16},{2,19},{3,18},{4,21},{5,20},{6,23},{7,22},{8,25},{9,... | collective-permute-start | bytes 26120 | tf_op jit(solution)/shard_map/ppermute | solution.py:501
  24.3 3.7 %collective-permute-start.9 = (f32[1,2176]{1,0:T(1,128)S(1)}, f32[1,2176]{1,0:T(1,128)S(1)}, u32[]{:S(2)}, u32[]{:S(2)}) collective-permute-start(f32[1,2176]{1,0:T(1,128)S(1)} %add_add_fusion.1), channel_id=1, source_target_pairs={{0,9},{1,8},{2,11},{3,10},{4,13},{5,12},{6,15},{7,14},{8,1},{9,0},... | collective-permute-start | bytes 26120 | tf_op jit(solution)/shard_map/ppermute | solution.py:501

commit v4 on v3

--- a/solution.py
+++ b/solution.py
@@ -151,14 +151,20 @@
 
 
 def read_share(ref, at, share):
-    weight = ref[at : at + share, :]
-    high, low = split(weight)
+    high, low = split(ref[at : at + share, :])
     return high, low, ref[at + share : at + share + 1, :], ref[at + share + 1 : at + share + 2, :]
+
+
+def probe_row(turned, r, rows):
+    parts, cells, _ = turned.shape
+    return jnp.concatenate(
+        [turned[c, pl.ds(r, cells // rows, stride=rows), :] for c in range(parts)], axis=1
+    )
 
 
 def edges_kernel(
     probes, velocity, viscosity, friction, weight, ids, precision,
-    omega, first, second, grid, owned, staged, staged_ids, staged_precision, turned, small, sems,
+    turned, first, second, grid, owned, staged, staged_ids, staged_precision, small, sems,
 ):
     count, rows, width = probes.shape
     share = weight.shape[1]
@@ -184,8 +190,6 @@
     for c in range(width // LANES):
         lanes = slice(c * LANES, (c + 1) * LANES)
         turned[c] = staged[:, :, lanes].astype(F32).reshape(count * rows, LANES)
-        for r in range(rows):
-            omega[r * count : (r + 1) * count, lanes] = turned[c, pl.ds(r, count, stride=rows), :]
     half = share // 2
     weights = owned[:share, :].astype(BF16)
     weights = jnp.concatenate([weights[:half], weights[half:]], axis=1)
@@ -194,8 +198,7 @@
         near = jnp.where(below, rows - 1, 0)
         beyond = jnp.where(below, rows - 2, 1)
         for i, r in enumerate((near, beyond)):
-            at = pl.multiple_of(r * count, count)
-            out[i * count : (i + 1) * count, :] = omega[pl.ds(at, count), :].astype(BF16)
+            out[i * count : (i + 1) * count, :] = probe_row(turned, r, rows).astype(BF16)
         out[2 * count : 2 * count + half, :] = weights
         small[...] = jnp.zeros_like(small)
         at = 0
@@ -215,13 +218,13 @@
 
 def forced_kernel(omega, grid, owned, forced, sent):
     _, rows, width = grid.shape
-    count = omega.shape[0] // rows
+    count = omega.shape[1] // rows
     blocks = []
     first = row_of((PAD, width)) == 0
     for r in range(rows):
         block = jnp.concatenate(
             [
-                grid[0, r : r + 1, :] * omega[r * count : (r + 1) * count, :],
+                grid[0, r : r + 1, :] * probe_row(omega, r, rows),
                 jnp.where(first, grid[1, r : r + 1, :], 0.0),
             ],
             axis=0,
@@ -263,7 +266,7 @@
     return parts, small[10:11, :LANES], small[11:12, :LANES] + small[12:13, :LANES]
 
 
-def far_kernel(count, share, first, second, inner, near, sent):
+def far_kernel(count, share, first, second, early, near, sent):
     blocks = []
     here, last = lax.axis_index("mesh"), lax.axis_size("mesh") - 1
     width = first.shape[1]
@@ -373,34 +376,40 @@
     return lower + square.T[:size] + spread
 
 
+def sketch_rows(rows, forced, omega, grid, sources, viscs, edges, visc_edges, parts):
+    total = None
+    for r in rows:
+        left, right = shifted(sources[r], *edges[r])
+        visc_side = shifted(viscs[r], *edges_from(*visc_edges, r))
+        gradient = grid[0, r : r + 1, :] * operate_row(
+            sources[r], sources[r - 1], sources[r + 1], left, right,
+            [viscs[r], viscs[r - 1], viscs[r + 1], *visc_side],
+            grid[2, r : r + 1, :],
+        )
+        value = jnp.concatenate(split(gradient + probe_row(omega, r, grid.shape[1])), axis=0)
+        parts(r)[...] = value
+        more = dot(value, value, 1)
+        total = more if total is None else total + more
+    return total
+
+
 def sketch_kernel(
-    cells, forced, near, omega, grid, visc_left, visc_right,
-    from_left, from_right, inner, outer, halo, sketch, gram,
+    cells, forced, near, omega, grid, visc_left, visc_right, from_left, from_right,
+    inner, outer, halo, parts, gram,
 ):
     rows, height, width = forced.shape
     count = height - PAD
-    values = [halo[:count, :], outer[:count, :]]
-    values += [inner[i * count : (i + 1) * count, :] for i in range(rows - 2)]
-    values += [outer[count:, :], halo[count:, :]]
-    viscs = [near[0, count : count + 1, :]]
-    viscs += [forced[r, count : count + 1, :] for r in range(rows)]
-    viscs += [near[1, count : count + 1, :]]
-    total = jnp.zeros((2 * count, 2 * count), F32)
-    for r in range(rows):
-        centre, visc = values[r + 1], viscs[r + 1]
-        left, right = shifted(centre, *edges_from(from_left, from_right, slice(0, count), r))
-        visc_side = shifted(
-            visc, *edges_from(visc_left, visc_right, slice(count, count + 1), r)
-        )
-        gradient = grid[0, r : r + 1, :] * operate_row(
-            centre, values[r], values[r + 2], left, right,
-            [visc, viscs[r], viscs[r + 2], *visc_side],
-            grid[2, r : r + 1, :],
-        )
-        value = gradient + omega[r * count : (r + 1) * count, :]
-        sketch[r * count : (r + 1) * count, :] = value
-        parts = jnp.concatenate(split(value), axis=0)
-        total = total + dot(parts, parts, 1)
+    sources = {r: inner[(r - 1) * count : r * count, :] for r in range(1, rows - 1)}
+    viscs = {r: forced[r, count : count + 1, :] for r in range(rows)}
+    for i, (r, beyond) in enumerate(((0, -1), (rows - 1, rows))):
+        sources[r] = outer[i * count : (i + 1) * count, :]
+        sources[beyond] = halo[i * count : (i + 1) * count, :]
+        viscs[beyond] = near[i, count : count + 1, :]
+    edges = {r: edges_from(from_left, from_right, slice(0, count), r) for r in range(rows)}
+    total = sketch_rows(
+        range(rows), forced, omega, grid, sources, viscs, edges,
+        (visc_left, visc_right, slice(count, count + 1)), parts.at.__getitem__,
+    )
     total = total + pltpu.roll(total, count, 1)
     total = (total[:count] + total[count:]) / cells
     body, diagonal = packed(total)
@@ -413,17 +422,23 @@
     size = matrix.shape[0]
     row = row_of((8, LANES))
     tiles = [matrix[t : t + 8] for t in range(0, size, 8)]
-    whole = functools.partial(jnp.broadcast_to, shape=(8, LANES))
-    for t in range(size // 8):
-        later = range(t + 1, size // 8)
-        columns = {
-            q: [whole(tiles[q][:, j : j + 1]) for j in range(8 * t, 8 * t + 8)]
-            for q in (t, *later)
-        }
-        square = [
-            [whole(columns[t][c][d : d + 1]) if d >= c else None for d in range(8)] for c in range(8)
-        ]
+    last = size // 8 - 1
+
+    def whole(x):
+        return jnp.broadcast_to(x, (8, LANES))
+
+    def columns_of(q, t):
+        return [whole(tiles[q][:, j : j + 1]) for j in range(8 * t, 8 * t + 8)]
+
+    def upper(block):
+        return [[whole(block[c][d : d + 1]) if d >= c else None for d in range(8)] for c in range(8)]
+
+    square = upper(columns_of(0, 0))
+    columns = {q: columns_of(q, 0) for q in range(1, last + 1)}
+    for t in range(last + 1):
+        later = range(t + 1, last + 1)
         rows = [whole(tiles[t][c : c + 1]) for c in range(8)]
+        block = columns_of(t + 1, t + 1) if t < last else None
         for c in range(8):
             root = lax.rsqrt(square[c][c])
             rows[c] = rows[c] * root
@@ -436,41 +451,54 @@
                 columns[q][c] = columns[q][c] * root
                 for d in range(c + 1, 8):
                     columns[q][d] = columns[q][d] - left[d] * columns[q][c]
-                tiles[q] = tiles[q] - columns[q][c] * rows[c]
         tiles[t] = rows[0]
         for c in range(1, 8):
             tiles[t] = jnp.where(row == c, rows[c], tiles[t])
+        if t < last:
+            for column in columns[t + 1]:
+                block = [block[e] - column * whole(column[e : e + 1]) for e in range(8)]
+            square = upper(block)
+            for q in later:
+                for c in range(8):
+                    tiles[q] = tiles[q] - columns[q][c] * rows[c]
+            columns = {q: columns_of(q, t + 1) for q in range(t + 2, last + 1)}
     return jnp.concatenate(tiles, axis=0)
 
 
-def basis_kernel(rank, gram, sketch, basis, factor, turned):
+def basis_kernel(rank, gram, parts, basis, factor, turned, lower, sems):
     count = factor.shape[0]
-    parts = gram.shape[1] // LANES - 1
-    row = row_of((parts, LANES))
-    body = jnp.zeros((parts, LANES), F32)
-    for i in range(parts):
+    lines = gram.shape[1] // LANES - 1
+    row = row_of((lines, LANES))
+    body = jnp.zeros((lines, LANES), F32)
+    for i in range(lines):
         body = jnp.where(row == i, gram[:, i * LANES : (i + 1) * LANES], body)
-    matrix = unpacked(body, gram[:, parts * LANES :])
+    matrix = unpacked(body, gram[:, lines * LANES :])
     row, lane = row_of(matrix.shape), lane_of(matrix.shape)
     matrix = jnp.where(lane == row + count, 1.0, matrix)
     done = factorize(matrix)
-    upper = jnp.where((lane < count) & (lane >= row), done, 0.0)
-    square = jnp.concatenate([upper, jnp.zeros((LANES - count, LANES), F32)], axis=0)
-    factor[...] = square.T[:count, :count]
     inverse = pltpu.roll(done, count, 1)
     inverse = jnp.where((lane <= row) & (row < rank[0]), inverse, 0.0)
     high = inverse.astype(BF16).astype(F32)
     high, low = (x + pltpu.roll(x, count, 1) for x in (high, inverse - high))
     left = jnp.concatenate([high, low], axis=1).astype(BF16)
-    rows = sketch.shape[0] // count
-    width = sketch.shape[1]
-    for r in range(rows):
-        parts = split(sketch[r * count : (r + 1) * count, :])
-        value = dot(left, jnp.concatenate([*parts, *parts], axis=0))
-        for c in range(width // LANES):
-            turned[c, pl.ds(r, count, stride=rows), :] = value[:, c * LANES : (c + 1) * LANES]
-    for c in range(width // LANES):
-        basis[:, :, c * LANES : (c + 1) * LANES] = turned[c].reshape(count, rows, LANES)
+    rows = parts.shape[0]
+    copies = [pltpu.make_async_copy(lower, factor, sems.at[turned.shape[0]])]
+    for c in range(turned.shape[0]):
+        lanes = slice(c * LANES, (c + 1) * LANES)
+        for r in range(rows):
+            part = parts[r, :, lanes]
+            value = dot(left, jnp.concatenate([part, part], axis=0))
+            turned[c, pl.ds(r, count, stride=rows), :] = value
+        copy = pltpu.make_async_copy(turned.at[c], basis.at[:, lanes], sems.at[c])
+        copy.start()
+        copies.append(copy)
+        if c == 0:
+            upper = jnp.where((lane < count) & (lane >= row), done, 0.0)
+            square = jnp.concatenate([upper, jnp.zeros((LANES - count, LANES), F32)], axis=0)
+            lower[...] = square.T[:count, :count]
+            copies[0].start()
+    for copy in copies:
+        copy.wait()
 
 
 def ring(x, axis, step):
@@ -525,7 +553,8 @@
     if size == 2:
         return [x, sides[0]]
     gathered = lax.all_gather(x, "obs")
-    return [gathered[i] for i in range(size)]
+    here = lax.axis_index("obs")
+    return [lax.dynamic_index_in_dim(gathered, (here + i) % size, 0, False) for i in range(size)]
 
 
 def per_device(probes, velocity, viscosity, friction, obs_block, obs_weight, obs_prec, rank):
@@ -537,10 +566,11 @@
     height = count + PAD
 
     payload = (2 * count + share // 2 + 16, width)
+    turned = (width // LANES, rows * count, LANES)
     omega, first, second, grid, owned = call(
         edges_kernel,
         [
-            ((rows * count, width), F32),
+            (turned, F32),
             (payload, BF16),
             (payload, BF16),
             ((3, rows, width), F32),
@@ -551,7 +581,6 @@
             pltpu.VMEM(probes.shape, probes.dtype),
             pltpu.VMEM(obs_block.shape, obs_block.dtype),
             pltpu.VMEM(obs_prec.shape, F32),
-            pltpu.VMEM((width // LANES, rows * count, LANES), F32),
             pltpu.VMEM((16, width), F32),
             pltpu.SemaphoreType.DMA((7,)),
         ],
@@ -595,9 +624,9 @@
         (forced, near, *arrived, *far_sides, *far_observed),
         name="halo",
     )
-    sketch, gram = call(
+    parts, gram = call(
         functools.partial(sketch_kernel, cells),
-        [((rows * count, width), F32), ((1, 17 * LANES), F32)],
+        [((rows, 2 * count, width), BF16), ((1, 17 * LANES), F32)],
         (forced, near, omega, grid, *sides, *source_sides, inner, outer, halo),
         name="sketch",
     )
@@ -605,19 +634,20 @@
     basis, factor = pl.pallas_call(
         basis_kernel,
         out_shape=[
-            jax.ShapeDtypeStruct((count, rows, width), F32),
+            jax.ShapeDtypeStruct((count * rows, width), F32),
             jax.ShapeDtypeStruct((count, count), F32),
         ],
-        in_specs=[
-            pl.BlockSpec(memory_space=pltpu.SMEM),
-            pl.BlockSpec(memory_space=pltpu.VMEM),
-            pl.BlockSpec(memory_space=pltpu.VMEM),
+        in_specs=[pl.BlockSpec(memory_space=pltpu.SMEM)] + [pl.BlockSpec(memory_space=pltpu.VMEM)] * 2,
+        out_specs=[pl.BlockSpec(memory_space=pl.ANY)] * 2,
+        scratch_shapes=[
+            pltpu.VMEM(turned, F32),
+            pltpu.VMEM((count, count), F32),
+            pltpu.SemaphoreType.DMA((width // LANES + 1,)),
         ],
-        scratch_shapes=[pltpu.VMEM((width // LANES, rows * count, LANES), F32)],
         compiler_params=pltpu.CompilerParams(vmem_limit_bytes=8 * 2**20),
         name="basis",
-    )(rank, gram, sketch)
-    return basis, factor
+    )(rank, gram, parts)
+    return basis.reshape(count, rows, width), factor
 
 
 def solution(mesh):

time: 31.4 us -> 30.6 us (0.975)
  Pallas kernels: 7.56 us -> 6.74 us
    pallas_call x1, Pallas kernels: 3.27 us -> 2.42 us  [per_device(): pl.pallas_call(basis_kernel, out_shape=[jax.ShapeDtypeStruct((count * row...]
where the time goes in v4:
time: 30.6 us; the launch traced here: 30.4 us
  starting transfers between devices  14.5 us (47%)
  waiting for transfers between devices  7.78 us (25%)
  Pallas kernels  6.74 us (22%)
  between operations  1.35 us (4%)
    ppermute x6, starting transfers between devices, summed(): lax.ppermute(x, ('mesh', 'obs'), [(i * columns + c, (i ^ offset) * column...  9.98 us
    ppermute x6, waiting for transfers between devices, summed(): lax.ppermute(x, ('mesh', 'obs'), [(i * columns + c, (i ^ offset) * column...  5.33 us
    pallas_call x7, Pallas kernels, call(): pl.pallas_call(body, out_shape=outs, in_specs=[pl.BlockSpec(memory_space=...  4.32 us
    ppermute x2, starting transfers between devices, exchanged(): return lax.ppermute(x, ('mesh', 'obs'), pairs)  3.01 us
    pallas_call x1, Pallas kernels, per_device(): pl.pallas_call(basis_kernel, out_shape=[jax.ShapeDtypeStruct((count * row...  2.42 us
    ppermute x4, waiting for transfers between devices, ring(): return lax.ppermute(x, axis, [(i, (i + step) % size) for i in range(size)])  2.33 us
    ppermute x4, starting transfers between devices, ring(): return lax.ppermute(x, axis, [(i, (i + step) % size) for i in range(size)])  1.53 us
  transfers between devices with their start and end apart: 12, of which 10 were waited for; matrix products, arithmetic and copies ran while one was open for 0% of the time, Pallas kernels for 6%

profile of v4, /device:TPU:0, one launch (start us, length us, event | category | flops | bytes accessed | tf_op | source)
XLA Modules:
  0.0 30.4 jit_solution(1383710650424446629)
XLA Ops:
  0.6 1.2 %edges.1 = (f32[2,512,128]{2,1,0:T(8,128)S(1)}, bf16[176,256]{1,0:T(8,128)(2,1)S(1)}, bf16[176,256]{1,0:T(8,128)(2,1)S(1)}, f32[3,8,256]{2,1,0:T(8,128)S(1)}, f32[72,128]{1,0:T(8,128)S(1)}) custom-call(bf16[64,8,256]{2,1,0:T(8,128)(2,1)} %probes.1, f32[8,256]{1,0:T(8,128)} %velocity.1, f32[8,256]{1,0:T(8,128)} %viscosity.1, f32[8,256]{1,0:T(8,128)} %friction.1, ...), custom_call_target="tpu_custom_call" | custom-call | bytes 1048576 | tf_op jit(solution)/shard_map/edges/pallas_call | solution.py:40
  1.8 3.0 %collective-permute-start = (bf16[176,256]{1,0:T(8,128)(2,1)S(1)}, bf16[176,256]{1,0:T(8,128)(2,1)S(1)}, u32[]{:S(2)}, u32[]{:S(2)}) collective-permute-start(bf16[176,256]{1,0:T(8,128)(2,1)S(1)} %get-tuple-element.21), channel_id=1, source_target_pairs={{0,2},{1,3},{2,0},{3,1},{4,6},{5,7},{6,4},{7,5},{8,10},{9,11},{10,... | collective-permute-start | bytes 270344 | tf_op jit(solution)/shard_map/ppermute | solution.py:517
  4.8 0.0 collective-permute-start.1
  4.8 0.3 forced.1
  5.1 0.6 %collective-permute-start.2 = (f32[144,128]{1,0:T(8,128)S(1)}, f32[144,128]{1,0:T(8,128)S(1)}, u32[]{:S(2)}, u32[]{:S(2)}) collective-permute-start(f32[144,128]{1,0:T(8,128)S(1)} %get-tuple-element.23.rest_0_), channel_id=1, source_target_pairs={{0,1},{1,0},{2,3},{3,2},{4,5},{5,4},{6,7},{7,6},{8,9},{9,8},{10,11... | collective-permute-start | bytes 221192 | tf_op jit(solution)/shard_map/ppermute | solution.py:506
  5.6 0.9 %collective-permute-done.2.from_left.from_right.rest_1_.visc_left.visc_right = f32[144,128]{1,0:T(8,128)S(1)} collective-permute-done((f32[144,128]{1,0:T(8,128)S(1)}, f32[144,128]{1,0:T(8,128)S(1)}, u32[]{:S(2)}, u32[]{:S(2)}) %collective-permute-start.2) | collective-permute-done | bytes 73760 | tf_op jit(solution)/shard_map/ppermute | solution.py:506
  6.5 0.7 %inner.1.early = f32[384,256]{1,0:T(8,128)S(1)} custom-call(f32[8,72,256]{2,1,0:T(8,128)S(1)} %get-tuple-element.20.forced, f32[3,8,256]{2,1,0:T(8,128)S(1)} %get-tuple-element.18.grid, f32[144,128]{1,0:T(8,128)S(1)} %collective-permute-done.2.from_left.from_right.rest_1_.visc_left.visc_right, ...), custom_call_target="tpu_custom_call" | custom-call | bytes 1048576 | tf_op jit(solution)/shard_map/inner/pallas_call | solution.py:40
  7.3 0.1 collective-permute-done.first
  7.4 0.0 collective-permute-done.1.second
  7.4 0.1 far.1
  7.5 0.3 %collective-permute-start.4 = (f32[216,128]{1,0:T(8,128)S(1)}, f32[216,128]{1,0:T(8,128)S(1)}, u32[]{:S(2)}, u32[]{:S(2)}) collective-permute-start(f32[216,128]{1,0:T(8,128)S(1)} %get-tuple-element.27.rest_0_), channel_id=1, source_target_pairs={{0,1},{1,0},{2,3},{3,2},{4,5},{5,4},{6,7},{7,6},{8,9},{9,8},{10,11... | collective-permute-start | bytes 331784 | tf_op jit(solution)/shard_map/ppermute | solution.py:506
  7.9 0.5 %outer.1 = (f32[128,256]{1,0:T(8,128)S(1)}, f32[64,128]{1,0:T(8,128)S(1)}) custom-call(f32[8,72,256]{2,1,0:T(8,128)S(1)} %get-tuple-element.20.forced, f32[2,72,256]{2,1,0:T(8,128)S(1)} %get-tuple-element.24.near, f32[3,8,256]{2,1,0:T(8,128)S(1)} %get-tuple-element.18.grid, ...), custom_call_target="tpu_custom_call" | custom-call | bytes 1048576 | tf_op jit(solution)/shard_map/outer/pallas_call | solution.py:40
  8.4 0.3 %collective-permute-start.3 = (f32[64,128]{1,0:T(8,128)S(1)}, f32[64,128]{1,0:T(8,128)S(1)}, u32[]{:S(2)}, u32[]{:S(2)}) collective-permute-start(f32[64,128]{1,0:T(8,128)S(1)} %get-tuple-element.25), channel_id=1, source_target_pairs={{0,1},{1,0},{2,3},{3,2},{4,5},{5,4},{6,7},{7,6},{8,9},{9,8},{10,11... | collective-permute-start | bytes 98312 | tf_op jit(solution)/shard_map/ppermute | solution.py:506
  8.7 0.2 collective-permute-done.4.from_left.from_right.rest_1_
  8.9 0.4 %halo.1 = f32[128,256]{1,0:T(8,128)S(1)} custom-call(f32[8,72,256]{2,1,0:T(8,128)S(1)} %get-tuple-element.20.forced, f32[2,72,256]{2,1,0:T(8,128)S(1)} %get-tuple-element.24.near, bf16[176,256]{1,0:T(8,128)(2,1)S(1)} %collective-permute-done.first, bf16[176,256]{1,0:T(8,128)(2,1)S(1)} %collective-permute-done.1.second, ...), custom_call_target="tpu_custom_call" | custom-call | bytes 1048576 | tf_op jit(solution)/shard_map/halo/pallas_call | solution.py:40
  9.4 0.3 collective-permute-done.3.from_left.from_right
  9.7 1.1 %sketch.1 = (bf16[8,128,256]{2,1,0:T(8,128)(2,1)S(1)}, f32[1,2176]{1,0:T(1,128)S(1)}) custom-call(f32[8,72,256]{2,1,0:T(8,128)S(1)} %get-tuple-element.20.forced, f32[2,72,256]{2,1,0:T(8,128)S(1)} %get-tuple-element.24.near, f32[2,512,128]{2,1,0:T(8,128)S(1)} %get-tuple-element.17.omega, f32[3,8,256]{2,1,0:T(8,128)S(1)} %get-tuple-element.18.grid, ...), custom_call_target="tpu_custom_call" | custom-call | bytes 1048576 | tf_op jit(solution)/shard_map/sketch/pallas_call | solution.py:40
  10.8 0.3 %collective-permute-start.5 = (f32[1,2176]{1,0:T(1,128)S(1)}, f32[1,2176]{1,0:T(1,128)S(1)}, u32[]{:S(2)}, u32[]{:S(2)}) collective-permute-start(f32[1,2176]{1,0:T(1,128)S(1)} %get-tuple-element.28), channel_id=1, source_target_pairs={{0,1},{1,0},{2,3},{3,2},{4,5},{5,4},{6,7},{7,6},{8,9},{9,8},{10,11... | collective-permute-start | bytes 26120 | tf_op jit(solution)/shard_map/ppermute | solution.py:506
  11.1 0.9 %collective-permute-done.5 = f32[1,2176]{1,0:T(1,128)S(1)} collective-permute-done((f32[1,2176]{1,0:T(1,128)S(1)}, f32[1,2176]{1,0:T(1,128)S(1)}, u32[]{:S(2)}, u32[]{:S(2)}) %collective-permute-start.5) | collective-permute-done | bytes 8736 | tf_op jit(solution)/shard_map/ppermute | solution.py:506
  12.0 4.5 %collective-permute-start.6 = (f32[1,2176]{1,0:T(1,128)S(1)}, f32[1,2176]{1,0:T(1,128)S(1)}, u32[]{:S(2)}, u32[]{:S(2)}) collective-permute-start(f32[1,2176]{1,0:T(1,128)S(1)} %add.21), channel_id=1, source_target_pairs={{0,3},{1,2},{2,1},{3,0},{4,7},{5,6},{6,5},{7,4},{8,11},{9,10},{10,... | collective-permute-start | bytes 26120 | tf_op jit(solution)/shard_map/ppermute | solution.py:529
  16.6 0.9 %collective-permute-start.7 = (f32[1,2176]{1,0:T(1,128)S(1)}, f32[1,2176]{1,0:T(1,128)S(1)}, u32[]{:S(2)}, u32[]{:S(2)}) collective-permute-start(f32[1,2176]{1,0:T(1,128)S(1)} %add.21), channel_id=1, source_target_pairs={{0,5},{1,4},{2,7},{3,6},{4,1},{5,0},{6,3},{7,2},{8,13},{9,12},{10,... | collective-permute-start | bytes 26120 | tf_op jit(solution)/shard_map/ppermute | solution.py:529
  17.5 0.4 %collective-permute-start.8 = (f32[1,2176]{1,0:T(1,128)S(1)}, f32[1,2176]{1,0:T(1,128)S(1)}, u32[]{:S(2)}, u32[]{:S(2)}) collective-permute-start(f32[1,2176]{1,0:T(1,128)S(1)} %add.21), channel_id=1, source_target_pairs={{0,7},{1,6},{2,5},{3,4},{4,3},{5,2},{6,1},{7,0},{8,15},{9,14},{10,... | collective-permute-start | bytes 26120 | tf_op jit(solution)/shard_map/ppermute | solution.py:529
  17.9 0.1 collective-permute-done.6
  17.9 1.7 %collective-permute-done.7 = f32[1,2176]{1,0:T(1,128)S(1)} collective-permute-done((f32[1,2176]{1,0:T(1,128)S(1)}, f32[1,2176]{1,0:T(1,128)S(1)}, u32[]{:S(2)}, u32[]{:S(2)}) %collective-permute-start.7) | collective-permute-done | bytes 8736 | tf_op jit(solution)/shard_map/ppermute | solution.py:529
  19.6 1.8 %collective-permute-done.8 = f32[1,2176]{1,0:T(1,128)S(1)} collective-permute-done((f32[1,2176]{1,0:T(1,128)S(1)}, f32[1,2176]{1,0:T(1,128)S(1)}, u32[]{:S(2)}, u32[]{:S(2)}) %collective-permute-start.8) | collective-permute-done | bytes 8736 | tf_op jit(solution)/shard_map/ppermute | solution.py:529
  21.5 2.5 %collective-permute-start.10 = (f32[1,2176]{1,0:T(1,128)S(1)}, f32[1,2176]{1,0:T(1,128)S(1)}, u32[]{:S(2)}, u32[]{:S(2)}) collective-permute-start(f32[1,2176]{1,0:T(1,128)S(1)} %add_add_fusion.1), channel_id=1, source_target_pairs={{0,25},{1,24},{2,27},{3,26},{4,29},{5,28},{6,31},{7,30},{8,17},{9,... | collective-permute-start | bytes 26120 | tf_op jit(solution)/shard_map/ppermute | solution.py:529
  24.0 0.3 collective-permute-start.11
  24.3 1.3 %collective-permute-start.9 = (f32[1,2176]{1,0:T(1,128)S(1)}, f32[1,2176]{1,0:T(1,128)S(1)}, u32[]{:S(2)}, u32[]{:S(2)}) collective-permute-start(f32[1,2176]{1,0:T(1,128)S(1)} %add_add_fusion.1), channel_id=1, source_target_pairs={{0,9},{1,8},{2,11},{3,10},{4,13},{5,12},{6,15},{7,14},{8,1},{9,0},... | collective-permute-start | bytes 26120 | tf_op jit(solution)/shard_map/ppermute | solution.py:529
  26.2 0.2 collective-permute-done.10
  26.4 1.6 %collective-permute-done.11 = f32[1,2176]{1,0:T(1,128)S(1)} collective-permute-done((f32[1,2176]{1,0:T(1,128)S(1)}, f32[1,2176]{1,0:T(1,128)S(1)}, u32[]{:S(2)}, u32[]{:S(2)}) %collective-permute-start.11) | collective-permute-done | bytes 8736 | tf_op jit(solution)/shard_map/ppermute | solution.py:529
  28.0 0.0 collective-permute-done.9
  28.0 2.4 %basis.1 = (f32[512,256]{1,0:T(8,128)}, f32[64,64]{1,0:T(8,128)}) custom-call(s32[1]{0:T(128)S(6)} %copy.10.rank, f32[1,2176]{1,0:T(1,128)S(1)} %add_add_fusion.gram, bf16[8,128,256]{2,1,0:T(8,128)(2,1)S(1)} %get-tuple-element.29.parts), custom_call_target="tpu_custom_call" | custom-call | tf_op jit(solution)/shard_map/basis/pallas_call | solution.py:634
  (3 shorter events, 0.0 us)
Async XLA Ops:
  1.8 5.6 %collective-permute-start = (bf16[176,256]{1,0:T(8,128)(2,1)S(1)}, bf16[176,256]{1,0:T(8,128)(2,1)S(1)}, u32[]{:S(2)}, u32[]{:S(2)}) collective-permute-start(bf16[176,256]{1,0:T(8,128)(2,1)S(1)} %get-tuple-element.21), channel_id=1, source_target_pairs={{0,2},{1,3},{2,0},{3,1},{4,6},{5,7},{6,4},{7,5},{8,10},{9,11},{10,... | collective-permute-start | bytes 270344 | tf_op jit(solution)/shard_map/ppermute | solution.py:517
  4.8 2.6 %collective-permute-start.1 = (bf16[176,256]{1,0:T(8,128)(2,1)S(1)}, bf16[176,256]{1,0:T(8,128)(2,1)S(1)}, u32[]{:S(2)}, u32[]{:S(2)}) collective-permute-start(bf16[176,256]{1,0:T(8,128)(2,1)S(1)} %get-tuple-element.22), channel_id=1, source_target_pairs={{0,1},{1,0},{2,4},{3,5},{4,2},{5,3},{6,8},{7,9},{8,6},{9,7},{10,12... | collective-permute-start | bytes 270344 | tf_op jit(solution)/shard_map/ppermute | solution.py:517
  5.1 1.5 %collective-permute-start.2 = (f32[144,128]{1,0:T(8,128)S(1)}, f32[144,128]{1,0:T(8,128)S(1)}, u32[]{:S(2)}, u32[]{:S(2)}) collective-permute-start(f32[144,128]{1,0:T(8,128)S(1)} %get-tuple-element.23.rest_0_), channel_id=1, source_target_pairs={{0,1},{1,0},{2,3},{3,2},{4,5},{5,4},{6,7},{7,6},{8,9},{9,8},{10,11... | collective-permute-start | bytes 221192 | tf_op jit(solution)/shard_map/ppermute | solution.py:506
  7.5 1.4 %collective-permute-start.4 = (f32[216,128]{1,0:T(8,128)S(1)}, f32[216,128]{1,0:T(8,128)S(1)}, u32[]{:S(2)}, u32[]{:S(2)}) collective-permute-start(f32[216,128]{1,0:T(8,128)S(1)} %get-tuple-element.27.rest_0_), channel_id=1, source_target_pairs={{0,1},{1,0},{2,3},{3,2},{4,5},{5,4},{6,7},{7,6},{8,9},{9,8},{10,11... | collective-permute-start | bytes 331784 | tf_op jit(solution)/shard_map/ppermute | solution.py:506
  8.4 1.3 %collective-permute-start.3 = (f32[64,128]{1,0:T(8,128)S(1)}, f32[64,128]{1,0:T(8,128)S(1)}, u32[]{:S(2)}, u32[]{:S(2)}) collective-permute-start(f32[64,128]{1,0:T(8,128)S(1)} %get-tuple-element.25), channel_id=1, source_target_pairs={{0,1},{1,0},{2,3},{3,2},{4,5},{5,4},{6,7},{7,6},{8,9},{9,8},{10,11... | collective-permute-start | bytes 98312 | tf_op jit(solution)/shard_map/ppermute | solution.py:506
  10.8 1.2 %collective-permute-start.5 = (f32[1,2176]{1,0:T(1,128)S(1)}, f32[1,2176]{1,0:T(1,128)S(1)}, u32[]{:S(2)}, u32[]{:S(2)}) collective-permute-start(f32[1,2176]{1,0:T(1,128)S(1)} %get-tuple-element.28), channel_id=1, source_target_pairs={{0,1},{1,0},{2,3},{3,2},{4,5},{5,4},{6,7},{7,6},{8,9},{9,8},{10,11... | collective-permute-start | bytes 26120 | tf_op jit(solution)/shard_map/ppermute | solution.py:506
  12.0 5.9 %collective-permute-start.6 = (f32[1,2176]{1,0:T(1,128)S(1)}, f32[1,2176]{1,0:T(1,128)S(1)}, u32[]{:S(2)}, u32[]{:S(2)}) collective-permute-start(f32[1,2176]{1,0:T(1,128)S(1)} %add.21), channel_id=1, source_target_pairs={{0,3},{1,2},{2,1},{3,0},{4,7},{5,6},{6,5},{7,4},{8,11},{9,10},{10,... | collective-permute-start | bytes 26120 | tf_op jit(solution)/shard_map/ppermute | solution.py:529
  16.6 3.1 %collective-permute-start.7 = (f32[1,2176]{1,0:T(1,128)S(1)}, f32[1,2176]{1,0:T(1,128)S(1)}, u32[]{:S(2)}, u32[]{:S(2)}) collective-permute-start(f32[1,2176]{1,0:T(1,128)S(1)} %add.21), channel_id=1, source_target_pairs={{0,5},{1,4},{2,7},{3,6},{4,1},{5,0},{6,3},{7,2},{8,13},{9,12},{10,... | collective-permute-start | bytes 26120 | tf_op jit(solution)/shard_map/ppermute | solution.py:529
  17.5 4.0 %collective-permute-start.8 = (f32[1,2176]{1,0:T(1,128)S(1)}, f32[1,2176]{1,0:T(1,128)S(1)}, u32[]{:S(2)}, u32[]{:S(2)}) collective-permute-start(f32[1,2176]{1,0:T(1,128)S(1)} %add.21), channel_id=1, source_target_pairs={{0,7},{1,6},{2,5},{3,4},{4,3},{5,2},{6,1},{7,0},{8,15},{9,14},{10,... | collective-permute-start | bytes 26120 | tf_op jit(solution)/shard_map/ppermute | solution.py:529
  21.5 4.9 %collective-permute-start.10 = (f32[1,2176]{1,0:T(1,128)S(1)}, f32[1,2176]{1,0:T(1,128)S(1)}, u32[]{:S(2)}, u32[]{:S(2)}) collective-permute-start(f32[1,2176]{1,0:T(1,128)S(1)} %add_add_fusion.1), channel_id=1, source_target_pairs={{0,25},{1,24},{2,27},{3,26},{4,29},{5,28},{6,31},{7,30},{8,17},{9,... | collective-permute-start | bytes 26120 | tf_op jit(solution)/shard_map/ppermute | solution.py:529
  24.0 4.0 %collective-permute-start.11 = (f32[1,2176]{1,0:T(1,128)S(1)}, f32[1,2176]{1,0:T(1,128)S(1)}, u32[]{:S(2)}, u32[]{:S(2)}) collective-permute-start(f32[1,2176]{1,0:T(1,128)S(1)} %add_add_fusion.1), channel_id=1, source_target_pairs={{0,17},{1,16},{2,19},{3,18},{4,21},{5,20},{6,23},{7,22},{8,25},{9,... | collective-permute-start | bytes 26120 | tf_op jit(solution)/shard_map/ppermute | solution.py:529
  24.3 3.7 %collective-permute-start.9 = (f32[1,2176]{1,0:T(1,128)S(1)}, f32[1,2176]{1,0:T(1,128)S(1)}, u32[]{:S(2)}, u32[]{:S(2)}) collective-permute-start(f32[1,2176]{1,0:T(1,128)S(1)} %add_add_fusion.1), channel_id=1, source_target_pairs={{0,9},{1,8},{2,11},{3,10},{4,13},{5,12},{6,15},{7,14},{8,1},{9,0},... | collective-permute-start | bytes 26120 | tf_op jit(solution)/shard_map/ppermute | solution.py:529

commit v5 on v4

--- a/solution.py
+++ b/solution.py
@@ -51,11 +51,15 @@
 
 
 def shifted(x, left_edge, right_edge):
-    lane = lane_of(x.shape)
     width = x.shape[1]
-    left = jnp.where(lane == 0, left_edge, pltpu.roll(x, 1, 1))
-    right = jnp.where(lane == width - 1, right_edge, pltpu.roll(x, width - 1, 1))
-    return left, right
+    lane = lane_of((x.shape[0], LANES))
+    left, right = pltpu.roll(x, 1, 1), pltpu.roll(x, width - 1, 1)
+    first = jnp.where(lane == 0, left_edge, left[:, :LANES])
+    last = jnp.where(lane == LANES - 1, right_edge, right[:, width - LANES :])
+    return (
+        jnp.concatenate([first, left[:, LANES:]], axis=1),
+        jnp.concatenate([right[:, : width - LANES], last], axis=1),
+    )
 
 
 def operate_row(centre, above, below, left, right, visc, friction):
@@ -67,18 +71,34 @@
     return result
 
 
-def tangent_row(count, centre, above, below, left_edge, right_edge, friction):
+def forced_row(count, centre, above, below, left_edge, right_edge, friction):
     left, right = shifted(centre, left_edge, right_edge)
     visc = [x[count : count + 1] for x in (centre, above, below, left, right)]
     values = [x[:count] for x in (centre, above, below, left, right)]
-    return operate_row(*values, visc, friction).astype(BF16)
-
-
-def edge_columns(rows):
-    height, width = rows[0].shape
-    lane = lane_of((height, LANES))
-    out = jnp.zeros((height, LANES), F32)
-    for at, x in enumerate(rows):
+    return operate_row(*values, visc, friction)
+
+
+def tangent_row(*args):
+    return forced_row(*args).astype(BF16)
+
+
+def with_edges(count, result, centre, left_edge, right_edge):
+    width = centre.shape[1]
+    lane = lane_of((count, LANES))
+    tiles = [result[:, at : at + LANES] for at in range(0, width, LANES)]
+    for at, edge, place in ((0, left_edge, 0), (-1, right_edge, LANES - 1)):
+        x = centre[:, :LANES] if at == 0 else centre[:, width - LANES :]
+        visc = edge[count : count + 1]
+        face = 0.5 * (x[count : count + 1] + visc)
+        tiles[at] = tiles[at] + jnp.where(lane == place, (0.5 * visc) * x[:count] - face * edge[:count], 0.0)
+    return jnp.concatenate(tiles, axis=1)
+
+
+def edge_columns(rows, out=None):
+    for at, x in rows.items():
+        height, width = x.shape
+        lane = lane_of((height, LANES))
+        out = jnp.zeros((height, LANES), F32) if out is None else out
         out = jnp.where(lane == at, x[:, :1], out)
         out = jnp.where(lane == RIGHT + at, x[:, width - 1 :], out)
     return out
@@ -105,12 +125,12 @@
         if len(pair) == 1:
             pair = pair + [tuple(jnp.zeros_like(x) for x in pair[0])]
         high = jnp.concatenate([x[0] for x in pair], axis=0)
-        low = jnp.concatenate([x[1] for x in pair], axis=0)
         share = pair[0][0].shape[0]
         lane = lane_of((1, LANES))
         ids = jnp.where(lane < share, pair[0][2], pltpu.roll(pair[1][2], share, 1))
         ids = ids.astype(jnp.int32)
         precision = jnp.where(lane < share, pair[0][3], pltpu.roll(pair[1][3], share, 1))
+        low = jnp.concatenate([x[1] for x in pair], axis=0)
         misfit = dot(doubled, jnp.concatenate([high, low], axis=1), 1)
         kept = []
         for i, row in enumerate(grid_rows):
@@ -119,8 +139,9 @@
                 scale = jnp.where(ids == row * slab_columns + first + c, precision, 0.0)
                 kept.append(misfit[k * count : (k + 1) * count] * scale)
         misfit_high, misfit_low = split(jnp.concatenate(kept, axis=0))
+        halves = jnp.concatenate([misfit_high, misfit_low], axis=1)
         both = dot(
-            jnp.concatenate([misfit_high, misfit_low], axis=1),
+            halves,
             jnp.concatenate(
                 [
                     jnp.concatenate([high, low], axis=1),
@@ -184,21 +205,18 @@
     ]
     for copy in copies:
         copy.start()
-    for copy in copies:
+    for copy in copies[1:]:
         copy.wait()
     owned[share:, :] = share_rows(staged_ids[...].astype(F32), staged_precision[...])
-    for c in range(width // LANES):
-        lanes = slice(c * LANES, (c + 1) * LANES)
-        turned[c] = staged[:, :, lanes].astype(F32).reshape(count * rows, LANES)
     half = share // 2
     weights = owned[:share, :].astype(BF16)
     weights = jnp.concatenate([weights[:half], weights[half:]], axis=1)
     even = lax.axis_index("mesh") % 2 == 0
+    sides = []
     for out, below in ((first, even), (second, jnp.logical_not(even))):
         near = jnp.where(below, rows - 1, 0)
         beyond = jnp.where(below, rows - 2, 1)
-        for i, r in enumerate((near, beyond)):
-            out[i * count : (i + 1) * count, :] = probe_row(turned, r, rows).astype(BF16)
+        sides.append((out, near, beyond))
         out[2 * count : 2 * count + half, :] = weights
         small[...] = jnp.zeros_like(small)
         at = 0
@@ -214,6 +232,13 @@
         small[at + 1 : at + 2, :LANES] = high
         small[at + 2 : at + 3, :LANES] = value - high
         out[2 * count + half :, :] = small[...].astype(BF16)
+    copies[0].wait()
+    for c in range(width // LANES):
+        lanes = slice(c * LANES, (c + 1) * LANES)
+        turned[c] = staged[:, :, lanes].astype(F32).reshape(count * rows, LANES)
+    for out, *picked in sides:
+        for i, r in enumerate(picked):
+            out[i * count : (i + 1) * count, :] = probe_row(turned, r, rows).astype(BF16)
 
 
 def forced_kernel(omega, grid, owned, forced, sent):
@@ -231,7 +256,7 @@
         )
         forced[r] = block
         blocks.append(block)
-    sent[: count + PAD, :] = edge_columns(blocks)
+    sent[: count + PAD, :] = edge_columns(dict(enumerate(blocks)))
     sent[count + PAD :, :] = owned[...]
 
 
@@ -240,7 +265,7 @@
 
 
 def inner_kernel(slab_columns, share, forced, grid, from_left, from_right, *rest):
-    *observed, out = rest
+    *observed, out, edge_sources = rest
     rows, height, width = forced.shape
     count = height - PAD
     tangents = []
@@ -253,6 +278,7 @@
     result = sources(tangents, inner, shares_of(observed, height, share), slab_columns)
     for i, x in enumerate(result):
         out[i * count : (i + 1) * count, :] = x
+    edge_sources[...] = edge_columns(dict(zip(inner, result)))
 
 
 def arrival(first, second, below):
@@ -289,11 +315,13 @@
             row == 0, ids, jnp.where(row == 1, precision, 0.0)
         )
         at += share + PAD
-    sent[: count + PAD, :] = edge_columns(blocks)
-
-
-def outer_kernel(slab_columns, share, forced, near, grid, from_left, from_right, inner, *rest):
-    *observed, out, sent = rest
+    sent[: count + PAD, :] = edge_columns(dict(enumerate(blocks)))
+
+
+def outer_kernel(
+    slab_columns, share, forced, near, grid, from_left, from_right, inner_edges, first_in, second_in, *rest
+):
+    *observed, out, sent, beside = rest
     rows, height, width = forced.shape
     count = height - PAD
     tangents = []
@@ -306,17 +334,9 @@
     first, last = sources(tangents, outer, shares_of(observed, height, share), slab_columns)
     out[:count, :] = first
     out[count:, :] = last
-    middle = [inner[i * count : (i + 1) * count, :] for i in range(rows - 2)]
-    sent[...] = edge_columns([first, *middle, last])
-
-
-def halo_kernel(slab_columns, share, forced, near, first, second, from_left, from_right, *rest):
-    *observed, out = rest
-    rows, height, width = forced.shape
-    count = height - PAD
-    here, last = lax.axis_index("mesh"), lax.axis_size("mesh") - 1
+    sent[...] = edge_columns({0: first, rows - 1: last}, inner_edges[...])
     for i in range(2):
-        x = arrival(first, second, i == 1)
+        x = arrival(first_in, second_in, i == 1)
         (_, velocity, _, viscosity, friction), _, _ = received(x, count, share)
         far = jnp.concatenate(
             [
@@ -327,11 +347,20 @@
         )
         own = forced[rows - 1 if i else 0]
         above, below = (own, far) if i else (far, own)
+        beside[i * count : (i + 1) * count, :] = forced_row(count, near[i], above, below, 0.0, 0.0, friction)
+
+
+def halo_kernel(slab_columns, share, rows, near, beside, from_left, from_right, *rest):
+    *observed, out = rest
+    _, height, width = near.shape
+    count = height - PAD
+    here, last = lax.axis_index("mesh"), lax.axis_size("mesh") - 1
+    for i in range(2):
         edges = edges_from(from_left, from_right, slice(0, height), i)
-        tangent = tangent_row(count, near[i], above, below, *edges, friction)
+        tangent = with_edges(count, beside[i * count : (i + 1) * count, :], near[i], *edges)
         at = height + i * (share + PAD)
         (source,) = sources(
-            [tangent], (0 if i else rows - 1,), shares_of(observed, at, share), slab_columns
+            [tangent.astype(BF16)], (0 if i else rows - 1,), shares_of(observed, at, share), slab_columns
         )
         inside = here < last if i else here > 0
         out[i * count : (i + 1) * count, :] = jnp.where(inside, source, 0.0)
@@ -376,40 +405,70 @@
     return lower + square.T[:size] + spread
 
 
-def sketch_rows(rows, forced, omega, grid, sources, viscs, edges, visc_edges, parts):
-    total = None
-    for r in rows:
-        left, right = shifted(sources[r], *edges[r])
-        visc_side = shifted(viscs[r], *edges_from(*visc_edges, r))
-        gradient = grid[0, r : r + 1, :] * operate_row(
-            sources[r], sources[r - 1], sources[r + 1], left, right,
-            [viscs[r], viscs[r - 1], viscs[r + 1], *visc_side],
-            grid[2, r : r + 1, :],
-        )
-        value = jnp.concatenate(split(gradient + probe_row(omega, r, grid.shape[1])), axis=0)
-        parts(r)[...] = value
-        more = dot(value, value, 1)
-        total = more if total is None else total + more
-    return total
+def sketch_row(r, omega, grid, sources, viscs, edges, visc_edges):
+    source, above, below = sources
+    left, right = shifted(source, *edges)
+    gradient = grid[0, r : r + 1, :] * operate_row(
+        source, above, below, left, right,
+        [*viscs, *shifted(viscs[0], *visc_edges)],
+        grid[2, r : r + 1, :],
+    )
+    return gradient + probe_row(omega, r, grid.shape[1])
+
+
+def middle_kernel(forced, omega, grid, visc_left, visc_right, inner, out):
+    rows, height, width = forced.shape
+    count = height - PAD
+    none = jnp.zeros((count, width), F32)
+    for r in range(1, rows - 1):
+        sources = [
+            inner[(i - 1) * count : i * count, :] if 0 < i < rows - 1 else none for i in (r, r - 1, r + 1)
+        ]
+        out[(r - 1) * count : r * count, :] = sketch_row(
+            r, omega, grid, sources,
+            [forced[i, count : count + 1, :] for i in (r, r - 1, r + 1)],
+            (0.0, 0.0),
+            edges_from(visc_left, visc_right, slice(count, count + 1), r),
+        )
 
 
 def sketch_kernel(
     cells, forced, near, omega, grid, visc_left, visc_right, from_left, from_right,
-    inner, outer, halo, parts, gram,
+    inner, outer, halo, middle, parts, gram,
 ):
     rows, height, width = forced.shape
     count = height - PAD
-    sources = {r: inner[(r - 1) * count : r * count, :] for r in range(1, rows - 1)}
-    viscs = {r: forced[r, count : count + 1, :] for r in range(rows)}
-    for i, (r, beyond) in enumerate(((0, -1), (rows - 1, rows))):
-        sources[r] = outer[i * count : (i + 1) * count, :]
-        sources[beyond] = halo[i * count : (i + 1) * count, :]
-        viscs[beyond] = near[i, count : count + 1, :]
-    edges = {r: edges_from(from_left, from_right, slice(0, count), r) for r in range(rows)}
-    total = sketch_rows(
-        range(rows), forced, omega, grid, sources, viscs, edges,
-        (visc_left, visc_right, slice(count, count + 1)), parts.at.__getitem__,
-    )
+    lane = lane_of((count, LANES))
+    total = jnp.zeros((2 * count, 2 * count), F32)
+    for r in range(rows):
+        edges = edges_from(from_left, from_right, slice(0, count), r)
+        visc_edges = edges_from(visc_left, visc_right, slice(count, count + 1), r)
+        own = forced[r, count : count + 1, :]
+        if 0 < r < rows - 1:
+            value = middle[(r - 1) * count : r * count, :]
+            for beyond, source in ((0, outer[:count, :]), (rows - 1, outer[count:, :])):
+                if abs(r - beyond) == 1:
+                    face = 0.5 * (own + forced[beyond, count : count + 1, :])
+                    value = value - (grid[0, r : r + 1, :] * face) * source
+            tiles = [value[:, at : at + LANES] for at in range(0, width, LANES)]
+            for at, edge, visc, place in ((0, edges[0], visc_edges[0], 0), (-1, edges[1], visc_edges[1], LANES - 1)):
+                lanes = slice(0, LANES) if at == 0 else slice(width - LANES, width)
+                face = grid[0, r : r + 1, lanes] * (0.5 * (own[:, lanes] + visc))
+                tiles[at] = tiles[at] - jnp.where(lane == place, face * edge, 0.0)
+            value = jnp.concatenate(tiles, axis=1)
+        else:
+            i = min(r, 1)
+            mine, beside = (outer[i * count : (i + 1) * count, :], halo[i * count : (i + 1) * count, :])
+            next_row = 1 if r == 0 else r - 1
+            inside = inner[(next_row - 1) * count : next_row * count, :]
+            sources = (mine, inside, beside) if i else (mine, beside, inside)
+            viscs = forced[next_row, count : count + 1, :], near[i, count : count + 1, :]
+            value = sketch_row(
+                r, omega, grid, sources, (own, *(viscs if i else viscs[::-1])), edges, visc_edges
+            )
+        value = jnp.concatenate(split(value), axis=0)
+        parts[r] = value
+        total = total + dot(value, value, 1)
     total = total + pltpu.roll(total, count, 1)
     total = (total[:count] + total[count:]) / cells
     body, diagonal = packed(total)
@@ -597,37 +656,43 @@
     )
     sides = both_sides(sent)
     observed = all_shares(sent, sides)
-    (inner,) = call(
+    inner, inner_edges = call(
         functools.partial(inner_kernel, slab_columns, share),
-        [(((rows - 2) * count, width), F32)],
+        [(((rows - 2) * count, width), F32), ((count, LANES), F32)],
         (forced, grid, *sides, *observed),
         name="inner",
+    )
+    (middle,) = call(
+        middle_kernel,
+        [(((rows - 2) * count, width), F32)],
+        (forced, omega, grid, *sides, inner),
+        name="middle",
     )
     near, far_sent = call(
         functools.partial(far_kernel, count, share),
         [((2, height, width), F32), ((height + 2 * (share + PAD), LANES), F32)],
-        (*arrived, inner),
+        (*arrived, middle),
         name="far",
     )
     far_sides = both_sides(far_sent)
     far_observed = all_shares(far_sent, far_sides)
-    outer, source_sent = call(
+    outer, source_sent, beside = call(
         functools.partial(outer_kernel, slab_columns, share),
-        [((2 * count, width), F32), ((count, LANES), F32)],
-        (forced, near, grid, *sides, inner, *observed),
+        [((2 * count, width), F32), ((count, LANES), F32), ((2 * count, width), F32)],
+        (forced, near, grid, *sides, inner_edges, *arrived, *observed),
         name="outer",
     )
     source_sides = both_sides(source_sent)
     (halo,) = call(
-        functools.partial(halo_kernel, slab_columns, share),
+        functools.partial(halo_kernel, slab_columns, share, rows),
         [((2 * count, width), F32)],
-        (forced, near, *arrived, *far_sides, *far_observed),
+        (near, beside, *far_sides, *far_observed),
         name="halo",
     )
     parts, gram = call(
         functools.partial(sketch_kernel, cells),
         [((rows, 2 * count, width), BF16), ((1, 17 * LANES), F32)],
-        (forced, near, omega, grid, *sides, *source_sides, inner, outer, halo),
+        (forced, near, omega, grid, *sides, *source_sides, inner, outer, halo, middle),
         name="sketch",
     )
     gram = summed(gram)

time: 30.6 us -> 30.3 us (level)
  starting transfers between devices: 14.5 us -> 13.9 us
    ppermute x6, starting transfers between devices: 9.98 us -> 9.45 us  [summed(): lax.ppermute(x, ('mesh', 'obs'), [(i * columns + c, (i ^ offset) * column...]
    pallas_call x7 -> x8, Pallas kernels: 4.32 us -> 4.49 us  [call(): pl.pallas_call(body, out_shape=outs, in_specs=[pl.BlockSpec(memory_space=...]
  transfers between devices with their start and end apart: 12 -> 12, of which waited for: 10 -> 9; matrix products, arithmetic and copies ran while one was open for 0% -> 0% of each run, Pallas kernels for 6% -> 8%
where the time goes in v5:
time: 30.3 us; the launch traced here: 30.1 us
  starting transfers between devices  13.9 us (46%)
  waiting for transfers between devices  7.88 us (26%)
  Pallas kernels  6.91 us (23%)
  between operations  1.37 us (5%)
    ppermute x6, starting transfers between devices, summed(): lax.ppermute(x, ('mesh', 'obs'), [(i * columns + c, (i ^ offset) * column...  9.45 us
    ppermute x6, waiting for transfers between devices, summed(): lax.ppermute(x, ('mesh', 'obs'), [(i * columns + c, (i ^ offset) * column...  5.33 us
    pallas_call x8, Pallas kernels, call(): pl.pallas_call(body, out_shape=outs, in_specs=[pl.BlockSpec(memory_space=...  4.49 us
    ppermute x2, starting transfers between devices, exchanged(): return lax.ppermute(x, ('mesh', 'obs'), pairs)  3.01 us
    ppermute x4, waiting for transfers between devices, ring(): return lax.ppermute(x, axis, [(i, (i + step) % size) for i in range(size)])  2.54 us
    pallas_call x1, Pallas kernels, per_device(): pl.pallas_call(basis_kernel, out_shape=[jax.ShapeDtypeStruct((count * row...  2.42 us
    ppermute x4, starting transfers between devices, ring(): return lax.ppermute(x, axis, [(i, (i + step) % size) for i in range(size)])  1.44 us
  transfers between devices with their start and end apart: 12, of which 9 were waited for; matrix products, arithmetic and copies ran while one was open for 0% of the time, Pallas kernels for 8%

profile of v5, /device:TPU:0, one launch (start us, length us, event | category | flops | bytes accessed | tf_op | source)
XLA Modules:
  0.0 30.1 jit_solution(7603557086436667506)
XLA Ops:
  0.6 1.1 %edges.1 = (f32[2,512,128]{2,1,0:T(8,128)S(1)}, bf16[176,256]{1,0:T(8,128)(2,1)S(1)}, bf16[176,256]{1,0:T(8,128)(2,1)S(1)}, f32[3,8,256]{2,1,0:T(8,128)S(1)}, f32[72,128]{1,0:T(8,128)S(1)}) custom-call(bf16[64,8,256]{2,1,0:T(8,128)(2,1)} %probes.1, f32[8,256]{1,0:T(8,128)} %velocity.1, f32[8,256]{1,0:T(8,128)} %viscosity.1, f32[8,256]{1,0:T(8,128)} %friction.1, ...), custom_call_target="tpu_custom_call" | custom-call | bytes 1048576 | tf_op jit(solution)/shard_map/edges/pallas_call | solution.py:40
  1.8 3.0 %collective-permute-start = (bf16[176,256]{1,0:T(8,128)(2,1)S(1)}, bf16[176,256]{1,0:T(8,128)(2,1)S(1)}, u32[]{:S(2)}, u32[]{:S(2)}) collective-permute-start(bf16[176,256]{1,0:T(8,128)(2,1)S(1)} %get-tuple-element.24), channel_id=1, source_target_pairs={{0,2},{1,3},{2,0},{3,1},{4,6},{5,7},{6,4},{7,5},{8,10},{9,11},{10,... | collective-permute-start | bytes 270344 | tf_op jit(solution)/shard_map/ppermute | solution.py:576
  4.8 0.0 collective-permute-start.1
  4.8 0.3 forced.1
  5.0 0.6 %collective-permute-start.2 = (f32[144,128]{1,0:T(8,128)S(1)}, f32[144,128]{1,0:T(8,128)S(1)}, u32[]{:S(2)}, u32[]{:S(2)}) collective-permute-start(f32[144,128]{1,0:T(8,128)S(1)} %get-tuple-element.26.rest_0_), channel_id=1, source_target_pairs={{0,1},{1,0},{2,3},{3,2},{4,5},{5,4},{6,7},{7,6},{8,9},{9,8},{10,11... | collective-permute-start | bytes 221192 | tf_op jit(solution)/shard_map/ppermute | solution.py:565
  5.6 0.9 %collective-permute-done.2.from_left.from_right.rest_1_.visc_left.visc_right = f32[144,128]{1,0:T(8,128)S(1)} collective-permute-done((f32[144,128]{1,0:T(8,128)S(1)}, f32[144,128]{1,0:T(8,128)S(1)}, u32[]{:S(2)}, u32[]{:S(2)}) %collective-permute-start.2) | collective-permute-done | bytes 73760 | tf_op jit(solution)/shard_map/ppermute | solution.py:565
  6.5 0.8 %inner.1 = (f32[384,256]{1,0:T(8,128)S(1)}, f32[64,128]{1,0:T(8,128)S(1)}) custom-call(f32[8,72,256]{2,1,0:T(8,128)S(1)} %get-tuple-element.23.forced, f32[3,8,256]{2,1,0:T(8,128)S(1)} %get-tuple-element.21.grid, f32[144,128]{1,0:T(8,128)S(1)} %collective-permute-done.2.from_left.from_right.rest_1_.visc_left.visc_right, ...), custom_call_target="tpu_custom_call" | custom-call | bytes 1048576 | tf_op jit(solution)/shard_map/inner/pallas_call | solution.py:40
  7.3 0.4 %middle.1.early = f32[384,256]{1,0:T(8,128)S(1)} custom-call(f32[8,72,256]{2,1,0:T(8,128)S(1)} %get-tuple-element.23.forced, f32[2,512,128]{2,1,0:T(8,128)S(1)} %get-tuple-element.20.omega, f32[3,8,256]{2,1,0:T(8,128)S(1)} %get-tuple-element.21.grid, f32[144,128]{1,0:T(8,128)S(1)} %collective-permute-done.2.from_left.from_right.rest_1_.visc_left.visc_right, ...), custom_call_target="tpu_custom_call" | custom-call | bytes 1048576 | tf_op jit(solution)/shard_map/middle/pallas_call | solution.py:40
  7.8 0.0 collective-permute-done.1.second.second_in
  7.8 0.1 far.1
  8.0 0.4 %collective-permute-start.4 = (f32[216,128]{1,0:T(8,128)S(1)}, f32[216,128]{1,0:T(8,128)S(1)}, u32[]{:S(2)}, u32[]{:S(2)}) collective-permute-start(f32[216,128]{1,0:T(8,128)S(1)} %get-tuple-element.33.rest_0_), channel_id=1, source_target_pairs={{0,1},{1,0},{2,3},{3,2},{4,5},{5,4},{6,7},{7,6},{8,9},{9,8},{10,11... | collective-permute-start | bytes 331784 | tf_op jit(solution)/shard_map/ppermute | solution.py:565
  8.4 0.5 %outer.1 = (f32[128,256]{1,0:T(8,128)S(1)}, f32[64,128]{1,0:T(8,128)S(1)}, f32[128,256]{1,0:T(8,128)S(1)}) custom-call(f32[8,72,256]{2,1,0:T(8,128)S(1)} %get-tuple-element.23.forced, f32[2,72,256]{2,1,0:T(8,128)S(1)} %get-tuple-element.28.near, f32[3,8,256]{2,1,0:T(8,128)S(1)} %get-tuple-element.21.grid, ...), custom_call_target="tpu_custom_call" | custom-call | bytes 1048576 | tf_op jit(solution)/shard_map/outer/pallas_call | solution.py:40
  8.9 0.2 collective-permute-start.3
  9.1 0.2 collective-permute-done.4.from_left.from_right.rest_1_
  9.3 0.4 %halo.1 = f32[128,256]{1,0:T(8,128)S(1)} custom-call(f32[2,72,256]{2,1,0:T(8,128)S(1)} %get-tuple-element.28.near, f32[128,256]{1,0:T(8,128)S(1)} %get-tuple-element.32.beside, f32[216,128]{1,0:T(8,128)S(1)} %collective-permute-done.4.from_left.from_right.rest_1_, f32[216,128]{1,0:T(8,128)S(1)} %collective-permute-done.4.from_left.from_right.rest_1_, ...), custom_call_target="tpu_custom_call" | custom-call | bytes 1048576 | tf_op jit(solution)/shard_map/halo/pallas_call | solution.py:40
  9.8 0.4 %collective-permute-done.3.from_left.from_right = f32[64,128]{1,0:T(8,128)S(1)} collective-permute-done((f32[64,128]{1,0:T(8,128)S(1)}, f32[64,128]{1,0:T(8,128)S(1)}, u32[]{:S(2)}, u32[]{:S(2)}) %collective-permute-start.3) | collective-permute-done | bytes 32800 | tf_op jit(solution)/shard_map/ppermute | solution.py:565
  10.2 0.8 %sketch.1 = (bf16[8,128,256]{2,1,0:T(8,128)(2,1)S(1)}, f32[1,2176]{1,0:T(1,128)S(1)}) custom-call(f32[8,72,256]{2,1,0:T(8,128)S(1)} %get-tuple-element.23.forced, f32[2,72,256]{2,1,0:T(8,128)S(1)} %get-tuple-element.28.near, f32[2,512,128]{2,1,0:T(8,128)S(1)} %get-tuple-element.20.omega, f32[3,8,256]{2,1,0:T(8,128)S(1)} %get-tuple-element.21.grid, ...), custom_call_target="tpu_custom_call" | custom-call | bytes 1048576 | tf_op jit(solution)/shard_map/sketch/pallas_call | solution.py:40
  11.0 0.2 collective-permute-start.5
  11.2 1.0 %collective-permute-done.5 = f32[1,2176]{1,0:T(1,128)S(1)} collective-permute-done((f32[1,2176]{1,0:T(1,128)S(1)}, f32[1,2176]{1,0:T(1,128)S(1)}, u32[]{:S(2)}, u32[]{:S(2)}) %collective-permute-start.5) | collective-permute-done | bytes 8736 | tf_op jit(solution)/shard_map/ppermute | solution.py:565
  12.2 4.0 %collective-permute-start.6 = (f32[1,2176]{1,0:T(1,128)S(1)}, f32[1,2176]{1,0:T(1,128)S(1)}, u32[]{:S(2)}, u32[]{:S(2)}) collective-permute-start(f32[1,2176]{1,0:T(1,128)S(1)} %add.21), channel_id=1, source_target_pairs={{0,3},{1,2},{2,1},{3,0},{4,7},{5,6},{6,5},{7,4},{8,11},{9,10},{10,... | collective-permute-start | bytes 26120 | tf_op jit(solution)/shard_map/ppermute | solution.py:588
  16.2 0.9 %collective-permute-start.7 = (f32[1,2176]{1,0:T(1,128)S(1)}, f32[1,2176]{1,0:T(1,128)S(1)}, u32[]{:S(2)}, u32[]{:S(2)}) collective-permute-start(f32[1,2176]{1,0:T(1,128)S(1)} %add.21), channel_id=1, source_target_pairs={{0,5},{1,4},{2,7},{3,6},{4,1},{5,0},{6,3},{7,2},{8,13},{9,12},{10,... | collective-permute-start | bytes 26120 | tf_op jit(solution)/shard_map/ppermute | solution.py:588
  17.1 0.4 %collective-permute-start.8 = (f32[1,2176]{1,0:T(1,128)S(1)}, f32[1,2176]{1,0:T(1,128)S(1)}, u32[]{:S(2)}, u32[]{:S(2)}) collective-permute-start(f32[1,2176]{1,0:T(1,128)S(1)} %add.21), channel_id=1, source_target_pairs={{0,7},{1,6},{2,5},{3,4},{4,3},{5,2},{6,1},{7,0},{8,15},{9,14},{10,... | collective-permute-start | bytes 26120 | tf_op jit(solution)/shard_map/ppermute | solution.py:588
  17.5 0.1 collective-permute-done.6
  17.6 1.7 %collective-permute-done.7 = f32[1,2176]{1,0:T(1,128)S(1)} collective-permute-done((f32[1,2176]{1,0:T(1,128)S(1)}, f32[1,2176]{1,0:T(1,128)S(1)}, u32[]{:S(2)}, u32[]{:S(2)}) %collective-permute-start.7) | collective-permute-done | bytes 8736 | tf_op jit(solution)/shard_map/ppermute | solution.py:588
  19.3 1.8 %collective-permute-done.8 = f32[1,2176]{1,0:T(1,128)S(1)} collective-permute-done((f32[1,2176]{1,0:T(1,128)S(1)}, f32[1,2176]{1,0:T(1,128)S(1)}, u32[]{:S(2)}, u32[]{:S(2)}) %collective-permute-start.8) | collective-permute-done | bytes 8736 | tf_op jit(solution)/shard_map/ppermute | solution.py:588
  21.1 2.5 %collective-permute-start.10 = (f32[1,2176]{1,0:T(1,128)S(1)}, f32[1,2176]{1,0:T(1,128)S(1)}, u32[]{:S(2)}, u32[]{:S(2)}) collective-permute-start(f32[1,2176]{1,0:T(1,128)S(1)} %add_add_fusion.1), channel_id=1, source_target_pairs={{0,25},{1,24},{2,27},{3,26},{4,29},{5,28},{6,31},{7,30},{8,17},{9,... | collective-permute-start | bytes 26120 | tf_op jit(solution)/shard_map/ppermute | solution.py:588
  23.7 0.3 collective-permute-start.11
  24.0 1.3 %collective-permute-start.9 = (f32[1,2176]{1,0:T(1,128)S(1)}, f32[1,2176]{1,0:T(1,128)S(1)}, u32[]{:S(2)}, u32[]{:S(2)}) collective-permute-start(f32[1,2176]{1,0:T(1,128)S(1)} %add_add_fusion.1), channel_id=1, source_target_pairs={{0,9},{1,8},{2,11},{3,10},{4,13},{5,12},{6,15},{7,14},{8,1},{9,0},... | collective-permute-start | bytes 26120 | tf_op jit(solution)/shard_map/ppermute | solution.py:588
  25.9 0.2 collective-permute-done.10
  26.1 1.6 %collective-permute-done.11 = f32[1,2176]{1,0:T(1,128)S(1)} collective-permute-done((f32[1,2176]{1,0:T(1,128)S(1)}, f32[1,2176]{1,0:T(1,128)S(1)}, u32[]{:S(2)}, u32[]{:S(2)}) %collective-permute-start.11) | collective-permute-done | bytes 8736 | tf_op jit(solution)/shard_map/ppermute | solution.py:588
  27.7 0.0 collective-permute-done.9
  27.7 2.4 %basis.1 = (f32[512,256]{1,0:T(8,128)}, f32[64,64]{1,0:T(8,128)}) custom-call(s32[1]{0:T(128)S(6)} %copy.10.rank, f32[1,2176]{1,0:T(1,128)S(1)} %add_add_fusion.gram, bf16[8,128,256]{2,1,0:T(8,128)(2,1)S(1)} %get-tuple-element.35.parts), custom_call_target="tpu_custom_call" | custom-call | tf_op jit(solution)/shard_map/basis/pallas_call | solution.py:699
  (4 shorter events, 0.0 us)
Async XLA Ops:
  1.8 6.0 %collective-permute-start = (bf16[176,256]{1,0:T(8,128)(2,1)S(1)}, bf16[176,256]{1,0:T(8,128)(2,1)S(1)}, u32[]{:S(2)}, u32[]{:S(2)}) collective-permute-start(bf16[176,256]{1,0:T(8,128)(2,1)S(1)} %get-tuple-element.24), channel_id=1, source_target_pairs={{0,2},{1,3},{2,0},{3,1},{4,6},{5,7},{6,4},{7,5},{8,10},{9,11},{10,... | collective-permute-start | bytes 270344 | tf_op jit(solution)/shard_map/ppermute | solution.py:576
  4.8 3.0 %collective-permute-start.1 = (bf16[176,256]{1,0:T(8,128)(2,1)S(1)}, bf16[176,256]{1,0:T(8,128)(2,1)S(1)}, u32[]{:S(2)}, u32[]{:S(2)}) collective-permute-start(bf16[176,256]{1,0:T(8,128)(2,1)S(1)} %get-tuple-element.25), channel_id=1, source_target_pairs={{0,1},{1,0},{2,4},{3,5},{4,2},{5,3},{6,8},{7,9},{8,6},{9,7},{10,12... | collective-permute-start | bytes 270344 | tf_op jit(solution)/shard_map/ppermute | solution.py:576
  5.0 1.5 %collective-permute-start.2 = (f32[144,128]{1,0:T(8,128)S(1)}, f32[144,128]{1,0:T(8,128)S(1)}, u32[]{:S(2)}, u32[]{:S(2)}) collective-permute-start(f32[144,128]{1,0:T(8,128)S(1)} %get-tuple-element.26.rest_0_), channel_id=1, source_target_pairs={{0,1},{1,0},{2,3},{3,2},{4,5},{5,4},{6,7},{7,6},{8,9},{9,8},{10,11... | collective-permute-start | bytes 221192 | tf_op jit(solution)/shard_map/ppermute | solution.py:565
  8.0 1.4 %collective-permute-start.4 = (f32[216,128]{1,0:T(8,128)S(1)}, f32[216,128]{1,0:T(8,128)S(1)}, u32[]{:S(2)}, u32[]{:S(2)}) collective-permute-start(f32[216,128]{1,0:T(8,128)S(1)} %get-tuple-element.33.rest_0_), channel_id=1, source_target_pairs={{0,1},{1,0},{2,3},{3,2},{4,5},{5,4},{6,7},{7,6},{8,9},{9,8},{10,11... | collective-permute-start | bytes 331784 | tf_op jit(solution)/shard_map/ppermute | solution.py:565
  8.9 1.3 %collective-permute-start.3 = (f32[64,128]{1,0:T(8,128)S(1)}, f32[64,128]{1,0:T(8,128)S(1)}, u32[]{:S(2)}, u32[]{:S(2)}) collective-permute-start(f32[64,128]{1,0:T(8,128)S(1)} %get-tuple-element.30), channel_id=1, source_target_pairs={{0,1},{1,0},{2,3},{3,2},{4,5},{5,4},{6,7},{7,6},{8,9},{9,8},{10,11... | collective-permute-start | bytes 98312 | tf_op jit(solution)/shard_map/ppermute | solution.py:565
  11.0 1.2 %collective-permute-start.5 = (f32[1,2176]{1,0:T(1,128)S(1)}, f32[1,2176]{1,0:T(1,128)S(1)}, u32[]{:S(2)}, u32[]{:S(2)}) collective-permute-start(f32[1,2176]{1,0:T(1,128)S(1)} %get-tuple-element.34), channel_id=1, source_target_pairs={{0,1},{1,0},{2,3},{3,2},{4,5},{5,4},{6,7},{7,6},{8,9},{9,8},{10,11... | collective-permute-start | bytes 26120 | tf_op jit(solution)/shard_map/ppermute | solution.py:565
  12.2 5.4 %collective-permute-start.6 = (f32[1,2176]{1,0:T(1,128)S(1)}, f32[1,2176]{1,0:T(1,128)S(1)}, u32[]{:S(2)}, u32[]{:S(2)}) collective-permute-start(f32[1,2176]{1,0:T(1,128)S(1)} %add.21), channel_id=1, source_target_pairs={{0,3},{1,2},{2,1},{3,0},{4,7},{5,6},{6,5},{7,4},{8,11},{9,10},{10,... | collective-permute-start | bytes 26120 | tf_op jit(solution)/shard_map/ppermute | solution.py:588
  16.2 3.1 %collective-permute-start.7 = (f32[1,2176]{1,0:T(1,128)S(1)}, f32[1,2176]{1,0:T(1,128)S(1)}, u32[]{:S(2)}, u32[]{:S(2)}) collective-permute-start(f32[1,2176]{1,0:T(1,128)S(1)} %add.21), channel_id=1, source_target_pairs={{0,5},{1,4},{2,7},{3,6},{4,1},{5,0},{6,3},{7,2},{8,13},{9,12},{10,... | collective-permute-start | bytes 26120 | tf_op jit(solution)/shard_map/ppermute | solution.py:588
  17.1 4.0 %collective-permute-start.8 = (f32[1,2176]{1,0:T(1,128)S(1)}, f32[1,2176]{1,0:T(1,128)S(1)}, u32[]{:S(2)}, u32[]{:S(2)}) collective-permute-start(f32[1,2176]{1,0:T(1,128)S(1)} %add.21), channel_id=1, source_target_pairs={{0,7},{1,6},{2,5},{3,4},{4,3},{5,2},{6,1},{7,0},{8,15},{9,14},{10,... | collective-permute-start | bytes 26120 | tf_op jit(solution)/shard_map/ppermute | solution.py:588
  21.1 4.9 %collective-permute-start.10 = (f32[1,2176]{1,0:T(1,128)S(1)}, f32[1,2176]{1,0:T(1,128)S(1)}, u32[]{:S(2)}, u32[]{:S(2)}) collective-permute-start(f32[1,2176]{1,0:T(1,128)S(1)} %add_add_fusion.1), channel_id=1, source_target_pairs={{0,25},{1,24},{2,27},{3,26},{4,29},{5,28},{6,31},{7,30},{8,17},{9,... | collective-permute-start | bytes 26120 | tf_op jit(solution)/shard_map/ppermute | solution.py:588
  23.7 4.0 %collective-permute-start.11 = (f32[1,2176]{1,0:T(1,128)S(1)}, f32[1,2176]{1,0:T(1,128)S(1)}, u32[]{:S(2)}, u32[]{:S(2)}) collective-permute-start(f32[1,2176]{1,0:T(1,128)S(1)} %add_add_fusion.1), channel_id=1, source_target_pairs={{0,17},{1,16},{2,19},{3,18},{4,21},{5,20},{6,23},{7,22},{8,25},{9,... | collective-permute-start | bytes 26120 | tf_op jit(solution)/shard_map/ppermute | solution.py:588
  24.0 3.7 %collective-permute-start.9 = (f32[1,2176]{1,0:T(1,128)S(1)}, f32[1,2176]{1,0:T(1,128)S(1)}, u32[]{:S(2)}, u32[]{:S(2)}) collective-permute-start(f32[1,2176]{1,0:T(1,128)S(1)} %add_add_fusion.1), channel_id=1, source_target_pairs={{0,9},{1,8},{2,11},{3,10},{4,13},{5,12},{6,15},{7,14},{8,1},{9,0},... | collective-permute-start | bytes 26120 | tf_op jit(solution)/shard_map/ppermute | solution.py:588

commit v6 on v5

--- a/solution.py
+++ b/solution.py
@@ -539,15 +539,15 @@
     inverse = jnp.where((lane <= row) & (row < rank[0]), inverse, 0.0)
     high = inverse.astype(BF16).astype(F32)
     high, low = (x + pltpu.roll(x, count, 1) for x in (high, inverse - high))
-    left = jnp.concatenate([high, low], axis=1).astype(BF16)
+    left = jnp.concatenate([high, low], axis=0).astype(BF16)
     rows = parts.shape[0]
     copies = [pltpu.make_async_copy(lower, factor, sems.at[turned.shape[0]])]
     for c in range(turned.shape[0]):
         lanes = slice(c * LANES, (c + 1) * LANES)
         for r in range(rows):
             part = parts[r, :, lanes]
-            value = dot(left, jnp.concatenate([part, part], axis=0))
-            turned[c, pl.ds(r, count, stride=rows), :] = value
+            value = dot(left, part)
+            turned[c, pl.ds(r, count, stride=rows), :] = value[:count] + value[count:]
         copy = pltpu.make_async_copy(turned.at[c], basis.at[:, lanes], sems.at[c])
         copy.start()
         copies.append(copy)
@@ -579,11 +579,12 @@
 def summed(x):
     rows, columns = lax.axis_size("mesh"), lax.axis_size("obs")
     x = x + ring(x, "obs", 1) if columns == 2 else lax.psum(x, "obs")
-    step = 1
-    while step < rows:
-        offsets = (step, 2 * step, 3 * step) if step == 1 else (step, 3 * step, 2 * step)
-        if rows % (4 * step):
-            offsets = (step,)
+    if rows & (rows - 1):
+        return lax.psum(x, "mesh")
+    rounds = [(1 << bit,) for bit in range(rows.bit_length() - 2, 2, -1)]
+    rounds += [(1, 3, 2) if rows > 2 else (1,)] if rows > 1 else []
+    rounds += [(4,)] if rows > 4 else []
+    for offsets in rounds:
         pieces = [
             lax.ppermute(
                 x,
@@ -598,7 +599,6 @@
         ]
         for piece in pieces:
             x = x + piece
-        step = step * (len(offsets) + 1)
     return x
 
 

time: 30.3 us -> 30.1 us (level)
  waiting for transfers between devices: 7.88 us -> 6.93 us
  starting transfers between devices: 13.9 us -> 14.7 us
    ppermute x6 -> x5, waiting for transfers between devices: 5.33 us -> 4.38 us  [summed(): lax.ppermute(x, ('mesh', 'obs'), [(i * columns + c, (i ^ offset) * column...]
    ppermute x6 -> x5, starting transfers between devices: 9.45 us -> 10.3 us  [summed(): lax.ppermute(x, ('mesh', 'obs'), [(i * columns + c, (i ^ offset) * column...]
  transfers between devices with their start and end apart: 12 -> 11, of which waited for: 9 -> 9; matrix products, arithmetic and copies ran while one was open for 0% -> 0% of each run, Pallas kernels for 8% -> 8%
where the time goes in v6:
time: 30.1 us; the launch traced here: 30 us
  starting transfers between devices  14.7 us (49%)
  waiting for transfers between devices  6.93 us (23%)
  Pallas kernels  6.91 us (23%)
  between operations  1.38 us (5%)
    ppermute x5, starting transfers between devices, summed(): lax.ppermute(x, ('mesh', 'obs'), [(i * columns + c, (i ^ offset) * column...  10.3 us
    pallas_call x8, Pallas kernels, call(): pl.pallas_call(body, out_shape=outs, in_specs=[pl.BlockSpec(memory_space=...  4.49 us
    ppermute x5, waiting for transfers between devices, summed(): lax.ppermute(x, ('mesh', 'obs'), [(i * columns + c, (i ^ offset) * column...  4.38 us
    ppermute x2, starting transfers between devices, exchanged(): return lax.ppermute(x, ('mesh', 'obs'), pairs)  3.01 us
    ppermute x4, waiting for transfers between devices, ring(): return lax.ppermute(x, axis, [(i, (i + step) % size) for i in range(size)])  2.54 us
    pallas_call x1, Pallas kernels, per_device(): pl.pallas_call(basis_kernel, out_shape=[jax.ShapeDtypeStruct((count * row...  2.42 us
    ppermute x4, starting transfers between devices, ring(): return lax.ppermute(x, axis, [(i, (i + step) % size) for i in range(size)])  1.44 us
  transfers between devices with their start and end apart: 11, of which 9 were waited for; matrix products, arithmetic and copies ran while one was open for 0% of the time, Pallas kernels for 8%

profile of v6, /device:TPU:0, one launch (start us, length us, event | category | flops | bytes accessed | tf_op | source)
XLA Modules:
  0.0 30.0 jit_solution(16619466565180328511)
XLA Ops:
  0.6 1.1 %edges.1 = (f32[2,512,128]{2,1,0:T(8,128)S(1)}, bf16[176,256]{1,0:T(8,128)(2,1)S(1)}, bf16[176,256]{1,0:T(8,128)(2,1)S(1)}, f32[3,8,256]{2,1,0:T(8,128)S(1)}, f32[72,128]{1,0:T(8,128)S(1)}) custom-call(bf16[64,8,256]{2,1,0:T(8,128)(2,1)} %probes.1, f32[8,256]{1,0:T(8,128)} %velocity.1, f32[8,256]{1,0:T(8,128)} %viscosity.1, f32[8,256]{1,0:T(8,128)} %friction.1, ...), custom_call_target="tpu_custom_call" | custom-call | bytes 1048576 | tf_op jit(solution)/shard_map/edges/pallas_call | solution.py:40
  1.8 3.0 %collective-permute-start = (bf16[176,256]{1,0:T(8,128)(2,1)S(1)}, bf16[176,256]{1,0:T(8,128)(2,1)S(1)}, u32[]{:S(2)}, u32[]{:S(2)}) collective-permute-start(bf16[176,256]{1,0:T(8,128)(2,1)S(1)} %get-tuple-element.24), channel_id=1, source_target_pairs={{0,2},{1,3},{2,0},{3,1},{4,6},{5,7},{6,4},{7,5},{8,10},{9,11},{10,... | collective-permute-start | bytes 270344 | tf_op jit(solution)/shard_map/ppermute | solution.py:576
  4.8 0.0 collective-permute-start.1
  4.8 0.3 forced.1
  5.0 0.6 %collective-permute-start.2 = (f32[144,128]{1,0:T(8,128)S(1)}, f32[144,128]{1,0:T(8,128)S(1)}, u32[]{:S(2)}, u32[]{:S(2)}) collective-permute-start(f32[144,128]{1,0:T(8,128)S(1)} %get-tuple-element.26.rest_0_), channel_id=1, source_target_pairs={{0,1},{1,0},{2,3},{3,2},{4,5},{5,4},{6,7},{7,6},{8,9},{9,8},{10,11... | collective-permute-start | bytes 221192 | tf_op jit(solution)/shard_map/ppermute | solution.py:565
  5.6 0.9 %collective-permute-done.2.from_left.from_right.rest_1_.visc_left.visc_right = f32[144,128]{1,0:T(8,128)S(1)} collective-permute-done((f32[144,128]{1,0:T(8,128)S(1)}, f32[144,128]{1,0:T(8,128)S(1)}, u32[]{:S(2)}, u32[]{:S(2)}) %collective-permute-start.2) | collective-permute-done | bytes 73760 | tf_op jit(solution)/shard_map/ppermute | solution.py:565
  6.5 0.8 %inner.1 = (f32[384,256]{1,0:T(8,128)S(1)}, f32[64,128]{1,0:T(8,128)S(1)}) custom-call(f32[8,72,256]{2,1,0:T(8,128)S(1)} %get-tuple-element.23.forced, f32[3,8,256]{2,1,0:T(8,128)S(1)} %get-tuple-element.21.grid, f32[144,128]{1,0:T(8,128)S(1)} %collective-permute-done.2.from_left.from_right.rest_1_.visc_left.visc_right, ...), custom_call_target="tpu_custom_call" | custom-call | bytes 1048576 | tf_op jit(solution)/shard_map/inner/pallas_call | solution.py:40
  7.3 0.4 %middle.1.early = f32[384,256]{1,0:T(8,128)S(1)} custom-call(f32[8,72,256]{2,1,0:T(8,128)S(1)} %get-tuple-element.23.forced, f32[2,512,128]{2,1,0:T(8,128)S(1)} %get-tuple-element.20.omega, f32[3,8,256]{2,1,0:T(8,128)S(1)} %get-tuple-element.21.grid, f32[144,128]{1,0:T(8,128)S(1)} %collective-permute-done.2.from_left.from_right.rest_1_.visc_left.visc_right, ...), custom_call_target="tpu_custom_call" | custom-call | bytes 1048576 | tf_op jit(solution)/shard_map/middle/pallas_call | solution.py:40
  7.8 0.0 collective-permute-done.first.first_in
  7.8 0.0 collective-permute-done.1.second.second_in
  7.8 0.1 far.1
  8.0 0.4 %collective-permute-start.4 = (f32[216,128]{1,0:T(8,128)S(1)}, f32[216,128]{1,0:T(8,128)S(1)}, u32[]{:S(2)}, u32[]{:S(2)}) collective-permute-start(f32[216,128]{1,0:T(8,128)S(1)} %get-tuple-element.33.rest_0_), channel_id=1, source_target_pairs={{0,1},{1,0},{2,3},{3,2},{4,5},{5,4},{6,7},{7,6},{8,9},{9,8},{10,11... | collective-permute-start | bytes 331784 | tf_op jit(solution)/shard_map/ppermute | solution.py:565
  8.4 0.5 %outer.1 = (f32[128,256]{1,0:T(8,128)S(1)}, f32[64,128]{1,0:T(8,128)S(1)}, f32[128,256]{1,0:T(8,128)S(1)}) custom-call(f32[8,72,256]{2,1,0:T(8,128)S(1)} %get-tuple-element.23.forced, f32[2,72,256]{2,1,0:T(8,128)S(1)} %get-tuple-element.28.near, f32[3,8,256]{2,1,0:T(8,128)S(1)} %get-tuple-element.21.grid, ...), custom_call_target="tpu_custom_call" | custom-call | bytes 1048576 | tf_op jit(solution)/shard_map/outer/pallas_call | solution.py:40
  8.9 0.2 collective-permute-start.3
  9.1 0.2 collective-permute-done.4.from_left.from_right.rest_1_
  9.3 0.4 %halo.1 = f32[128,256]{1,0:T(8,128)S(1)} custom-call(f32[2,72,256]{2,1,0:T(8,128)S(1)} %get-tuple-element.28.near, f32[128,256]{1,0:T(8,128)S(1)} %get-tuple-element.32.beside, f32[216,128]{1,0:T(8,128)S(1)} %collective-permute-done.4.from_left.from_right.rest_1_, f32[216,128]{1,0:T(8,128)S(1)} %collective-permute-done.4.from_left.from_right.rest_1_, ...), custom_call_target="tpu_custom_call" | custom-call | bytes 1048576 | tf_op jit(solution)/shard_map/halo/pallas_call | solution.py:40
  9.8 0.4 %collective-permute-done.3.from_left.from_right = f32[64,128]{1,0:T(8,128)S(1)} collective-permute-done((f32[64,128]{1,0:T(8,128)S(1)}, f32[64,128]{1,0:T(8,128)S(1)}, u32[]{:S(2)}, u32[]{:S(2)}) %collective-permute-start.3) | collective-permute-done | bytes 32800 | tf_op jit(solution)/shard_map/ppermute | solution.py:565
  10.2 0.8 %sketch.1 = (bf16[8,128,256]{2,1,0:T(8,128)(2,1)S(1)}, f32[1,2176]{1,0:T(1,128)S(1)}) custom-call(f32[8,72,256]{2,1,0:T(8,128)S(1)} %get-tuple-element.23.forced, f32[2,72,256]{2,1,0:T(8,128)S(1)} %get-tuple-element.28.near, f32[2,512,128]{2,1,0:T(8,128)S(1)} %get-tuple-element.20.omega, f32[3,8,256]{2,1,0:T(8,128)S(1)} %get-tuple-element.21.grid, ...), custom_call_target="tpu_custom_call" | custom-call | bytes 1048576 | tf_op jit(solution)/shard_map/sketch/pallas_call | solution.py:40
  11.0 0.2 collective-permute-start.5
  11.2 1.0 %collective-permute-done.5 = f32[1,2176]{1,0:T(1,128)S(1)} collective-permute-done((f32[1,2176]{1,0:T(1,128)S(1)}, f32[1,2176]{1,0:T(1,128)S(1)}, u32[]{:S(2)}, u32[]{:S(2)}) %collective-permute-start.5) | collective-permute-done | bytes 8736 | tf_op jit(solution)/shard_map/ppermute | solution.py:565
  12.2 5.7 %collective-permute-start.6 = (f32[1,2176]{1,0:T(1,128)S(1)}, f32[1,2176]{1,0:T(1,128)S(1)}, u32[]{:S(2)}, u32[]{:S(2)}) collective-permute-start(f32[1,2176]{1,0:T(1,128)S(1)} %add.18), channel_id=1, source_target_pairs={{0,17},{1,16},{2,19},{3,18},{4,21},{5,20},{6,23},{7,22},{8,25},{9,... | collective-permute-start | bytes 26120 | tf_op jit(solution)/shard_map/ppermute | solution.py:589
  17.9 1.4 %collective-permute-done.6 = f32[1,2176]{1,0:T(1,128)S(1)} collective-permute-done((f32[1,2176]{1,0:T(1,128)S(1)}, f32[1,2176]{1,0:T(1,128)S(1)}, u32[]{:S(2)}, u32[]{:S(2)}) %collective-permute-start.6) | collective-permute-done | bytes 8736 | tf_op jit(solution)/shard_map/ppermute | solution.py:589
  19.3 1.0 %collective-permute-start.7 = (f32[1,2176]{1,0:T(1,128)S(1)}, f32[1,2176]{1,0:T(1,128)S(1)}, u32[]{:S(2)}, u32[]{:S(2)}) collective-permute-start(f32[1,2176]{1,0:T(1,128)S(1)} %add.19), channel_id=1, source_target_pairs={{0,3},{1,2},{2,1},{3,0},{4,7},{5,6},{6,5},{7,4},{8,11},{9,10},{10,... | collective-permute-start | bytes 26120 | tf_op jit(solution)/shard_map/ppermute | solution.py:589
  20.3 0.9 %collective-permute-start.8 = (f32[1,2176]{1,0:T(1,128)S(1)}, f32[1,2176]{1,0:T(1,128)S(1)}, u32[]{:S(2)}, u32[]{:S(2)}) collective-permute-start(f32[1,2176]{1,0:T(1,128)S(1)} %add.19), channel_id=1, source_target_pairs={{0,7},{1,6},{2,5},{3,4},{4,3},{5,2},{6,1},{7,0},{8,15},{9,14},{10,... | collective-permute-start | bytes 26120 | tf_op jit(solution)/shard_map/ppermute | solution.py:589
  21.2 1.1 %collective-permute-start.9 = (f32[1,2176]{1,0:T(1,128)S(1)}, f32[1,2176]{1,0:T(1,128)S(1)}, u32[]{:S(2)}, u32[]{:S(2)}) collective-permute-start(f32[1,2176]{1,0:T(1,128)S(1)} %add.19), channel_id=1, source_target_pairs={{0,5},{1,4},{2,7},{3,6},{4,1},{5,0},{6,3},{7,2},{8,13},{9,12},{10,... | collective-permute-start | bytes 26120 | tf_op jit(solution)/shard_map/ppermute | solution.py:589
  22.3 0.1 collective-permute-done.7
  22.4 1.8 %collective-permute-done.8 = f32[1,2176]{1,0:T(1,128)S(1)} collective-permute-done((f32[1,2176]{1,0:T(1,128)S(1)}, f32[1,2176]{1,0:T(1,128)S(1)}, u32[]{:S(2)}, u32[]{:S(2)}) %collective-permute-start.8) | collective-permute-done | bytes 8736 | tf_op jit(solution)/shard_map/ppermute | solution.py:589
  24.3 0.1 collective-permute-done.9
  24.4 1.5 %collective-permute-start.10 = (f32[1,2176]{1,0:T(1,128)S(1)}, f32[1,2176]{1,0:T(1,128)S(1)}, u32[]{:S(2)}, u32[]{:S(2)}) collective-permute-start(f32[1,2176]{1,0:T(1,128)S(1)} %add_add_fusion), channel_id=1, source_target_pairs={{0,9},{1,8},{2,11},{3,10},{4,13},{5,12},{6,15},{7,14},{8,1},{9,0},... | collective-permute-start | bytes 26120 | tf_op jit(solution)/shard_map/ppermute | solution.py:589
  26.6 1.0 %collective-permute-done.10 = f32[1,2176]{1,0:T(1,128)S(1)} collective-permute-done((f32[1,2176]{1,0:T(1,128)S(1)}, f32[1,2176]{1,0:T(1,128)S(1)}, u32[]{:S(2)}, u32[]{:S(2)}) %collective-permute-start.10) | collective-permute-done | bytes 8736 | tf_op jit(solution)/shard_map/ppermute | solution.py:589
  27.5 2.4 %basis.1 = (f32[512,256]{1,0:T(8,128)}, f32[64,64]{1,0:T(8,128)}) custom-call(s32[1]{0:T(128)S(6)} %copy.10.rank, f32[1,2176]{1,0:T(1,128)S(1)} %add.23.gram, bf16[8,128,256]{2,1,0:T(8,128)(2,1)S(1)} %get-tuple-element.35.parts), custom_call_target="tpu_custom_call" | custom-call | tf_op jit(solution)/shard_map/basis/pallas_call | solution.py:699
  (4 shorter events, 0.0 us)
Async XLA Ops:
  1.8 6.0 %collective-permute-start = (bf16[176,256]{1,0:T(8,128)(2,1)S(1)}, bf16[176,256]{1,0:T(8,128)(2,1)S(1)}, u32[]{:S(2)}, u32[]{:S(2)}) collective-permute-start(bf16[176,256]{1,0:T(8,128)(2,1)S(1)} %get-tuple-element.24), channel_id=1, source_target_pairs={{0,2},{1,3},{2,0},{3,1},{4,6},{5,7},{6,4},{7,5},{8,10},{9,11},{10,... | collective-permute-start | bytes 270344 | tf_op jit(solution)/shard_map/ppermute | solution.py:576
  4.8 3.0 %collective-permute-start.1 = (bf16[176,256]{1,0:T(8,128)(2,1)S(1)}, bf16[176,256]{1,0:T(8,128)(2,1)S(1)}, u32[]{:S(2)}, u32[]{:S(2)}) collective-permute-start(bf16[176,256]{1,0:T(8,128)(2,1)S(1)} %get-tuple-element.25), channel_id=1, source_target_pairs={{0,1},{1,0},{2,4},{3,5},{4,2},{5,3},{6,8},{7,9},{8,6},{9,7},{10,12... | collective-permute-start | bytes 270344 | tf_op jit(solution)/shard_map/ppermute | solution.py:576
  5.0 1.5 %collective-permute-start.2 = (f32[144,128]{1,0:T(8,128)S(1)}, f32[144,128]{1,0:T(8,128)S(1)}, u32[]{:S(2)}, u32[]{:S(2)}) collective-permute-start(f32[144,128]{1,0:T(8,128)S(1)} %get-tuple-element.26.rest_0_), channel_id=1, source_target_pairs={{0,1},{1,0},{2,3},{3,2},{4,5},{5,4},{6,7},{7,6},{8,9},{9,8},{10,11... | collective-permute-start | bytes 221192 | tf_op jit(solution)/shard_map/ppermute | solution.py:565
  8.0 1.4 %collective-permute-start.4 = (f32[216,128]{1,0:T(8,128)S(1)}, f32[216,128]{1,0:T(8,128)S(1)}, u32[]{:S(2)}, u32[]{:S(2)}) collective-permute-start(f32[216,128]{1,0:T(8,128)S(1)} %get-tuple-element.33.rest_0_), channel_id=1, source_target_pairs={{0,1},{1,0},{2,3},{3,2},{4,5},{5,4},{6,7},{7,6},{8,9},{9,8},{10,11... | collective-permute-start | bytes 331784 | tf_op jit(solution)/shard_map/ppermute | solution.py:565
  8.9 1.3 %collective-permute-start.3 = (f32[64,128]{1,0:T(8,128)S(1)}, f32[64,128]{1,0:T(8,128)S(1)}, u32[]{:S(2)}, u32[]{:S(2)}) collective-permute-start(f32[64,128]{1,0:T(8,128)S(1)} %get-tuple-element.30), channel_id=1, source_target_pairs={{0,1},{1,0},{2,3},{3,2},{4,5},{5,4},{6,7},{7,6},{8,9},{9,8},{10,11... | collective-permute-start | bytes 98312 | tf_op jit(solution)/shard_map/ppermute | solution.py:565
  11.0 1.2 %collective-permute-start.5 = (f32[1,2176]{1,0:T(1,128)S(1)}, f32[1,2176]{1,0:T(1,128)S(1)}, u32[]{:S(2)}, u32[]{:S(2)}) collective-permute-start(f32[1,2176]{1,0:T(1,128)S(1)} %get-tuple-element.34), channel_id=1, source_target_pairs={{0,1},{1,0},{2,3},{3,2},{4,5},{5,4},{6,7},{7,6},{8,9},{9,8},{10,11... | collective-permute-start | bytes 26120 | tf_op jit(solution)/shard_map/ppermute | solution.py:565
  12.2 7.1 %collective-permute-start.6 = (f32[1,2176]{1,0:T(1,128)S(1)}, f32[1,2176]{1,0:T(1,128)S(1)}, u32[]{:S(2)}, u32[]{:S(2)}) collective-permute-start(f32[1,2176]{1,0:T(1,128)S(1)} %add.18), channel_id=1, source_target_pairs={{0,17},{1,16},{2,19},{3,18},{4,21},{5,20},{6,23},{7,22},{8,25},{9,... | collective-permute-start | bytes 26120 | tf_op jit(solution)/shard_map/ppermute | solution.py:589
  19.3 3.1 %collective-permute-start.7 = (f32[1,2176]{1,0:T(1,128)S(1)}, f32[1,2176]{1,0:T(1,128)S(1)}, u32[]{:S(2)}, u32[]{:S(2)}) collective-permute-start(f32[1,2176]{1,0:T(1,128)S(1)} %add.19), channel_id=1, source_target_pairs={{0,3},{1,2},{2,1},{3,0},{4,7},{5,6},{6,5},{7,4},{8,11},{9,10},{10,... | collective-permute-start | bytes 26120 | tf_op jit(solution)/shard_map/ppermute | solution.py:589
  20.3 4.0 %collective-permute-start.8 = (f32[1,2176]{1,0:T(1,128)S(1)}, f32[1,2176]{1,0:T(1,128)S(1)}, u32[]{:S(2)}, u32[]{:S(2)}) collective-permute-start(f32[1,2176]{1,0:T(1,128)S(1)} %add.19), channel_id=1, source_target_pairs={{0,7},{1,6},{2,5},{3,4},{4,3},{5,2},{6,1},{7,0},{8,15},{9,14},{10,... | collective-permute-start | bytes 26120 | tf_op jit(solution)/shard_map/ppermute | solution.py:589
  21.2 3.1 %collective-permute-start.9 = (f32[1,2176]{1,0:T(1,128)S(1)}, f32[1,2176]{1,0:T(1,128)S(1)}, u32[]{:S(2)}, u32[]{:S(2)}) collective-permute-start(f32[1,2176]{1,0:T(1,128)S(1)} %add.19), channel_id=1, source_target_pairs={{0,5},{1,4},{2,7},{3,6},{4,1},{5,0},{6,3},{7,2},{8,13},{9,12},{10,... | collective-permute-start | bytes 26120 | tf_op jit(solution)/shard_map/ppermute | solution.py:589
  24.4 3.1 %collective-permute-start.10 = (f32[1,2176]{1,0:T(1,128)S(1)}, f32[1,2176]{1,0:T(1,128)S(1)}, u32[]{:S(2)}, u32[]{:S(2)}) collective-permute-start(f32[1,2176]{1,0:T(1,128)S(1)} %add_add_fusion), channel_id=1, source_target_pairs={{0,9},{1,8},{2,11},{3,10},{4,13},{5,12},{6,15},{7,14},{8,1},{9,0},... | collective-permute-start | bytes 26120 | tf_op jit(solution)/shard_map/ppermute | solution.py:589

commit v7 on v6

--- a/solution.py
+++ b/solution.py
@@ -477,7 +477,7 @@
     gram[:, body.shape[0] * LANES :] = diagonal
 
 
-def factorize(matrix):
+def factorize(matrix, take):
     size = matrix.shape[0]
     row = row_of((8, LANES))
     tiles = [matrix[t : t + 8] for t in range(0, size, 8)]
@@ -521,7 +521,9 @@
                 for c in range(8):
                     tiles[q] = tiles[q] - columns[q][c] * rows[c]
             columns = {q: columns_of(q, t + 1) for q in range(t + 2, last + 1)}
-    return jnp.concatenate(tiles, axis=0)
+        if t in (last // 2, last):
+            first = 0 if t < last else t // 2 + 1
+            take(8 * first, jnp.concatenate(tiles[first : t + 1], axis=0))
 
 
 def basis_kernel(rank, gram, parts, basis, factor, turned, lower, sems):
@@ -534,28 +536,39 @@
     matrix = unpacked(body, gram[:, lines * LANES :])
     row, lane = row_of(matrix.shape), lane_of(matrix.shape)
     matrix = jnp.where(lane == row + count, 1.0, matrix)
-    done = factorize(matrix)
-    inverse = pltpu.roll(done, count, 1)
-    inverse = jnp.where((lane <= row) & (row < rank[0]), inverse, 0.0)
-    high = inverse.astype(BF16).astype(F32)
-    high, low = (x + pltpu.roll(x, count, 1) for x in (high, inverse - high))
-    left = jnp.concatenate([high, low], axis=0).astype(BF16)
     rows = parts.shape[0]
-    copies = [pltpu.make_async_copy(lower, factor, sems.at[turned.shape[0]])]
-    for c in range(turned.shape[0]):
-        lanes = slice(c * LANES, (c + 1) * LANES)
-        for r in range(rows):
-            part = parts[r, :, lanes]
-            value = dot(left, part)
-            turned[c, pl.ds(r, count, stride=rows), :] = value[:count] + value[count:]
-        copy = pltpu.make_async_copy(turned.at[c], basis.at[:, lanes], sems.at[c])
-        copy.start()
-        copies.append(copy)
-        if c == 0:
-            upper = jnp.where((lane < count) & (lane >= row), done, 0.0)
-            square = jnp.concatenate([upper, jnp.zeros((LANES - count, LANES), F32)], axis=0)
-            lower[...] = square.T[:count, :count]
-            copies[0].start()
+    copies = []
+    finals = []
+
+    def take(at, done):
+        finals.append(done)
+        height = done.shape[0]
+        for copy in copies:
+            copy.start()
+        row, lane = row_of(done.shape) + at, lane_of(done.shape)
+        inverse = pltpu.roll(done, count, 1)
+        inverse = jnp.where((lane <= row) & (row < rank[0]), inverse, 0.0)
+        high = inverse.astype(BF16).astype(F32)
+        high, low = (x + pltpu.roll(x, count, 1) for x in (high, inverse - high))
+        left = jnp.concatenate([high, low], axis=0).astype(BF16)
+        for c in range(turned.shape[0]):
+            lanes = slice(c * LANES, (c + 1) * LANES)
+            for r in range(rows):
+                value = dot(left, parts[r, :, lanes])
+                turned[c, pl.ds(at * rows + r, height, stride=rows), :] = value[:height] + value[height:]
+            cells = slice(at * rows, (at + height) * rows)
+            copies.append(
+                pltpu.make_async_copy(turned.at[c, cells], basis.at[cells, lanes], sems.at[len(copies)])
+            )
+            if at:
+                copies[-1].start()
+
+    factorize(matrix, take)
+    upper = jnp.where((lane < count) & (lane >= row), jnp.concatenate(finals, axis=0), 0.0)
+    square = jnp.concatenate([upper, jnp.zeros((LANES - count, LANES), F32)], axis=0)
+    lower[...] = square.T[:count, :count]
+    copies.append(pltpu.make_async_copy(lower, factor, sems.at[len(copies)]))
+    copies[-1].start()
     for copy in copies:
         copy.wait()
 
@@ -707,7 +720,7 @@
         scratch_shapes=[
             pltpu.VMEM(turned, F32),
             pltpu.VMEM((count, count), F32),
-            pltpu.SemaphoreType.DMA((width // LANES + 1,)),
+            pltpu.SemaphoreType.DMA((2 * width // LANES + 1,)),
         ],
         compiler_params=pltpu.CompilerParams(vmem_limit_bytes=8 * 2**20),
         name="basis",

time: 30.1 us -> 30.1 us (level)
  no operation moved by 1% of the time
where the time goes in v7:
time: 30.1 us; the launch traced here: 29.9 us
  starting transfers between devices  14.7 us (49%)
  waiting for transfers between devices  6.93 us (23%)
  Pallas kernels  6.85 us (23%)
  between operations  1.38 us (5%)
    ppermute x5, starting transfers between devices, summed(): lax.ppermute(x, ('mesh', 'obs'), [(i * columns + c, (i ^ offset) * column...  10.3 us
    pallas_call x8, Pallas kernels, call(): pl.pallas_call(body, out_shape=outs, in_specs=[pl.BlockSpec(memory_space=...  4.49 us
    ppermute x5, waiting for transfers between devices, summed(): lax.ppermute(x, ('mesh', 'obs'), [(i * columns + c, (i ^ offset) * column...  4.38 us
    ppermute x2, starting transfers between devices, exchanged(): return lax.ppermute(x, ('mesh', 'obs'), pairs)  3.01 us
    ppermute x4, waiting for transfers between devices, ring(): return lax.ppermute(x, axis, [(i, (i + step) % size) for i in range(size)])  2.54 us
    pallas_call x1, Pallas kernels, per_device(): pl.pallas_call(basis_kernel, out_shape=[jax.ShapeDtypeStruct((count * row...  2.36 us
    ppermute x4, starting transfers between devices, ring(): return lax.ppermute(x, axis, [(i, (i + step) % size) for i in range(size)])  1.44 us
  transfers between devices with their start and end apart: 11, of which 9 were waited for; matrix products, arithmetic and copies ran while one was open for 0% of the time, Pallas kernels for 8%

profile of v7, /device:TPU:0, one launch (start us, length us, event | category | flops | bytes accessed | tf_op | source)
XLA Modules:
  0.0 29.9 jit_solution(12890156249336329700)
XLA Ops:
  0.6 1.1 %edges.1 = (f32[2,512,128]{2,1,0:T(8,128)S(1)}, bf16[176,256]{1,0:T(8,128)(2,1)S(1)}, bf16[176,256]{1,0:T(8,128)(2,1)S(1)}, f32[3,8,256]{2,1,0:T(8,128)S(1)}, f32[72,128]{1,0:T(8,128)S(1)}) custom-call(bf16[64,8,256]{2,1,0:T(8,128)(2,1)} %probes.1, f32[8,256]{1,0:T(8,128)} %velocity.1, f32[8,256]{1,0:T(8,128)} %viscosity.1, f32[8,256]{1,0:T(8,128)} %friction.1, ...), custom_call_target="tpu_custom_call" | custom-call | bytes 1048576 | tf_op jit(solution)/shard_map/edges/pallas_call | solution.py:40
  1.8 3.0 %collective-permute-start = (bf16[176,256]{1,0:T(8,128)(2,1)S(1)}, bf16[176,256]{1,0:T(8,128)(2,1)S(1)}, u32[]{:S(2)}, u32[]{:S(2)}) collective-permute-start(bf16[176,256]{1,0:T(8,128)(2,1)S(1)} %get-tuple-element.24), channel_id=1, source_target_pairs={{0,2},{1,3},{2,0},{3,1},{4,6},{5,7},{6,4},{7,5},{8,10},{9,11},{10,... | collective-permute-start | bytes 270344 | tf_op jit(solution)/shard_map/ppermute | solution.py:589
  4.8 0.0 collective-permute-start.1
  4.8 0.3 forced.1
  5.0 0.6 %collective-permute-start.2 = (f32[144,128]{1,0:T(8,128)S(1)}, f32[144,128]{1,0:T(8,128)S(1)}, u32[]{:S(2)}, u32[]{:S(2)}) collective-permute-start(f32[144,128]{1,0:T(8,128)S(1)} %get-tuple-element.26.rest_0_), channel_id=1, source_target_pairs={{0,1},{1,0},{2,3},{3,2},{4,5},{5,4},{6,7},{7,6},{8,9},{9,8},{10,11... | collective-permute-start | bytes 221192 | tf_op jit(solution)/shard_map/ppermute | solution.py:578
  5.6 0.9 %collective-permute-done.2.from_left.from_right.rest_1_.visc_left.visc_right = f32[144,128]{1,0:T(8,128)S(1)} collective-permute-done((f32[144,128]{1,0:T(8,128)S(1)}, f32[144,128]{1,0:T(8,128)S(1)}, u32[]{:S(2)}, u32[]{:S(2)}) %collective-permute-start.2) | collective-permute-done | bytes 73760 | tf_op jit(solution)/shard_map/ppermute | solution.py:578
  6.5 0.8 %inner.1 = (f32[384,256]{1,0:T(8,128)S(1)}, f32[64,128]{1,0:T(8,128)S(1)}) custom-call(f32[8,72,256]{2,1,0:T(8,128)S(1)} %get-tuple-element.23.forced, f32[3,8,256]{2,1,0:T(8,128)S(1)} %get-tuple-element.21.grid, f32[144,128]{1,0:T(8,128)S(1)} %collective-permute-done.2.from_left.from_right.rest_1_.visc_left.visc_right, ...), custom_call_target="tpu_custom_call" | custom-call | bytes 1048576 | tf_op jit(solution)/shard_map/inner/pallas_call | solution.py:40
  7.3 0.4 %middle.1.early = f32[384,256]{1,0:T(8,128)S(1)} custom-call(f32[8,72,256]{2,1,0:T(8,128)S(1)} %get-tuple-element.23.forced, f32[2,512,128]{2,1,0:T(8,128)S(1)} %get-tuple-element.20.omega, f32[3,8,256]{2,1,0:T(8,128)S(1)} %get-tuple-element.21.grid, f32[144,128]{1,0:T(8,128)S(1)} %collective-permute-done.2.from_left.from_right.rest_1_.visc_left.visc_right, ...), custom_call_target="tpu_custom_call" | custom-call | bytes 1048576 | tf_op jit(solution)/shard_map/middle/pallas_call | solution.py:40
  7.8 0.0 collective-permute-done.first.first_in
  7.8 0.0 collective-permute-done.1.second.second_in
  7.8 0.1 far.1
  8.0 0.4 %collective-permute-start.4 = (f32[216,128]{1,0:T(8,128)S(1)}, f32[216,128]{1,0:T(8,128)S(1)}, u32[]{:S(2)}, u32[]{:S(2)}) collective-permute-start(f32[216,128]{1,0:T(8,128)S(1)} %get-tuple-element.33.rest_0_), channel_id=1, source_target_pairs={{0,1},{1,0},{2,3},{3,2},{4,5},{5,4},{6,7},{7,6},{8,9},{9,8},{10,11... | collective-permute-start | bytes 331784 | tf_op jit(solution)/shard_map/ppermute | solution.py:578
  8.4 0.5 %outer.1 = (f32[128,256]{1,0:T(8,128)S(1)}, f32[64,128]{1,0:T(8,128)S(1)}, f32[128,256]{1,0:T(8,128)S(1)}) custom-call(f32[8,72,256]{2,1,0:T(8,128)S(1)} %get-tuple-element.23.forced, f32[2,72,256]{2,1,0:T(8,128)S(1)} %get-tuple-element.28.near, f32[3,8,256]{2,1,0:T(8,128)S(1)} %get-tuple-element.21.grid, ...), custom_call_target="tpu_custom_call" | custom-call | bytes 1048576 | tf_op jit(solution)/shard_map/outer/pallas_call | solution.py:40
  8.9 0.2 collective-permute-start.3
  9.1 0.2 collective-permute-done.4.from_left.from_right.rest_1_
  9.3 0.4 %halo.1 = f32[128,256]{1,0:T(8,128)S(1)} custom-call(f32[2,72,256]{2,1,0:T(8,128)S(1)} %get-tuple-element.28.near, f32[128,256]{1,0:T(8,128)S(1)} %get-tuple-element.32.beside, f32[216,128]{1,0:T(8,128)S(1)} %collective-permute-done.4.from_left.from_right.rest_1_, f32[216,128]{1,0:T(8,128)S(1)} %collective-permute-done.4.from_left.from_right.rest_1_, ...), custom_call_target="tpu_custom_call" | custom-call | bytes 1048576 | tf_op jit(solution)/shard_map/halo/pallas_call | solution.py:40
  9.8 0.4 %collective-permute-done.3.from_left.from_right = f32[64,128]{1,0:T(8,128)S(1)} collective-permute-done((f32[64,128]{1,0:T(8,128)S(1)}, f32[64,128]{1,0:T(8,128)S(1)}, u32[]{:S(2)}, u32[]{:S(2)}) %collective-permute-start.3) | collective-permute-done | bytes 32800 | tf_op jit(solution)/shard_map/ppermute | solution.py:578
  10.2 0.8 %sketch.1 = (bf16[8,128,256]{2,1,0:T(8,128)(2,1)S(1)}, f32[1,2176]{1,0:T(1,128)S(1)}) custom-call(f32[8,72,256]{2,1,0:T(8,128)S(1)} %get-tuple-element.23.forced, f32[2,72,256]{2,1,0:T(8,128)S(1)} %get-tuple-element.28.near, f32[2,512,128]{2,1,0:T(8,128)S(1)} %get-tuple-element.20.omega, f32[3,8,256]{2,1,0:T(8,128)S(1)} %get-tuple-element.21.grid, ...), custom_call_target="tpu_custom_call" | custom-call | bytes 1048576 | tf_op jit(solution)/shard_map/sketch/pallas_call | solution.py:40
  11.0 0.2 collective-permute-start.5
  11.2 1.0 %collective-permute-done.5 = f32[1,2176]{1,0:T(1,128)S(1)} collective-permute-done((f32[1,2176]{1,0:T(1,128)S(1)}, f32[1,2176]{1,0:T(1,128)S(1)}, u32[]{:S(2)}, u32[]{:S(2)}) %collective-permute-start.5) | collective-permute-done | bytes 8736 | tf_op jit(solution)/shard_map/ppermute | solution.py:578
  12.2 5.7 %collective-permute-start.6 = (f32[1,2176]{1,0:T(1,128)S(1)}, f32[1,2176]{1,0:T(1,128)S(1)}, u32[]{:S(2)}, u32[]{:S(2)}) collective-permute-start(f32[1,2176]{1,0:T(1,128)S(1)} %add.18), channel_id=1, source_target_pairs={{0,17},{1,16},{2,19},{3,18},{4,21},{5,20},{6,23},{7,22},{8,25},{9,... | collective-permute-start | bytes 26120 | tf_op jit(solution)/shard_map/ppermute | solution.py:602
  17.9 1.4 %collective-permute-done.6 = f32[1,2176]{1,0:T(1,128)S(1)} collective-permute-done((f32[1,2176]{1,0:T(1,128)S(1)}, f32[1,2176]{1,0:T(1,128)S(1)}, u32[]{:S(2)}, u32[]{:S(2)}) %collective-permute-start.6) | collective-permute-done | bytes 8736 | tf_op jit(solution)/shard_map/ppermute | solution.py:602
  19.3 1.0 %collective-permute-start.7 = (f32[1,2176]{1,0:T(1,128)S(1)}, f32[1,2176]{1,0:T(1,128)S(1)}, u32[]{:S(2)}, u32[]{:S(2)}) collective-permute-start(f32[1,2176]{1,0:T(1,128)S(1)} %add.19), channel_id=1, source_target_pairs={{0,3},{1,2},{2,1},{3,0},{4,7},{5,6},{6,5},{7,4},{8,11},{9,10},{10,... | collective-permute-start | bytes 26120 | tf_op jit(solution)/shard_map/ppermute | solution.py:602
  20.3 0.9 %collective-permute-start.8 = (f32[1,2176]{1,0:T(1,128)S(1)}, f32[1,2176]{1,0:T(1,128)S(1)}, u32[]{:S(2)}, u32[]{:S(2)}) collective-permute-start(f32[1,2176]{1,0:T(1,128)S(1)} %add.19), channel_id=1, source_target_pairs={{0,7},{1,6},{2,5},{3,4},{4,3},{5,2},{6,1},{7,0},{8,15},{9,14},{10,... | collective-permute-start | bytes 26120 | tf_op jit(solution)/shard_map/ppermute | solution.py:602
  21.2 1.1 %collective-permute-start.9 = (f32[1,2176]{1,0:T(1,128)S(1)}, f32[1,2176]{1,0:T(1,128)S(1)}, u32[]{:S(2)}, u32[]{:S(2)}) collective-permute-start(f32[1,2176]{1,0:T(1,128)S(1)} %add.19), channel_id=1, source_target_pairs={{0,5},{1,4},{2,7},{3,6},{4,1},{5,0},{6,3},{7,2},{8,13},{9,12},{10,... | collective-permute-start | bytes 26120 | tf_op jit(solution)/shard_map/ppermute | solution.py:602
  22.3 0.1 collective-permute-done.7
  22.4 1.8 %collective-permute-done.8 = f32[1,2176]{1,0:T(1,128)S(1)} collective-permute-done((f32[1,2176]{1,0:T(1,128)S(1)}, f32[1,2176]{1,0:T(1,128)S(1)}, u32[]{:S(2)}, u32[]{:S(2)}) %collective-permute-start.8) | collective-permute-done | bytes 8736 | tf_op jit(solution)/shard_map/ppermute | solution.py:602
  24.3 0.1 collective-permute-done.9
  24.4 1.5 %collective-permute-start.10 = (f32[1,2176]{1,0:T(1,128)S(1)}, f32[1,2176]{1,0:T(1,128)S(1)}, u32[]{:S(2)}, u32[]{:S(2)}) collective-permute-start(f32[1,2176]{1,0:T(1,128)S(1)} %add_add_fusion), channel_id=1, source_target_pairs={{0,9},{1,8},{2,11},{3,10},{4,13},{5,12},{6,15},{7,14},{8,1},{9,0},... | collective-permute-start | bytes 26120 | tf_op jit(solution)/shard_map/ppermute | solution.py:602
  26.6 1.0 %collective-permute-done.10 = f32[1,2176]{1,0:T(1,128)S(1)} collective-permute-done((f32[1,2176]{1,0:T(1,128)S(1)}, f32[1,2176]{1,0:T(1,128)S(1)}, u32[]{:S(2)}, u32[]{:S(2)}) %collective-permute-start.10) | collective-permute-done | bytes 8736 | tf_op jit(solution)/shard_map/ppermute | solution.py:602
  27.5 2.4 %basis.1 = (f32[512,256]{1,0:T(8,128)}, f32[64,64]{1,0:T(8,128)}) custom-call(s32[1]{0:T(128)S(6)} %copy.10.rank, f32[1,2176]{1,0:T(1,128)S(1)} %add.23.gram, bf16[8,128,256]{2,1,0:T(8,128)(2,1)S(1)} %get-tuple-element.35.parts), custom_call_target="tpu_custom_call" | custom-call | tf_op jit(solution)/shard_map/basis/pallas_call | solution.py:712
  (4 shorter events, 0.0 us)
Async XLA Ops:
  1.8 6.0 %collective-permute-start = (bf16[176,256]{1,0:T(8,128)(2,1)S(1)}, bf16[176,256]{1,0:T(8,128)(2,1)S(1)}, u32[]{:S(2)}, u32[]{:S(2)}) collective-permute-start(bf16[176,256]{1,0:T(8,128)(2,1)S(1)} %get-tuple-element.24), channel_id=1, source_target_pairs={{0,2},{1,3},{2,0},{3,1},{4,6},{5,7},{6,4},{7,5},{8,10},{9,11},{10,... | collective-permute-start | bytes 270344 | tf_op jit(solution)/shard_map/ppermute | solution.py:589
  4.8 3.0 %collective-permute-start.1 = (bf16[176,256]{1,0:T(8,128)(2,1)S(1)}, bf16[176,256]{1,0:T(8,128)(2,1)S(1)}, u32[]{:S(2)}, u32[]{:S(2)}) collective-permute-start(bf16[176,256]{1,0:T(8,128)(2,1)S(1)} %get-tuple-element.25), channel_id=1, source_target_pairs={{0,1},{1,0},{2,4},{3,5},{4,2},{5,3},{6,8},{7,9},{8,6},{9,7},{10,12... | collective-permute-start | bytes 270344 | tf_op jit(solution)/shard_map/ppermute | solution.py:589
  5.0 1.5 %collective-permute-start.2 = (f32[144,128]{1,0:T(8,128)S(1)}, f32[144,128]{1,0:T(8,128)S(1)}, u32[]{:S(2)}, u32[]{:S(2)}) collective-permute-start(f32[144,128]{1,0:T(8,128)S(1)} %get-tuple-element.26.rest_0_), channel_id=1, source_target_pairs={{0,1},{1,0},{2,3},{3,2},{4,5},{5,4},{6,7},{7,6},{8,9},{9,8},{10,11... | collective-permute-start | bytes 221192 | tf_op jit(solution)/shard_map/ppermute | solution.py:578
  8.0 1.4 %collective-permute-start.4 = (f32[216,128]{1,0:T(8,128)S(1)}, f32[216,128]{1,0:T(8,128)S(1)}, u32[]{:S(2)}, u32[]{:S(2)}) collective-permute-start(f32[216,128]{1,0:T(8,128)S(1)} %get-tuple-element.33.rest_0_), channel_id=1, source_target_pairs={{0,1},{1,0},{2,3},{3,2},{4,5},{5,4},{6,7},{7,6},{8,9},{9,8},{10,11... | collective-permute-start | bytes 331784 | tf_op jit(solution)/shard_map/ppermute | solution.py:578
  8.9 1.3 %collective-permute-start.3 = (f32[64,128]{1,0:T(8,128)S(1)}, f32[64,128]{1,0:T(8,128)S(1)}, u32[]{:S(2)}, u32[]{:S(2)}) collective-permute-start(f32[64,128]{1,0:T(8,128)S(1)} %get-tuple-element.30), channel_id=1, source_target_pairs={{0,1},{1,0},{2,3},{3,2},{4,5},{5,4},{6,7},{7,6},{8,9},{9,8},{10,11... | collective-permute-start | bytes 98312 | tf_op jit(solution)/shard_map/ppermute | solution.py:578
  11.0 1.2 %collective-permute-start.5 = (f32[1,2176]{1,0:T(1,128)S(1)}, f32[1,2176]{1,0:T(1,128)S(1)}, u32[]{:S(2)}, u32[]{:S(2)}) collective-permute-start(f32[1,2176]{1,0:T(1,128)S(1)} %get-tuple-element.34), channel_id=1, source_target_pairs={{0,1},{1,0},{2,3},{3,2},{4,5},{5,4},{6,7},{7,6},{8,9},{9,8},{10,11... | collective-permute-start | bytes 26120 | tf_op jit(solution)/shard_map/ppermute | solution.py:578
  12.2 7.1 %collective-permute-start.6 = (f32[1,2176]{1,0:T(1,128)S(1)}, f32[1,2176]{1,0:T(1,128)S(1)}, u32[]{:S(2)}, u32[]{:S(2)}) collective-permute-start(f32[1,2176]{1,0:T(1,128)S(1)} %add.18), channel_id=1, source_target_pairs={{0,17},{1,16},{2,19},{3,18},{4,21},{5,20},{6,23},{7,22},{8,25},{9,... | collective-permute-start | bytes 26120 | tf_op jit(solution)/shard_map/ppermute | solution.py:602
  19.3 3.1 %collective-permute-start.7 = (f32[1,2176]{1,0:T(1,128)S(1)}, f32[1,2176]{1,0:T(1,128)S(1)}, u32[]{:S(2)}, u32[]{:S(2)}) collective-permute-start(f32[1,2176]{1,0:T(1,128)S(1)} %add.19), channel_id=1, source_target_pairs={{0,3},{1,2},{2,1},{3,0},{4,7},{5,6},{6,5},{7,4},{8,11},{9,10},{10,... | collective-permute-start | bytes 26120 | tf_op jit(solution)/shard_map/ppermute | solution.py:602
  20.3 4.0 %collective-permute-start.8 = (f32[1,2176]{1,0:T(1,128)S(1)}, f32[1,2176]{1,0:T(1,128)S(1)}, u32[]{:S(2)}, u32[]{:S(2)}) collective-permute-start(f32[1,2176]{1,0:T(1,128)S(1)} %add.19), channel_id=1, source_target_pairs={{0,7},{1,6},{2,5},{3,4},{4,3},{5,2},{6,1},{7,0},{8,15},{9,14},{10,... | collective-permute-start | bytes 26120 | tf_op jit(solution)/shard_map/ppermute | solution.py:602
  21.2 3.1 %collective-permute-start.9 = (f32[1,2176]{1,0:T(1,128)S(1)}, f32[1,2176]{1,0:T(1,128)S(1)}, u32[]{:S(2)}, u32[]{:S(2)}) collective-permute-start(f32[1,2176]{1,0:T(1,128)S(1)} %add.19), channel_id=1, source_target_pairs={{0,5},{1,4},{2,7},{3,6},{4,1},{5,0},{6,3},{7,2},{8,13},{9,12},{10,... | collective-permute-start | bytes 26120 | tf_op jit(solution)/shard_map/ppermute | solution.py:602
  24.4 3.1 %collective-permute-start.10 = (f32[1,2176]{1,0:T(1,128)S(1)}, f32[1,2176]{1,0:T(1,128)S(1)}, u32[]{:S(2)}, u32[]{:S(2)}) collective-permute-start(f32[1,2176]{1,0:T(1,128)S(1)} %add_add_fusion), channel_id=1, source_target_pairs={{0,9},{1,8},{2,11},{3,10},{4,13},{5,12},{6,15},{7,14},{8,1},{9,0},... | collective-permute-start | bytes 26120 | tf_op jit(solution)/shard_map/ppermute | solution.py:602

commit v8 on v6

--- a/solution.py
+++ b/solution.py
@@ -581,9 +581,9 @@
     x = x + ring(x, "obs", 1) if columns == 2 else lax.psum(x, "obs")
     if rows & (rows - 1):
         return lax.psum(x, "mesh")
-    rounds = [(1 << bit,) for bit in range(rows.bit_length() - 2, 2, -1)]
+    rounds = [(4,)] if rows > 4 else []
     rounds += [(1, 3, 2) if rows > 2 else (1,)] if rows > 1 else []
-    rounds += [(4,)] if rows > 4 else []
+    rounds += [(1 << bit,) for bit in range(3, rows.bit_length() - 1)]
     for offsets in rounds:
         pieces = [
             lax.ppermute(

time: 30.1 us -> 30.1 us (level)
  no operation moved by 1% of the time
where the time goes in v8:
time: 30.1 us; the launch traced here: 30 us
  starting transfers between devices  14.7 us (49%)
  waiting for transfers between devices  6.93 us (23%)
  Pallas kernels  6.91 us (23%)
  between operations  1.38 us (5%)
    ppermute x5, starting transfers between devices, summed(): lax.ppermute(x, ('mesh', 'obs'), [(i * columns + c, (i ^ offset) * column...  10.3 us
    pallas_call x8, Pallas kernels, call(): pl.pallas_call(body, out_shape=outs, in_specs=[pl.BlockSpec(memory_space=...  4.49 us
    ppermute x5, waiting for transfers between devices, summed(): lax.ppermute(x, ('mesh', 'obs'), [(i * columns + c, (i ^ offset) * column...  4.38 us
    ppermute x2, starting transfers between devices, exchanged(): return lax.ppermute(x, ('mesh', 'obs'), pairs)  3.01 us
    ppermute x4, waiting for transfers between devices, ring(): return lax.ppermute(x, axis, [(i, (i + step) % size) for i in range(size)])  2.54 us
    pallas_call x1, Pallas kernels, per_device(): pl.pallas_call(basis_kernel, out_shape=[jax.ShapeDtypeStruct((count * row...  2.42 us
    ppermute x4, starting transfers between devices, ring(): return lax.ppermute(x, axis, [(i, (i + step) % size) for i in range(size)])  1.44 us
  transfers between devices with their start and end apart: 11, of which 9 were waited for; matrix products, arithmetic and copies ran while one was open for 0% of the time, Pallas kernels for 8%

profile of v8, /device:TPU:0, one launch (start us, length us, event | category | flops | bytes accessed | tf_op | source)
XLA Modules:
  0.0 30.0 jit_solution(2610138147336314713)
XLA Ops:
  0.6 1.1 %edges.1 = (f32[2,512,128]{2,1,0:T(8,128)S(1)}, bf16[176,256]{1,0:T(8,128)(2,1)S(1)}, bf16[176,256]{1,0:T(8,128)(2,1)S(1)}, f32[3,8,256]{2,1,0:T(8,128)S(1)}, f32[72,128]{1,0:T(8,128)S(1)}) custom-call(bf16[64,8,256]{2,1,0:T(8,128)(2,1)} %probes.1, f32[8,256]{1,0:T(8,128)} %velocity.1, f32[8,256]{1,0:T(8,128)} %viscosity.1, f32[8,256]{1,0:T(8,128)} %friction.1, ...), custom_call_target="tpu_custom_call" | custom-call | bytes 1048576 | tf_op jit(solution)/shard_map/edges/pallas_call | solution.py:40
  1.8 3.0 %collective-permute-start = (bf16[176,256]{1,0:T(8,128)(2,1)S(1)}, bf16[176,256]{1,0:T(8,128)(2,1)S(1)}, u32[]{:S(2)}, u32[]{:S(2)}) collective-permute-start(bf16[176,256]{1,0:T(8,128)(2,1)S(1)} %get-tuple-element.24), channel_id=1, source_target_pairs={{0,2},{1,3},{2,0},{3,1},{4,6},{5,7},{6,4},{7,5},{8,10},{9,11},{10,... | collective-permute-start | bytes 270344 | tf_op jit(solution)/shard_map/ppermute | solution.py:576
  4.8 0.0 collective-permute-start.1
  4.8 0.3 forced.1
  5.0 0.6 %collective-permute-start.2 = (f32[144,128]{1,0:T(8,128)S(1)}, f32[144,128]{1,0:T(8,128)S(1)}, u32[]{:S(2)}, u32[]{:S(2)}) collective-permute-start(f32[144,128]{1,0:T(8,128)S(1)} %get-tuple-element.26.rest_0_), channel_id=1, source_target_pairs={{0,1},{1,0},{2,3},{3,2},{4,5},{5,4},{6,7},{7,6},{8,9},{9,8},{10,11... | collective-permute-start | bytes 221192 | tf_op jit(solution)/shard_map/ppermute | solution.py:565
  5.6 0.9 %collective-permute-done.2.from_left.from_right.rest_1_.visc_left.visc_right = f32[144,128]{1,0:T(8,128)S(1)} collective-permute-done((f32[144,128]{1,0:T(8,128)S(1)}, f32[144,128]{1,0:T(8,128)S(1)}, u32[]{:S(2)}, u32[]{:S(2)}) %collective-permute-start.2) | collective-permute-done | bytes 73760 | tf_op jit(solution)/shard_map/ppermute | solution.py:565
  6.5 0.8 %inner.1 = (f32[384,256]{1,0:T(8,128)S(1)}, f32[64,128]{1,0:T(8,128)S(1)}) custom-call(f32[8,72,256]{2,1,0:T(8,128)S(1)} %get-tuple-element.23.forced, f32[3,8,256]{2,1,0:T(8,128)S(1)} %get-tuple-element.21.grid, f32[144,128]{1,0:T(8,128)S(1)} %collective-permute-done.2.from_left.from_right.rest_1_.visc_left.visc_right, ...), custom_call_target="tpu_custom_call" | custom-call | bytes 1048576 | tf_op jit(solution)/shard_map/inner/pallas_call | solution.py:40
  7.3 0.4 %middle.1.early = f32[384,256]{1,0:T(8,128)S(1)} custom-call(f32[8,72,256]{2,1,0:T(8,128)S(1)} %get-tuple-element.23.forced, f32[2,512,128]{2,1,0:T(8,128)S(1)} %get-tuple-element.20.omega, f32[3,8,256]{2,1,0:T(8,128)S(1)} %get-tuple-element.21.grid, f32[144,128]{1,0:T(8,128)S(1)} %collective-permute-done.2.from_left.from_right.rest_1_.visc_left.visc_right, ...), custom_call_target="tpu_custom_call" | custom-call | bytes 1048576 | tf_op jit(solution)/shard_map/middle/pallas_call | solution.py:40
  7.8 0.0 collective-permute-done.first.first_in
  7.8 0.0 collective-permute-done.1.second.second_in
  7.8 0.1 far.1
  8.0 0.4 %collective-permute-start.4 = (f32[216,128]{1,0:T(8,128)S(1)}, f32[216,128]{1,0:T(8,128)S(1)}, u32[]{:S(2)}, u32[]{:S(2)}) collective-permute-start(f32[216,128]{1,0:T(8,128)S(1)} %get-tuple-element.33.rest_0_), channel_id=1, source_target_pairs={{0,1},{1,0},{2,3},{3,2},{4,5},{5,4},{6,7},{7,6},{8,9},{9,8},{10,11... | collective-permute-start | bytes 331784 | tf_op jit(solution)/shard_map/ppermute | solution.py:565
  8.4 0.5 %outer.1 = (f32[128,256]{1,0:T(8,128)S(1)}, f32[64,128]{1,0:T(8,128)S(1)}, f32[128,256]{1,0:T(8,128)S(1)}) custom-call(f32[8,72,256]{2,1,0:T(8,128)S(1)} %get-tuple-element.23.forced, f32[2,72,256]{2,1,0:T(8,128)S(1)} %get-tuple-element.28.near, f32[3,8,256]{2,1,0:T(8,128)S(1)} %get-tuple-element.21.grid, ...), custom_call_target="tpu_custom_call" | custom-call | bytes 1048576 | tf_op jit(solution)/shard_map/outer/pallas_call | solution.py:40
  8.9 0.2 collective-permute-start.3
  9.1 0.2 collective-permute-done.4.from_left.from_right.rest_1_
  9.3 0.4 %halo.1 = f32[128,256]{1,0:T(8,128)S(1)} custom-call(f32[2,72,256]{2,1,0:T(8,128)S(1)} %get-tuple-element.28.near, f32[128,256]{1,0:T(8,128)S(1)} %get-tuple-element.32.beside, f32[216,128]{1,0:T(8,128)S(1)} %collective-permute-done.4.from_left.from_right.rest_1_, f32[216,128]{1,0:T(8,128)S(1)} %collective-permute-done.4.from_left.from_right.rest_1_, ...), custom_call_target="tpu_custom_call" | custom-call | bytes 1048576 | tf_op jit(solution)/shard_map/halo/pallas_call | solution.py:40
  9.8 0.4 %collective-permute-done.3.from_left.from_right = f32[64,128]{1,0:T(8,128)S(1)} collective-permute-done((f32[64,128]{1,0:T(8,128)S(1)}, f32[64,128]{1,0:T(8,128)S(1)}, u32[]{:S(2)}, u32[]{:S(2)}) %collective-permute-start.3) | collective-permute-done | bytes 32800 | tf_op jit(solution)/shard_map/ppermute | solution.py:565
  10.2 0.8 %sketch.1 = (bf16[8,128,256]{2,1,0:T(8,128)(2,1)S(1)}, f32[1,2176]{1,0:T(1,128)S(1)}) custom-call(f32[8,72,256]{2,1,0:T(8,128)S(1)} %get-tuple-element.23.forced, f32[2,72,256]{2,1,0:T(8,128)S(1)} %get-tuple-element.28.near, f32[2,512,128]{2,1,0:T(8,128)S(1)} %get-tuple-element.20.omega, f32[3,8,256]{2,1,0:T(8,128)S(1)} %get-tuple-element.21.grid, ...), custom_call_target="tpu_custom_call" | custom-call | bytes 1048576 | tf_op jit(solution)/shard_map/sketch/pallas_call | solution.py:40
  11.0 0.2 collective-permute-start.5
  11.2 1.0 %collective-permute-done.5 = f32[1,2176]{1,0:T(1,128)S(1)} collective-permute-done((f32[1,2176]{1,0:T(1,128)S(1)}, f32[1,2176]{1,0:T(1,128)S(1)}, u32[]{:S(2)}, u32[]{:S(2)}) %collective-permute-start.5) | collective-permute-done | bytes 8736 | tf_op jit(solution)/shard_map/ppermute | solution.py:565
  12.2 4.7 %collective-permute-start.6 = (f32[1,2176]{1,0:T(1,128)S(1)}, f32[1,2176]{1,0:T(1,128)S(1)}, u32[]{:S(2)}, u32[]{:S(2)}) collective-permute-start(f32[1,2176]{1,0:T(1,128)S(1)} %add.18), channel_id=1, source_target_pairs={{0,9},{1,8},{2,11},{3,10},{4,13},{5,12},{6,15},{7,14},{8,1},{9,0},... | collective-permute-start | bytes 26120 | tf_op jit(solution)/shard_map/ppermute | solution.py:589
  16.9 1.4 %collective-permute-done.6 = f32[1,2176]{1,0:T(1,128)S(1)} collective-permute-done((f32[1,2176]{1,0:T(1,128)S(1)}, f32[1,2176]{1,0:T(1,128)S(1)}, u32[]{:S(2)}, u32[]{:S(2)}) %collective-permute-start.6) | collective-permute-done | bytes 8736 | tf_op jit(solution)/shard_map/ppermute | solution.py:589
  18.3 1.1 %collective-permute-start.7 = (f32[1,2176]{1,0:T(1,128)S(1)}, f32[1,2176]{1,0:T(1,128)S(1)}, u32[]{:S(2)}, u32[]{:S(2)}) collective-permute-start(f32[1,2176]{1,0:T(1,128)S(1)} %add.19), channel_id=1, source_target_pairs={{0,3},{1,2},{2,1},{3,0},{4,7},{5,6},{6,5},{7,4},{8,11},{9,10},{10,... | collective-permute-start | bytes 26120 | tf_op jit(solution)/shard_map/ppermute | solution.py:589
  19.4 0.9 %collective-permute-start.8 = (f32[1,2176]{1,0:T(1,128)S(1)}, f32[1,2176]{1,0:T(1,128)S(1)}, u32[]{:S(2)}, u32[]{:S(2)}) collective-permute-start(f32[1,2176]{1,0:T(1,128)S(1)} %add.19), channel_id=1, source_target_pairs={{0,7},{1,6},{2,5},{3,4},{4,3},{5,2},{6,1},{7,0},{8,15},{9,14},{10,... | collective-permute-start | bytes 26120 | tf_op jit(solution)/shard_map/ppermute | solution.py:589
  20.3 1.0 %collective-permute-start.9 = (f32[1,2176]{1,0:T(1,128)S(1)}, f32[1,2176]{1,0:T(1,128)S(1)}, u32[]{:S(2)}, u32[]{:S(2)}) collective-permute-start(f32[1,2176]{1,0:T(1,128)S(1)} %add.19), channel_id=1, source_target_pairs={{0,5},{1,4},{2,7},{3,6},{4,1},{5,0},{6,3},{7,2},{8,13},{9,12},{10,... | collective-permute-start | bytes 26120 | tf_op jit(solution)/shard_map/ppermute | solution.py:589
  21.3 0.1 collective-permute-done.7
  21.4 2.0 %collective-permute-done.8 = f32[1,2176]{1,0:T(1,128)S(1)} collective-permute-done((f32[1,2176]{1,0:T(1,128)S(1)}, f32[1,2176]{1,0:T(1,128)S(1)}, u32[]{:S(2)}, u32[]{:S(2)}) %collective-permute-start.8) | collective-permute-done | bytes 8736 | tf_op jit(solution)/shard_map/ppermute | solution.py:589
  23.4 0.1 collective-permute-done.9
  23.5 2.5 %collective-permute-start.10 = (f32[1,2176]{1,0:T(1,128)S(1)}, f32[1,2176]{1,0:T(1,128)S(1)}, u32[]{:S(2)}, u32[]{:S(2)}) collective-permute-start(f32[1,2176]{1,0:T(1,128)S(1)} %add_add_fusion), channel_id=1, source_target_pairs={{0,17},{1,16},{2,19},{3,18},{4,21},{5,20},{6,23},{7,22},{8,25},{9,... | collective-permute-start | bytes 26120 | tf_op jit(solution)/shard_map/ppermute | solution.py:589
  26.7 0.8 %collective-permute-done.10 = f32[1,2176]{1,0:T(1,128)S(1)} collective-permute-done((f32[1,2176]{1,0:T(1,128)S(1)}, f32[1,2176]{1,0:T(1,128)S(1)}, u32[]{:S(2)}, u32[]{:S(2)}) %collective-permute-start.10) | collective-permute-done | bytes 8736 | tf_op jit(solution)/shard_map/ppermute | solution.py:589
  27.5 2.4 %basis.1 = (f32[512,256]{1,0:T(8,128)}, f32[64,64]{1,0:T(8,128)}) custom-call(s32[1]{0:T(128)S(6)} %copy.10.rank, f32[1,2176]{1,0:T(1,128)S(1)} %add.23.gram, bf16[8,128,256]{2,1,0:T(8,128)(2,1)S(1)} %get-tuple-element.35.parts), custom_call_target="tpu_custom_call" | custom-call | tf_op jit(solution)/shard_map/basis/pallas_call | solution.py:699
  (4 shorter events, 0.0 us)
Async XLA Ops:
  1.8 6.0 %collective-permute-start = (bf16[176,256]{1,0:T(8,128)(2,1)S(1)}, bf16[176,256]{1,0:T(8,128)(2,1)S(1)}, u32[]{:S(2)}, u32[]{:S(2)}) collective-permute-start(bf16[176,256]{1,0:T(8,128)(2,1)S(1)} %get-tuple-element.24), channel_id=1, source_target_pairs={{0,2},{1,3},{2,0},{3,1},{4,6},{5,7},{6,4},{7,5},{8,10},{9,11},{10,... | collective-permute-start | bytes 270344 | tf_op jit(solution)/shard_map/ppermute | solution.py:576
  4.8 3.0 %collective-permute-start.1 = (bf16[176,256]{1,0:T(8,128)(2,1)S(1)}, bf16[176,256]{1,0:T(8,128)(2,1)S(1)}, u32[]{:S(2)}, u32[]{:S(2)}) collective-permute-start(bf16[176,256]{1,0:T(8,128)(2,1)S(1)} %get-tuple-element.25), channel_id=1, source_target_pairs={{0,1},{1,0},{2,4},{3,5},{4,2},{5,3},{6,8},{7,9},{8,6},{9,7},{10,12... | collective-permute-start | bytes 270344 | tf_op jit(solution)/shard_map/ppermute | solution.py:576
  5.0 1.5 %collective-permute-start.2 = (f32[144,128]{1,0:T(8,128)S(1)}, f32[144,128]{1,0:T(8,128)S(1)}, u32[]{:S(2)}, u32[]{:S(2)}) collective-permute-start(f32[144,128]{1,0:T(8,128)S(1)} %get-tuple-element.26.rest_0_), channel_id=1, source_target_pairs={{0,1},{1,0},{2,3},{3,2},{4,5},{5,4},{6,7},{7,6},{8,9},{9,8},{10,11... | collective-permute-start | bytes 221192 | tf_op jit(solution)/shard_map/ppermute | solution.py:565
  8.0 1.4 %collective-permute-start.4 = (f32[216,128]{1,0:T(8,128)S(1)}, f32[216,128]{1,0:T(8,128)S(1)}, u32[]{:S(2)}, u32[]{:S(2)}) collective-permute-start(f32[216,128]{1,0:T(8,128)S(1)} %get-tuple-element.33.rest_0_), channel_id=1, source_target_pairs={{0,1},{1,0},{2,3},{3,2},{4,5},{5,4},{6,7},{7,6},{8,9},{9,8},{10,11... | collective-permute-start | bytes 331784 | tf_op jit(solution)/shard_map/ppermute | solution.py:565
  8.9 1.3 %collective-permute-start.3 = (f32[64,128]{1,0:T(8,128)S(1)}, f32[64,128]{1,0:T(8,128)S(1)}, u32[]{:S(2)}, u32[]{:S(2)}) collective-permute-start(f32[64,128]{1,0:T(8,128)S(1)} %get-tuple-element.30), channel_id=1, source_target_pairs={{0,1},{1,0},{2,3},{3,2},{4,5},{5,4},{6,7},{7,6},{8,9},{9,8},{10,11... | collective-permute-start | bytes 98312 | tf_op jit(solution)/shard_map/ppermute | solution.py:565
  11.0 1.2 %collective-permute-start.5 = (f32[1,2176]{1,0:T(1,128)S(1)}, f32[1,2176]{1,0:T(1,128)S(1)}, u32[]{:S(2)}, u32[]{:S(2)}) collective-permute-start(f32[1,2176]{1,0:T(1,128)S(1)} %get-tuple-element.34), channel_id=1, source_target_pairs={{0,1},{1,0},{2,3},{3,2},{4,5},{5,4},{6,7},{7,6},{8,9},{9,8},{10,11... | collective-permute-start | bytes 26120 | tf_op jit(solution)/shard_map/ppermute | solution.py:565
  12.2 6.0 %collective-permute-start.6 = (f32[1,2176]{1,0:T(1,128)S(1)}, f32[1,2176]{1,0:T(1,128)S(1)}, u32[]{:S(2)}, u32[]{:S(2)}) collective-permute-start(f32[1,2176]{1,0:T(1,128)S(1)} %add.18), channel_id=1, source_target_pairs={{0,9},{1,8},{2,11},{3,10},{4,13},{5,12},{6,15},{7,14},{8,1},{9,0},... | collective-permute-start | bytes 26120 | tf_op jit(solution)/shard_map/ppermute | solution.py:589
  18.3 3.1 %collective-permute-start.7 = (f32[1,2176]{1,0:T(1,128)S(1)}, f32[1,2176]{1,0:T(1,128)S(1)}, u32[]{:S(2)}, u32[]{:S(2)}) collective-permute-start(f32[1,2176]{1,0:T(1,128)S(1)} %add.19), channel_id=1, source_target_pairs={{0,3},{1,2},{2,1},{3,0},{4,7},{5,6},{6,5},{7,4},{8,11},{9,10},{10,... | collective-permute-start | bytes 26120 | tf_op jit(solution)/shard_map/ppermute | solution.py:589
  19.4 4.0 %collective-permute-start.8 = (f32[1,2176]{1,0:T(1,128)S(1)}, f32[1,2176]{1,0:T(1,128)S(1)}, u32[]{:S(2)}, u32[]{:S(2)}) collective-permute-start(f32[1,2176]{1,0:T(1,128)S(1)} %add.19), channel_id=1, source_target_pairs={{0,7},{1,6},{2,5},{3,4},{4,3},{5,2},{6,1},{7,0},{8,15},{9,14},{10,... | collective-permute-start | bytes 26120 | tf_op jit(solution)/shard_map/ppermute | solution.py:589
  20.3 3.1 %collective-permute-start.9 = (f32[1,2176]{1,0:T(1,128)S(1)}, f32[1,2176]{1,0:T(1,128)S(1)}, u32[]{:S(2)}, u32[]{:S(2)}) collective-permute-start(f32[1,2176]{1,0:T(1,128)S(1)} %add.19), channel_id=1, source_target_pairs={{0,5},{1,4},{2,7},{3,6},{4,1},{5,0},{6,3},{7,2},{8,13},{9,12},{10,... | collective-permute-start | bytes 26120 | tf_op jit(solution)/shard_map/ppermute | solution.py:589
  23.5 4.0 %collective-permute-start.10 = (f32[1,2176]{1,0:T(1,128)S(1)}, f32[1,2176]{1,0:T(1,128)S(1)}, u32[]{:S(2)}, u32[]{:S(2)}) collective-permute-start(f32[1,2176]{1,0:T(1,128)S(1)} %add_add_fusion), channel_id=1, source_target_pairs={{0,17},{1,16},{2,19},{3,18},{4,21},{5,20},{6,23},{7,22},{8,25},{9,... | collective-permute-start | bytes 26120 | tf_op jit(solution)/shard_map/ppermute | solution.py:589
